TPU v7x, 32 devices: a whole 2x2x4 slice. The times are simulated.
32 devices in a mesh: dp: 2 (over core), head: 4 (over y, x), mlp: 4 (over z).
Axes of the slice: x: 2, y: 2, z: 4, core: 2. Of those that a mesh axis runs over, the one named last changes fastest.
Arguments:
- tokens: bfloat16 [2048, 8, 1024], P('head', ('dp', 'mlp')), may hold values from -6 to 6
- first_values: bfloat16 [2048, 8, 1024], P(None, ('dp', 'mlp'), 'head'), may hold values from -10.5 to 10.5
- segment_ids: int32 [2048, 8], P(None, ('dp', 'mlp')), may hold values from 0 to 7, as said below
- positions: int32 [2048, 8], P(None, ('dp', 'mlp')), may hold values from 0 to 2047, as said below
- attn_gain: float32 [1024], replicated, may hold values from 0.5 to 1.5
- w_query: bfloat16 [1024, 1024], P(None, 'head'), may hold values from -0.1875 to 0.1875
- w_key: bfloat16 [1024, 1024], P(None, 'head'), may hold values from -0.1875 to 0.1875
- w_value: bfloat16 [1024, 1024], P(None, 'head'), may hold values from -0.1875 to 0.1875
- w_out: bfloat16 [1024, 1024], P('head'), may hold values from -2 to 2
- mlp_gain: float32 [1024], replicated, may hold values from 0.5 to 1.5
- w_gate: bfloat16 [1024, 2816], P(None, 'mlp'), may hold values from -0.1875 to 0.1875
- w_up: bfloat16 [1024, 2816], P(None, 'mlp'), may hold values from -0.1875 to 0.1875
- w_down: bfloat16 [2816, 1024], P('mlp'), may hold values from -0.109375 to 0.109375
- out_grad: bfloat16 [2048, 8, 1024], P('head', ('dp', 'mlp')), may hold values from -6 to 6
Outputs:
- output: bfloat16 [2048, 8, 1024], P('head', ('dp', 'mlp'))
- input_grad: bfloat16 [2048, 8, 1024], P('head', ('dp', 'mlp'))
- first_values_grad: bfloat16 [2048, 8, 1024], P(None, ('dp', 'mlp'), 'head')
- attn_gain_grad: float32 [1024], replicated
- w_query_grad: float32 [1024, 1024], P(None, 'head')
- w_key_grad: float32 [1024, 1024], P(None, 'head')
- w_value_grad: float32 [1024, 1024], P(None, 'head')
- w_out_grad: float32 [1024, 1024], P('head')
- mlp_gain_grad: float32 [1024], replicated
- w_gate_grad: float32 [1024, 2816], P(None, 'mlp')
- w_up_grad: float32 [1024, 2816], P(None, 'mlp')
- w_down_grad: float32 [2816, 1024], P('mlp')
- value_norms: float32 [2], replicated
Inputs may be any that keep to these rules, and one draw needn't show every extreme that they name: `segment_ids`: along each packed row (dimension 0) the ids start at 0 and rise by at most one from one position to the next; packed row 0 holds a single document, every other packed row exactly 8. `positions`: 0 at a row's start and wherever the segment id changes, else one more than at the previous position.
All inputs are finite; a program needn't handle non-finite values.
Results may differ from a plain program's by a relative error of at most 0.019.
Values may be sent and summed in bfloat16 or wider, within the bound.
No kernel may reach another device: no remote copies, remote signals or barrier semaphores. Data moves between devices by JAX's collectives and lax.ppermute only.
A program may use at most 256 MiB of HBM per device.

v0:
```python
import functools

import jax
import jax.numpy as jnp
from jax import lax
from jax.experimental import pallas as pl
from jax.experimental.pallas import tpu as pltpu
from jax.sharding import PartitionSpec as P

HEAD_DIM = 64
epsilon = 1e-06
theta_base = 10000.0
blend_weight = 0.5
masked_score = -1e30
NT=(((1,),(1,)),((),()))
NN=(((1,),(0,)),((),()))
TN=(((0,),(0,)),((),()))
def dot(a,b,dims): return lax.dot_general(a,b,dims,preferred_element_type=jnp.float32)

def head_lanes(lanes):
    return lanes//HEAD_DIM

def only_head(x,number,lanes,other=0.0):
    if lanes==HEAD_DIM: return x
    lane=lax.broadcasted_iota(jnp.int32,x.shape,1)
    return jnp.where(lane//HEAD_DIM==number,x,jnp.asarray(other,x.dtype))

def fwd2_kernel(block,firsts,lasts,q_ref,k_ref,v_ref,start_ref,*rest):
    o_ref,lse_ref,vt_ref=rest[-3:]
    i=pl.program_id(1)
    length,lanes=k_ref.shape
    heads=lanes//HEAD_DIM
    @pl.when(i==0)
    def _():
        for r in range(length//block):
            rows=pl.ds(r*block,block)
            t=jnp.transpose(v_ref[rows,:])
            for n in range(heads):
                vt_ref[n,0:HEAD_DIM,rows]=t[n*HEAD_DIM:(n+1)*HEAD_DIM]
                vt_ref[n,HEAD_DIM:,rows]=jnp.ones((16,block),jnp.bfloat16)
    q=q_ref[...]*jnp.asarray(HEAD_DIM**-0.5,q_ref.dtype)
    qs=[only_head(q,n,lanes) for n in range(heads)]
    part=256 if block%256==0 else block
    def update(masked,at,size,first,carry):
        rows=pl.ds(pl.multiple_of(at,part),size)
        k=k_ref[rows,:]
        ss=[dot(k,x[first:],NT) for x in qs]
        if masked:
            shape=ss[0].shape
            key=at+lax.broadcasted_iota(jnp.int32,shape,0)
            query=i*block+first+lax.broadcasted_iota(jnp.int32,shape,1)
            allowed=(key<=query)&(key>=start_ref[:,first:])
            ss=[jnp.where(allowed,s,masked_score) for s in ss]
        ms=[jnp.maximum(carry[n][0],jnp.max(ss[n],axis=0,keepdims=True)) for n in range(heads)]
        ps=[jnp.exp(ss[n]-ms[n]).astype(jnp.bfloat16) for n in range(heads)]
        return tuple((ms[n],carry[n][1]*jnp.exp(carry[n][0]-ms[n])+dot(vt_ref[n,:,rows],ps[n],NN)) for n in range(heads))
    def step(masked,j,carry):
        return update(masked,j*block,block,0,carry)
    carry=tuple((jnp.full((1,block),masked_score,jnp.float32),jnp.zeros((HEAD_DIM+16,block),jnp.float32)) for _ in range(heads))
    a=firsts[i]//block
    b=jnp.clip((lasts[i]+block-1)//block,a,i)
    carry=lax.fori_loop(a,b,functools.partial(step,True),carry)
    carry=lax.fori_loop(b,i,functools.partial(step,False),carry)
    for at in range(0,block,part):
        late=update(True,i*block+at,part,at,tuple((m[:,at:],x[:,at:]) for m,x in carry))
        if at: late=tuple(tuple(jnp.concatenate([x[:,:at],y],axis=1) for x,y in zip(c,l)) for c,l in zip(carry,late))
        carry=late
    outs=[]
    for n in range(heads):
        m,acc=carry[n]
        l=acc[HEAD_DIM:HEAD_DIM+1]
        outs.append(acc[:HEAD_DIM]/l)
        lse_ref[0,n:n+1,:]=m+jnp.log(l)
    o=outs[0] if heads==1 else jnp.concatenate(outs,axis=0)
    o_ref[...]=jnp.transpose(o).astype(o_ref.dtype)

def attend_forward2(q,k,v,start,block,group,earlier=()):
    length,width=q.shape
    lanes=min(128,width); nq=length//block
    firsts=start[::block]; lasts=start[block-1::block]
    spec=pltpu.PrefetchScalarGridSpec(num_scalar_prefetch=2,grid=(1,nq),
        in_specs=[pl.BlockSpec((block,lanes),lambda g,i,*_:(i,group)),
                  pl.BlockSpec((length,lanes),lambda g,i,*_:(0,group)),
                  pl.BlockSpec((length,lanes),lambda g,i,*_:(0,group)),
                  pl.BlockSpec((1,block),lambda g,i,*_:(0,i))]+[pl.BlockSpec(memory_space=pl.ANY)]*len(earlier),
        out_specs=[pl.BlockSpec((block,lanes),lambda g,i,*_:(i,g)),
                   pl.BlockSpec((1,8,block),lambda g,i,*_:(g,0,i))],
        scratch_shapes=[pltpu.VMEM((lanes//HEAD_DIM,HEAD_DIM+16,length),jnp.bfloat16)])
    return pl.pallas_call(functools.partial(fwd2_kernel,block),grid_spec=spec,
        out_shape=[jax.ShapeDtypeStruct((length,lanes),jnp.bfloat16),jax.ShapeDtypeStruct((1,8,length),jnp.float32)],
        compiler_params=pltpu.CompilerParams(vmem_limit_bytes=60*1024*1024),
        cost_estimate=pl.CostEstimate(flops=29*length*length*lanes,bytes_accessed=8*length*lanes,transcendentals=0),
        name="attend_forward")(firsts,lasts,q,k,v,start[None,:],*earlier)

def backward_kernel(block,full_end,some_end,q_ref,k_ref,v_ref,d_ref,o_ref,lse_ref,start_ref,cos_ref,sin_ref,*rest):
    p_ref,first_ref,dq_ref,delta_ref=rest[-4:]
    j=pl.program_id(1)
    length,lanes=q_ref.shape
    heads=lanes//HEAD_DIM
    @pl.when(j==0)
    def _():
        dq_ref[...]=jnp.zeros_like(dq_ref)
        for i in range(length//block):
            rows=pl.ds(i*block,block)
            prod=jnp.transpose(d_ref[rows,:].astype(jnp.float32)*o_ref[rows,:].astype(jnp.float32))
            for n in range(heads):
                delta_ref[n:n+1,rows]=jnp.sum(prod[n*HEAD_DIM:(n+1)*HEAD_DIM],axis=0,keepdims=True)
    k=k_ref[...]; v=v_ref[...]
    scale=HEAD_DIM**-0.5
    kl=[only_head(k,n,lanes) for n in range(heads)]
    ks=[x*jnp.asarray(scale,k.dtype) for x in kl]
    vs=[only_head(v,n,lanes) for n in range(heads)]
    part=256 if block%256==0 else block
    def terms(masked,keys,at,size):
        rows=pl.ds(pl.multiple_of(at,part),size)
        q=q_ref[rows,:]; d=d_ref[rows,:]
        ss=[dot(x[keys],q,NT) for x in ks]
        dps=[dot(x[keys],d,NT) for x in vs]
        if masked:
            shape=ss[0].shape
            key=j*block+keys.start+lax.broadcasted_iota(jnp.int32,shape,0)
            query=at+lax.broadcasted_iota(jnp.int32,shape,1)
            allowed=(key<=query)&(key>=start_ref[0:1,rows])
            ss=[jnp.where(allowed,s,masked_score) for s in ss]
        ps=[jnp.exp(ss[n]-lse_ref[0,n:n+1,rows]) for n in range(heads)]
        dss=[(ps[n]*(dps[n]-delta_ref[n:n+1,rows])).astype(jnp.bfloat16) for n in range(heads)]
        pv=[dot(p.astype(jnp.bfloat16),d,NN) for p in ps]
        pk=[dot(x,q,NN) for x in dss]
        dq_ref[rows,:]+=sum(dot(dss[n],ks[n][keys],TN) for n in range(heads))
        if heads==2:
            lane=lax.broadcasted_iota(jnp.int32,pv[0].shape,1)<HEAD_DIM
            return jnp.where(lane,pk[0],pk[1]),jnp.where(lane,pv[0],pv[1])
        return pk[0],pv[0]
    def step(masked,i,carry):
        dk,dv=terms(masked,slice(0,block),i*block,block)
        return carry[0]+dk,carry[1]+dv
    pieces=[terms(True,slice(at,at+part),j*block+at,block-at) for at in range(0,block,part)]
    carry=tuple(jnp.concatenate(x,axis=0) if len(x)>1 else x[0] for x in zip(*pieces))
    carry=lax.fori_loop(j+1,full_end[j],functools.partial(step,False),carry)
    dk,dv=lax.fori_loop(full_end[j],some_end[j],functools.partial(step,True),carry)
    here=pl.ds(pl.multiple_of(j*block,block),block)
    p_ref[here,lanes:2*lanes]=turned(dk*scale,cos_ref[here,:],-sin_ref[here,:]).astype(jnp.bfloat16)
    blend=dv.astype(jnp.bfloat16).astype(jnp.float32)
    p_ref[here,2*lanes:]=(blend_weight*blend).astype(jnp.bfloat16)
    first_ref[...]=((1.0-blend_weight)*blend).astype(jnp.bfloat16)
    @pl.when(j==pl.num_programs(1)-1)
    def _():
        for i in range(length//block):
            rows=pl.ds(i*block,block)
            p_ref[rows,:lanes]=turned(dq_ref[rows,:],cos_ref[rows,:],-sin_ref[rows,:]).astype(jnp.bfloat16)

def attend_backward(q,k,v,d,start,cosine,sine,block,group,o,lse,before=(),earlier=()):
    length,width=q.shape
    lanes=cosine.shape[1]; n=length//block
    lasts=start[block-1::block]
    edge=jnp.arange(n,dtype=jnp.int32)
    full_end=jnp.maximum(edge+1,jnp.sum((lasts[None,:]<=edge[:,None]*block).astype(jnp.int32),axis=1))
    reach=jnp.sum((start[None,:]<=edge[:,None]*block+block-1).astype(jnp.int32),axis=1)
    some_end=jnp.maximum(full_end,(reach+block-1)//block)
    whole=pl.BlockSpec((length,lanes),lambda g,j,*_:(0,group))
    part=pl.BlockSpec((block,lanes),lambda g,j,*_:(j,group))
    table=pl.BlockSpec((length,lanes),lambda g,j,*_:(0,0))
    more=list(earlier)+list(before)
    spec=pltpu.PrefetchScalarGridSpec(num_scalar_prefetch=2,grid=(1,n),
        in_specs=[whole,part,part,whole,table,pl.BlockSpec((1,8,length),lambda g,j,*_:(0,0,0)),pl.BlockSpec((1,length),lambda g,j,*_:(0,0)),table,table]+[pl.BlockSpec(memory_space=pl.ANY)]*len(more),
        out_specs=[pl.BlockSpec((length,3*lanes),lambda g,j,*_:(0,group)),part],
        scratch_shapes=[pltpu.VMEM((length,lanes),jnp.float32),pltpu.VMEM((8,length),jnp.float32)])
    return pl.pallas_call(functools.partial(backward_kernel,block),grid_spec=spec,
        out_shape=[jax.ShapeDtypeStruct((length,3*width),jnp.bfloat16),jax.ShapeDtypeStruct((length,width),jnp.bfloat16)],
        input_output_aliases={11+len(earlier)+k:k for k in range(len(before))},
        compiler_params=pltpu.CompilerParams(vmem_limit_bytes=56*1024*1024),
        cost_estimate=pl.CostEstimate(flops=52*length*length*lanes,bytes_accessed=22*length*lanes,transcendentals=0),
        name="attend_backward")(full_end,some_end,q,k,v,d,o,lse,start[None,:],cosine,sine,*more)


f32 = jnp.float32
bf16 = jnp.bfloat16
everywhere = pl.BlockSpec(memory_space=pl.ANY)


def swap(x, axis, mask):
    return lax.ppermute(x, axis, [(i, i ^ mask) for i in range(lax.axis_size(axis))])


def cut_of(rows):
    half = rows // 2
    return half - half % 8 if half >= 8 else half


def after(x, *earlier):
    def kernel(*refs):
        pass

    return pl.pallas_call(
        kernel,
        in_specs=[everywhere] * (1 + len(earlier)),
        out_specs=everywhere,
        out_shape=jax.ShapeDtypeStruct(x.shape, x.dtype),
        input_output_aliases={0: 0},
        name="after",
    )(x, *earlier)


def spread_relay(x, axis):
    count = lax.axis_size(axis)
    if count != 4:
        return [[x]] + [[swap(x, axis, e)] for e in range(1, count)]
    cut = cut_of(x.shape[0])
    one, two = swap(x, axis, 1), swap(x, axis, 2)
    return [[x], [one], [two], [swap(two[:cut], axis, 1), swap(one[cut:], axis, 2)]]


def spread(x, axis):
    return [x] + [swap(x, axis, e) for e in range(1, lax.axis_size(axis))]


def add_low(*terms):
    return sum(t.astype(f32) for t in terms).astype(bf16)


def collect(parts, axis):
    return sum((swap(p, axis, e) if e else p).astype(f32) for e, p in enumerate(parts))


def in_order(parts, rank):
    rows = parts[0].shape[0]
    whole = jnp.zeros((len(parts) * rows,) + parts[0].shape[1:], parts[0].dtype)
    for e, part in enumerate(parts):
        whole = lax.dynamic_update_slice_in_dim(whole, part, (rank ^ e) * rows, 0)
    return whole


def block_of(x, number, rows):
    return lax.dynamic_slice_in_dim(x, number * rows, rows, 0)


def both_cores(own, other, core):
    first = core == 0
    return jnp.concatenate([jnp.where(first, own, other), jnp.where(first, other, own)])


def sum_over_all(x):
    for axis in ("mlp", "dp", "head"):
        mask = 1
        while mask < lax.axis_size(axis):
            x = x + swap(x, axis, mask)
            mask *= 2
    return x


def rms_scale(rows):
    return lax.rsqrt(jnp.mean(rows * rows, axis=-1, keepdims=True) + epsilon)


def norm_back(rows, scale, gain, grad):
    weighted = grad * gain
    return scale * weighted - rows * scale * scale * scale * jnp.mean(
        weighted * rows, axis=-1, keepdims=True
    )


def turned(x, cosine, sine):
    half = HEAD_DIM // 2
    if x.shape[1] == HEAD_DIM:
        other = jnp.concatenate([x[:, half:], x[:, :half]], axis=1)
    else:
        lanes = x.shape[1]
        lane = lax.broadcasted_iota(jnp.int32, x.shape, 1)
        other = jnp.where(
            lane % HEAD_DIM < half, pltpu.roll(x, lanes - half, 1), pltpu.roll(x, half, 1)
        )
    return x * cosine + other * sine


def load_rows(refs, counts, number, target):
    at = 0
    for k, pieces in enumerate(counts):
        mine = refs[at : at + pieces]
        at += pieces

        @pl.when(number == k)
        def _(mine=mine):
            row = 0
            for ref in mine:
                target[row : row + ref.shape[0], :] = ref[...]
                row += ref.shape[0]


def project_kernel(counts, rank_ref, *refs):
    total = sum(counts)
    parts, (w_ref, gain_ref, cos_ref, sin_ref, first_ref) = refs[:total], refs[total : total + 5]
    a_ref, q_ref, k_ref, v_ref, norm_ref, rows_ref = refs[-6:]
    i = pl.program_id(0)
    load_rows(parts, counts, i, rows_ref)
    x = rows_ref[...].astype(f32)
    a = (x * rms_scale(x) * gain_ref[...]).astype(bf16)
    a_ref[...] = a
    width = q_ref.shape[1]
    lanes = cos_ref.shape[1]
    cosine, sine = cos_ref[...], sin_ref[...]
    joined = dot(a, w_ref[...], NN)
    of = lax.broadcasted_iota(jnp.int32, (lanes, 128), 0) // HEAD_DIM
    one_hot = (of == lax.broadcasted_iota(jnp.int32, (lanes, 128), 1)).astype(f32)

    def norms(value):
        squares = lax.dot_general(
            value * value, one_hot, NN, precision=lax.Precision.HIGHEST, preferred_element_type=f32
        )
        return jnp.sum(jnp.sqrt(jnp.maximum(squares, 0.0)), axis=0, keepdims=True)

    @pl.when(i == 0)
    def _():
        norm_ref[...] = jnp.zeros_like(norm_ref)

    for g in range(width // lanes):
        at = slice(g * lanes, (g + 1) * lanes)
        query, key, value = (
            joined[:, (3 * g + k) * lanes : (3 * g + k + 1) * lanes] for k in range(3)
        )
        q_ref[:, at] = turned(query, cosine, sine).astype(bf16)
        k_ref[:, at] = turned(key, cosine, sine).astype(bf16)
        first = first_ref[:, at].astype(f32)
        blended = blend_weight * value + (1.0 - blend_weight) * first
        v_ref[:, at] = blended.astype(bf16)
        norm_ref[0:1, :] += norms(first)
        norm_ref[1:2, :] += norms(blended)


def spec_whole(x):
    return pl.BlockSpec(x.shape, lambda *_: (0,) * x.ndim)


def cost(us):
    return pl.CostEstimate(flops=int(us * 1.1e9), bytes_accessed=int(us * 1e5), transcendentals=0)


big = pltpu.CompilerParams(vmem_limit_bytes=56 * 1024 * 1024)


def project(rank, parts, base, weights, gain, cosine, sine, firsts, before=()):
    counts = tuple(len(p) for p in parts)
    flat = [x for p in parts for x in p]
    chunk = sum(x.shape[0] for x in parts[0])
    length, width = firsts.shape
    model, lanes = flat[0].shape[1], cosine.shape[1]
    there = lambda i, r: (r[0] ^ (base + i), 0)
    block = lambda n: pl.BlockSpec((chunk, n), there)
    spec = pltpu.PrefetchScalarGridSpec(
        num_scalar_prefetch=1,
        grid=(len(parts),),
        in_specs=[spec_whole(x) for x in flat]
        + [spec_whole(weights), spec_whole(gain), block(lanes), block(lanes), block(width)]
        + [everywhere] * len(before),
        out_specs=[block(model), block(width), block(width), block(width)]
        + [pl.BlockSpec((8, 128), lambda i, r: (0, 0))],
        scratch_shapes=[pltpu.VMEM((chunk, model), bf16)],
    )
    low = jax.ShapeDtypeStruct((length, width), bf16)
    return pl.pallas_call(
        functools.partial(project_kernel, counts),
        grid_spec=spec,
        out_shape=[jax.ShapeDtypeStruct((length, model), bf16), low, low, low]
        + [jax.ShapeDtypeStruct((8, 128), f32)],
        input_output_aliases={len(flat) + 6 + k: k for k in range(len(before))},
        compiler_params=big,
        cost_estimate=cost(4.5 * len(parts)),
        name="project",
    )(rank[None], *flat, weights, gain, cosine, sine, firsts, *before)


def assemble_kernel(ranks, rank_ref, *refs):
    far_ref, out_ref = refs[-2:]
    rows = far_ref.shape[2]
    e = pl.program_id(0)
    for k in range(ranks):

        @pl.when(e == k)
        def _(ref=refs[k]):
            for a in range(3):
                far_ref[a, 0] = ref[a * rows : (a + 1) * rows, :]
            out_ref[0] = ref[3 * rows :, :]


def assemble(rank, bundles, rows, earlier):
    ranks = len(bundles)
    wide, model = bundles[0].shape
    spec = pltpu.PrefetchScalarGridSpec(
        num_scalar_prefetch=1,
        grid=(ranks,),
        in_specs=[spec_whole(b) for b in bundles] + [everywhere] * len(earlier),
        out_specs=[
            pl.BlockSpec((3, 1, rows, model), lambda e, r: (0, e, 0, 0)),
            pl.BlockSpec((1, wide - 3 * rows, model), lambda e, r: (r[0] ^ e, 0, 0)),
        ],
    )
    return pl.pallas_call(
        functools.partial(assemble_kernel, ranks),
        grid_spec=spec,
        out_shape=[
            jax.ShapeDtypeStruct((3, ranks, rows, model), bf16),
            jax.ShapeDtypeStruct((ranks, wide - 3 * rows, model), bf16),
        ],
        compiler_params=big,
        cost_estimate=cost(3),
        name="assemble",
    )(rank[None], *bundles, *earlier)


def feed_kernel(x_ref, g_ref, *refs):
    sources, (act_ref, in_ref, sum_ref) = (refs[0:3], refs[3:6], refs[6:9]), refs[-3:]
    f = pl.program_id(0)
    steps = pl.num_programs(0)

    @pl.when(f == 0)
    def _():
        sum_ref[...] = jnp.zeros_like(sum_ref)

    def work(gate_w, up_w, down_w):
        x, g = x_ref[...], g_ref[...]
        gate, up = dot(gate_w[...], x, NT), dot(up_w[...], x, NT)
        hidden_grad = dot(down_w[...], g, NT)
        sigma = 1.0 / (1.0 + jnp.exp(-gate))
        gate_sigma = gate * sigma
        hidden = (gate_sigma * up).astype(bf16)
        gate_grad = (hidden_grad * up * (sigma + gate_sigma * (1.0 - sigma))).astype(bf16)
        up_grad = (hidden_grad * gate_sigma).astype(bf16)
        act_ref[0, 0], act_ref[0, 1], act_ref[0, 2] = gate_grad, up_grad, hidden
        sum_ref[...] += dot(gate_grad, gate_w[...], TN) + dot(up_grad, up_w[...], TN)

    for k, condition in enumerate((f < 2, f == 2, f == 3)):

        @pl.when(condition)
        def _(k=k):
            work(*sources[k])

    @pl.when(f == steps - 1)
    def _():
        in_ref[...] = sum_ref[...].astype(in_ref.dtype)


def feed(x, grad, own, far, far_other, dtype, earlier=()):
    tokens, model = x.shape
    part = own.shape[0] // 6
    block = lambda at: pl.BlockSpec((part, model), at)
    return pl.pallas_call(
        feed_kernel,
        grid=(4,),
        in_specs=[spec_whole(x), spec_whole(grad)]
        + [block(lambda f, a=a: (2 * a + jnp.minimum(f, 1), 0)) for a in range(3)]
        + [block(lambda f, a=a: (a, 0)) for a in range(3)] * 2
        + [everywhere] * len(earlier),
        out_specs=[
            pl.BlockSpec((1, 3, part, tokens), lambda f: (f, 0, 0, 0)),
            pl.BlockSpec((tokens, model), lambda f: (0, 0)),
        ],
        out_shape=[
            jax.ShapeDtypeStruct((4, 3, part, tokens), bf16),
            jax.ShapeDtypeStruct((tokens, model), dtype),
        ],
        scratch_shapes=[pltpu.VMEM((tokens, model), f32)],
        compiler_params=big,
        cost_estimate=cost(16),
        name="feed",
    )(x, grad, *([own] * 3), *([far] * 3), *([far_other] * 3), *earlier)


def half_grads(act_ref, near_ref, x_ref, xn_ref, g_ref, gn_ref, result_ref):
    a = pl.program_id(0)

    @pl.when(a < 2)
    def _():
        result_ref[...] = dot(act_ref[0, 0], x_ref[...], NN) + dot(near_ref[0, 0], xn_ref[...], NN)

    @pl.when(a == 2)
    def _():
        result_ref[...] = dot(act_ref[0, 0], g_ref[...], NN) + dot(near_ref[0, 0], gn_ref[...], NN)


def other_grads_kernel(scalars, *refs):
    out_ref, result_ref = refs[-2:]
    half_grads(*refs[:6], result_ref)
    out_ref[...] = result_ref[...].astype(bf16)


def far_grads_kernel(ranks, scalars, *refs):
    got_ref, out_refs, result_ref = refs[6], refs[7 : 7 + ranks], refs[-1]
    half_grads(*refs[:6], result_ref)
    rows = result_ref.shape[0] // ranks
    for e in range(ranks):
        at = slice(e * rows, (e + 1) * rows)
        out_refs[e][0] = (result_ref[at, :] + got_ref[at, :].astype(f32)).astype(bf16)


def own_grads_kernel(ranks, scalars, *refs):
    got_ref, out_ref, out_got_ref = refs[6:9]
    own_refs, result_ref = refs[9 : 9 + ranks], refs[-1]
    half_grads(*refs[:6], result_ref)
    i = pl.program_id(0)
    rows = result_ref.shape[0] // ranks
    result_ref[...] += got_ref[...].astype(f32)

    @pl.when(i == 0)
    def _():
        for e in range(ranks):
            number = scalars[1] ^ e
            both = out_ref[number].astype(f32) + out_got_ref[number].astype(f32)
            own_refs[e][3 * rows :, :] = both.astype(bf16)

    for a in range(3):

        @pl.when(i == a)
        def _(a=a):
            to = slice(a * rows, (a + 1) * rows)
            for e in range(ranks):
                if rows % 8 == 0:
                    at = pl.ds(pl.multiple_of((scalars[1] ^ e) * rows, 8), rows)
                    own_refs[e][to, :] = result_ref[at, :].astype(bf16)
                else:
                    for h in range(ranks):

                        @pl.when(scalars[1] ^ e == h)
                        def _(e=e, h=h):
                            own_refs[e][to, :] = result_ref[h * rows : (h + 1) * rows, :].astype(bf16)


def shard_grads(scalars, ranks, far, here, near, x, x_near, grad, grad_near, got=None):
    _, _, part, tokens = here.shape
    model = x.shape[1]
    if got is None:
        number = lambda c: 3 if far else 1 - c[0]
    else:
        number = lambda c: 2 if far else c[0]
    act = pl.BlockSpec((1, 1, part, tokens), lambda i, c: (number(c), i, 0, 0))
    in_specs = [act, act] + [spec_whole(x)] * 4
    args = [here, near, x, x_near, grad, grad_near]
    row_block = pl.BlockSpec((part, model), lambda i, c: (i, 0))
    rows = part // ranks
    if got is None:
        kernel, out_specs = other_grads_kernel, row_block
        out_shape = jax.ShapeDtypeStruct((3 * part, model), bf16)
    elif far:
        kernel = functools.partial(far_grads_kernel, ranks)
        in_specs.append(row_block)
        args += got
        out_specs = [pl.BlockSpec((1, rows, model), lambda i, c: (i, 0, 0))] * ranks
        out_shape = [jax.ShapeDtypeStruct((3, rows, model), bf16)] * ranks
    else:
        kernel = functools.partial(own_grads_kernel, ranks)
        in_specs += [row_block] + [spec_whole(g) for g in got[1:]]
        args += got
        wide = 3 * rows + got[1].shape[1]
        out_specs = [pl.BlockSpec((wide, model), lambda i, c: (0, 0))] * ranks
        out_shape = [jax.ShapeDtypeStruct((wide, model), bf16)] * ranks
    spec = pltpu.PrefetchScalarGridSpec(
        num_scalar_prefetch=1,
        grid=(3,),
        in_specs=in_specs,
        out_specs=out_specs,
        scratch_shapes=[pltpu.VMEM((part, model), f32)],
    )
    return pl.pallas_call(
        kernel,
        grid_spec=spec,
        out_shape=out_shape,
        compiler_params=big,
        cost_estimate=cost(8),
        name=("far" if far else "own") + ("_other" if got is None else "_sum"),
    )(scalars, *args)


def others_kernel(scalars, act_ref, near_ref, x_ref, xn_ref, g_ref, gn_ref, *refs):
    own_ref, far_ref, far_other_ref, far_out, own_out, out_ref, out_near_ref, sum_ref = refs
    i = pl.program_id(0)
    for a in range(6):

        @pl.when(i == a)
        def _(a=a):
            first, second = (x_ref, xn_ref) if a % 3 < 2 else (g_ref, gn_ref)
            target = far_out if a < 3 else own_out
            target[...] = (
                dot(act_ref[0, 0], first[...], NN) + dot(near_ref[0, 0], second[...], NN)
            ).astype(bf16)

    @pl.when(i == 5)
    def _():
        sum_ref[...] = jnp.zeros_like(sum_ref)

    for condition, ref in (((i == 6) | (i == 7), own_ref), (i == 8, far_ref), (i == 9, far_other_ref)):

        @pl.when(condition)
        def _(ref=ref):
            sum_ref[0] += dot(act_ref[0, 0], ref[...], TN)
            sum_ref[1] += dot(near_ref[0, 0], ref[...], TN)

    @pl.when(i == 9)
    def _():
        out_ref[...] = sum_ref[0]
        out_near_ref[...] = sum_ref[1].astype(bf16)


def others(scalars, here, near, x, x_near, grad, grad_near, own, far, far_other):
    _, _, part, tokens = here.shape
    model = x.shape[1]

    def act_at(i, c):
        number = jnp.where(i < 3, 3, jnp.where(i < 6, 1 - c[0], i - 6))
        return (number, jnp.where(i < 6, i % 3, 2), 0, 0)

    act = pl.BlockSpec((1, 1, part, tokens), act_at)
    row = lambda at: pl.BlockSpec((part, model), at)
    spec = pltpu.PrefetchScalarGridSpec(
        num_scalar_prefetch=1,
        grid=(10,),
        in_specs=[act, act]
        + [spec_whole(x)] * 4
        + [row(lambda i, c: (4 + jnp.clip(i - 6, 0, 1), 0))]
        + [row(lambda i, c: (2, 0))] * 2,
        out_specs=[
            row(lambda i, c: (jnp.minimum(i, 2), 0)),
            row(lambda i, c: (jnp.clip(i - 3, 0, 2), 0)),
            spec_whole(x),
            spec_whole(x),
        ],
        scratch_shapes=[pltpu.VMEM((2, tokens, model), f32)],
    )
    half = jax.ShapeDtypeStruct((3 * part, model), bf16)
    return pl.pallas_call(
        others_kernel,
        grid_spec=spec,
        out_shape=[half, half]
        + [jax.ShapeDtypeStruct((tokens, model), f32), jax.ShapeDtypeStruct((tokens, model), bf16)],
        compiler_params=big,
        cost_estimate=cost(19),
        name="others",
    )(scalars, here, near, x, x_near, grad, grad_near, own, far, far_other)


def regroup_kernel(ranks, rank_ref, *refs):
    out_ref = refs[-1]
    rows = out_ref.shape[2]
    e = pl.program_id(0)
    for k in range(ranks):

        @pl.when(e == k)
        def _(k=k):
            low, high = refs[2 * k], refs[2 * k + 1]
            cut = low.shape[0]
            for a in range(3):
                first, last = a * rows, (a + 1) * rows
                if last <= cut:
                    out_ref[a, 0] = low[first:last, :]
                elif first >= cut:
                    out_ref[a, 0] = high[first - cut : last - cut, :]
                else:
                    out_ref[a, 0, : cut - first] = low[first:, :]
                    out_ref[a, 0, cut - first :] = high[: last - cut, :]


def regroup(rank, pieces, rows, earlier=()):
    ranks = len(pieces)
    flat, specs = [], []
    for low, high in pieces:
        for x, at, size in (low, high):
            flat.append(x)
            specs.append(pl.BlockSpec((size, x.shape[1]), lambda e, r, at=at: (at, 0)))
    model = flat[0].shape[1]
    spec = pltpu.PrefetchScalarGridSpec(
        num_scalar_prefetch=1,
        grid=(ranks,),
        in_specs=specs + [everywhere] * len(earlier),
        out_specs=pl.BlockSpec((3, 1, rows, model), lambda e, r: (0, r[0] ^ e, 0, 0)),
    )
    return pl.pallas_call(
        functools.partial(regroup_kernel, ranks),
        grid_spec=spec,
        out_shape=jax.ShapeDtypeStruct((3, ranks, rows, model), bf16),
        compiler_params=big,
        cost_estimate=cost(2),
        name="regroup",
    )(rank[None], *flat, *earlier)


def unproject_kernel(counts, cuts, rank_ref, *refs):
    total = sum(counts)
    parts, w_ref, p_ref = refs[:total], refs[total], refs[total + 1]
    pieces = sum(len(c) for c in cuts)
    outs, gain_ref, rows_ref = refs[-2 - pieces : -2], refs[-2], refs[-1]
    i = pl.program_id(0)
    load_rows(parts, counts, i, rows_ref)
    x = rows_ref[...].astype(f32)
    grad = dot(p_ref[...], w_ref[...], NT)
    at = 0
    for k, sizes in enumerate(cuts):
        mine = outs[at : at + len(sizes)]
        at += len(sizes)

        @pl.when(i == k)
        def _(mine=mine):
            row = 0
            for ref in mine:
                ref[...] = grad[row : row + ref.shape[0]].astype(bf16)
                row += ref.shape[0]

    @pl.when(i == 0)
    def _():
        gain_ref[...] = jnp.zeros_like(gain_ref)

    gain_ref[...] += jnp.sum(grad * (x * rms_scale(x)), axis=0, keepdims=True)


def unproject(rank, parts, base, cuts, weights, grads, earlier=()):
    counts = tuple(len(p) for p in parts)
    flat = [x for p in parts for x in p]
    chunk, model = sum(x.shape[0] for x in parts[0]), flat[0].shape[1]
    block = lambda n: pl.BlockSpec((chunk, n), lambda i, r: (r[0] ^ (base + i), 0))
    sizes = [n for c in cuts for n in c]
    spec = pltpu.PrefetchScalarGridSpec(
        num_scalar_prefetch=1,
        grid=(len(parts),),
        in_specs=[spec_whole(x) for x in flat]
        + [spec_whole(weights)]
        + [block(grads.shape[1])]
        + [everywhere] * len(earlier),
        out_specs=[pl.BlockSpec((n, model), lambda i, r: (0, 0)) for n in sizes]
        + [pl.BlockSpec((1, model), lambda i, r: (0, 0))],
        scratch_shapes=[pltpu.VMEM((chunk, model), bf16)],
    )
    out = pl.pallas_call(
        functools.partial(unproject_kernel, counts, cuts),
        grid_spec=spec,
        out_shape=[jax.ShapeDtypeStruct((n, model), bf16) for n in sizes]
        + [jax.ShapeDtypeStruct((1, model), f32)],
        compiler_params=big,
        cost_estimate=cost(3.5 * len(parts)),
        name="unproject",
    )(rank[None], *flat, weights, grads, *earlier)
    return out[:-1], out[-1]


def state_kernel(back_ref, terms_ref, hidden_ref, grad_ref, gain_ref, w_ref, state_ref, low_ref, mixed_ref, sum_ref):
    hidden, gain = hidden_ref[...], gain_ref[...]
    grad = back_ref[...].astype(f32) + terms_ref[...]
    scale = rms_scale(hidden)
    state = grad_ref[...].astype(f32) + norm_back(hidden, scale, gain, grad)
    low = state.astype(bf16)
    state_ref[...] = state
    low_ref[...] = low
    for h in range(mixed_ref.shape[0]):
        mixed_ref[h] = dot(low, w_ref[h], NT).astype(bf16)

    @pl.when(pl.program_id(0) == 0)
    def _():
        sum_ref[...] = jnp.zeros_like(sum_ref)

    sum_ref[...] += jnp.sum(grad * hidden * scale, axis=0, keepdims=True)


def state_back(back, terms, hidden, grad, gain, weights):
    tokens, model = back.shape
    ranks, width, _ = weights.shape
    size = 128 if tokens % 128 == 0 else tokens
    row = pl.BlockSpec((size, model), lambda i: (i, 0))
    return pl.pallas_call(
        state_kernel,
        grid=(tokens // size,),
        in_specs=[row, row, row, row, spec_whole(gain), spec_whole(weights)],
        out_specs=[
            row,
            row,
            pl.BlockSpec((ranks, size, width), lambda i: (0, i, 0)),
            pl.BlockSpec((1, model), lambda i: (0, 0)),
        ],
        out_shape=[
            jax.ShapeDtypeStruct((tokens, model), f32),
            jax.ShapeDtypeStruct((tokens, model), bf16),
            jax.ShapeDtypeStruct((ranks, tokens, width), bf16),
            jax.ShapeDtypeStruct((1, model), f32),
        ],
        compiler_params=big,
        cost_estimate=cost(6),
        name="state_back",
    )(back, terms, hidden, grad, gain, weights)


def on_device(
    tokens,
    first_values,
    segment_ids,
    positions,
    attn_gain,
    w_query,
    w_key,
    w_value,
    w_out,
    mlp_gain,
    w_gate,
    w_up,
    w_down,
    out_grad,
):
    core, rank = lax.axis_index("dp"), lax.axis_index("head")
    ranks = lax.axis_size("head")
    chunk, width = tokens.shape[0], w_query.shape[1]
    model = tokens.shape[2]
    length, ff = segment_ids.shape[0], w_gate.shape[1]
    block = min(512, length)
    tokens, firsts, out_grad = tokens[:, 0], first_values[:, 0], out_grad[:, 0]
    places = positions[:, 0]
    start = jnp.arange(length, dtype=jnp.int32) - places

    row_parts = spread_relay(tokens, "head")

    part = ff // 2
    rows = part // ranks
    stack = jnp.concatenate([w_gate.T, w_up.T, w_down])
    cut_stack = stack.reshape(3, 2 * ranks, rows, model)
    far_piece = swap(
        lax.dynamic_index_in_dim(cut_stack, core * ranks + rank, 1, False), "mlp", 2
    ).reshape(3 * rows, model)
    out_grad_near = swap(out_grad, "mlp", 1)
    half_out = width // 2
    far_piece = after(far_piece, *row_parts[-1])
    bundle = jnp.concatenate([far_piece, block_of(w_out, core, half_out)])
    bundles = spread(bundle, "head")

    lanes = min(128, width)
    w_project = jnp.concatenate(
        [
            w[:, g * lanes : (g + 1) * lanes]
            for g in range(width // lanes)
            for w in (w_query, w_key, w_value)
        ],
        axis=1,
    )
    lane = jnp.arange(lanes)
    freq = theta_base ** (-(lane % (HEAD_DIM // 2)).astype(f32) * 2.0 / HEAD_DIM)
    angles = places.astype(f32)[:, None] * freq
    cosine = jnp.cos(angles)
    sine = jnp.sin(angles) * jnp.where(lane % HEAD_DIM < HEAD_DIM // 2, -1.0, 1.0)
    heads_args = (w_project, attn_gain[None], cosine, sine, firsts)
    soon = 3 if ranks == 4 else ranks
    *projected, norms = project(rank, row_parts[:soon], 0, *heads_args)
    if soon < ranks:
        *projected, more = project(rank, row_parts[soon:], soon, *heads_args, projected)
        norms = norms + more
    gathered, queries, keys, values = projected
    groups = width // lanes
    mixed, log_total, mixed_here = [], [], []
    for g in range(groups):
        one_mixed, one_total = attend_forward2(
            queries, keys, values, start, min(1024, length), g, tuple(mixed[-1:])
        )
        mixed.append(one_mixed)
        log_total.append(one_total)
        mixed_here.append(
            lax.all_to_all(one_mixed, "head", 0, 0, tiled=True).reshape(ranks, chunk, lanes)
        )

    far_half, out_half = assemble(rank, bundles, rows, (mixed_here[0], mixed[-1]))
    far_half = far_half.reshape(3 * part, model)
    far_other, out_other = swap(far_half, "dp", 1), swap(out_half, "dp", 1)
    first = core == 0
    out_all = jnp.concatenate(
        [jnp.where(first, out_half, out_other), jnp.where(first, out_other, out_half)], axis=1
    )

    residual = tokens.astype(f32)
    hidden_state = residual + sum(
        jnp.einsum("htk,hkd->td", m, out_all[:, g * lanes : (g + 1) * lanes], preferred_element_type=f32)
        for g, m in enumerate(mixed_here)
    )
    mlp_scale = rms_scale(hidden_state)
    mlp_input = (hidden_state * mlp_scale * mlp_gain).astype(bf16)
    mlp_input_near = swap(mlp_input, "mlp", 1)

    acts, terms = feed(mlp_input, out_grad, stack, far_half, far_other, f32)
    acts_near, terms_near = feed(
        mlp_input_near, out_grad_near, stack, far_half, far_other, bf16, (terms,)
    )
    terms_back = swap(terms_near, "mlp", 1)
    scalars = jnp.stack([core, rank]).astype(jnp.int32)
    tokens_two = (acts, acts_near, mlp_input, mlp_input_near, out_grad, out_grad_near)
    far_other_grads, own_other_grads, down_here, down_near = others(
        scalars, *tokens_two, stack, far_half, far_other
    )
    terms_back = after(terms_back, down_near)
    far_half_got = swap(after(far_other_grads, terms_back), "dp", 1)
    own_half_got = swap(after(own_other_grads, far_half_got), "dp", 1)
    state_grad, state_grad_low, mixed_grad, mlp_gain_grad = state_back(
        terms_back, terms, hidden_state, out_grad, mlp_gain[None], out_all
    )
    mlp_gain_grad = mlp_gain_grad[0]
    mixed_grad_rows = lax.all_to_all(mixed_grad, "head", 0, 0, tiled=True).reshape(length, width)

    low_grad = after(state_grad_low, mixed_grad)
    out_grads = [
        jnp.einsum("htk,td->hkd", m, low_grad, preferred_element_type=f32).astype(bf16)
        for m in mixed_here
    ]
    out_grads = jnp.concatenate(out_grads, axis=1).reshape(ranks, 2, half_out, model)
    out_got = swap(lax.dynamic_index_in_dim(out_grads, 1 - core, 1, False), "dp", 1)
    out_own = lax.dynamic_index_in_dim(out_grads, core, 1, False)
    far_half_got = after(far_half_got, mixed_grad)
    far_chip = shard_grads(scalars, ranks, True, *tokens_two, [far_half_got])
    far_got = [swap(f, "head", e) for e, f in enumerate(far_chip) if e]
    own_half_got = after(own_half_got, far_chip[0])
    own_chip = shard_grads(scalars, ranks, False, *tokens_two, [own_half_got, out_own, out_got])
    mixed_grad_rows = after(mixed_grad_rows, own_chip[0])

    down_back = swap(after(down_near, mixed_grad_rows), "mlp", 1)
    back_args = (queries, keys, values, mixed_grad_rows, start, cosine, sine, block)
    grads = attend_backward(*back_args, 0, mixed[0], log_total[0])
    far_got = [after(f, grads[0]) for f in far_got]
    far_sum = add_low(far_chip[0], *far_got)
    far_here = swap(far_sum, "mlp", 2)
    own_chip = [own_chip[0]] + [after(f, far_sum) for f in own_chip[1:]]
    own_got = [swap(f, "head", e) for e, f in enumerate(own_chip) if e]
    for g in range(1, width // lanes):
        grads = attend_backward(
            *back_args, g, mixed[g], log_total[g], grads, (far_sum, down_back, *own_chip[1:])
        )
    proj_grad, first_values_grad = grads
    cut = cut_of(chunk)
    half_proj = model // 2
    proj_wgrad = dot(gathered, proj_grad, TN).astype(bf16)
    proj_got = swap(block_of(proj_wgrad, 1 - core, half_proj), "dp", 1)
    if ranks == 4:
        (low, high), gain_last = unproject(
            rank, row_parts[3:], 3, ((cut, chunk - cut),), w_project, proj_grad, (proj_wgrad,)
        )
        for_two, for_one = swap(low, "head", 1), swap(high, "head", 2)
        own_got = [after(f, low) for f in own_got]
    else:
        own_got = [after(f, proj_grad) for f in own_got]
    own_all = (own_chip[0], *own_got)
    piece_sum = add_low(*(f[: 3 * rows] for f in own_all), far_here.reshape(3 * rows, model))
    out_sum = add_low(*(f[3 * rows :] for f in own_all))
    proj_mine = add_low(block_of(proj_wgrad, core, half_proj), proj_got)
    both_mine = jnp.concatenate([proj_mine, out_sum.reshape(half_proj, -1)], axis=1)
    line, count = lax.axis_index("mlp"), lax.axis_size("mlp")

    def line_sum(x):
        size = x.shape[0] // count
        return collect([block_of(x, line ^ e, size) for e in range(count)], "mlp").astype(bf16)

    if ranks == 4:
        cut_p = cut_of(3 * rows)
        cut_q = 3 * rows - cut_p
        low_p, high_p = piece_sum[:cut_p], piece_sum[cut_p:]
        low_x, high_y = swap(low_p, "head", 1), swap(high_p, "head", 2)
        low_yy = swap(jnp.concatenate([low_p, low_x]), "head", 2)
        high_xx = swap(jnp.concatenate([high_p, high_y]), "head", 1)
        (own, one, two), gain_rest = unproject(
            rank,
            row_parts[:3],
            0,
            ((chunk,),) * 3,
            w_project,
            proj_grad,
            (piece_sum, both_mine),
        )
        attn_gain_grad = gain_last + gain_rest
        one = after(one.at[cut:].set(add_low(one[cut:], for_one)), low_yy, high_xx)
        two = after(two.at[:cut].set(add_low(two[:cut], for_two)), low_yy, high_xx)
        one_got, two_got = swap(one, "head", 1), swap(two, "head", 2)
        half_sum = regroup(
            rank,
            [
                ((low_p, 0, cut_p), (high_p, 0, cut_q)),
                ((low_x, 0, cut_p), (high_xx, 0, cut_q)),
                ((low_yy, 0, cut_p), (high_y, 0, cut_q)),
                ((low_yy, 1, cut_p), (high_xx, 1, cut_q)),
            ],
            rows,
        )
        line_piece = after(line_sum(both_mine), one, two, half_sum)
        attn_normed_grad = own.astype(f32) + one_got.astype(f32) + two_got.astype(f32)
        ended = (one_got, two_got)
    else:
        parts, attn_gain_grad = unproject(
            rank, row_parts, 0, ((chunk,),) * ranks, w_project, proj_grad
        )
        half_sum = jnp.zeros((3, ranks, rows, model), bf16)
        for e, piece in enumerate(spread(piece_sum, "head")):
            piece = piece.reshape(3, 1, rows, model)
            half_sum = lax.dynamic_update_slice_in_dim(half_sum, piece, rank ^ e, 1)
        attn_normed_grad = collect(parts, "head")
        ended = (attn_normed_grad,)
        line_piece = line_sum(both_mine)
    half_sum = half_sum.reshape(3, part, model)

    norm_row = jnp.zeros((model,), f32).at[:2].set(jnp.sum(norms[:2], axis=1))
    if count == 4:
        line_one = swap(line_piece, "mlp", 1)
        line_two = swap(jnp.concatenate([line_piece, line_one]), "mlp", 2)
        size = line_piece.shape[0]
        line_got = [line_piece, line_one, line_two[:size], line_two[size:]]
    else:
        line_got = spread(line_piece, "mlp")
    small = jnp.stack([attn_gain_grad[0], mlp_gain_grad, norm_row])
    small = sum_over_all(after(small, line_got[1]))
    output = (hidden_state + after(down_back, line_piece).astype(f32) + down_here).astype(bf16)

    half_sum = after(half_sum, line_piece)
    other_sum = swap(half_sum, "dp", 1)
    ff_grads = jnp.concatenate(
        [jnp.where(first, half_sum, other_sum), jnp.where(first, other_sum, half_sum)], axis=1
    ).astype(f32)
    gate_wgrad, up_wgrad, down_wgrad = ff_grads[0].T, ff_grads[1].T, ff_grads[2]
    input_grad = (
        state_grad + norm_back(residual, rms_scale(residual), attn_gain, attn_normed_grad)
    ).astype(bf16)

    line_got = [after(line_got[0], output, input_grad, down_wgrad, small)] + line_got[1:]
    both_half = in_order(line_got, line)
    both_other = swap(both_half, "dp", 1)
    proj_sum = both_cores(both_half[:, : 3 * width], both_other[:, : 3 * width], core).astype(f32)
    query_wgrad, key_wgrad, value_wgrad = (
        jnp.concatenate(
            [proj_sum[:, (3 * g + k) * lanes : (3 * g + k + 1) * lanes] for g in range(width // lanes)],
            axis=1,
        )
        for k in range(3)
    )
    out_wgrad = both_cores(
        both_half[:, 3 * width :].reshape(half_out, model),
        both_other[:, 3 * width :].reshape(half_out, model),
        core,
    ).astype(f32)

    devices = lax.axis_size("dp") * ranks * count
    value_norms = small[2, :2] / (length * (width // HEAD_DIM) * devices)
    return (
        output[:, None],
        input_grad[:, None],
        first_values_grad[:, None],
        small[0],
        query_wgrad,
        key_wgrad,
        value_wgrad,
        out_wgrad,
        small[1],
        gate_wgrad,
        up_wgrad,
        down_wgrad,
        value_norms,
    )


def solution(mesh):
    placed = (
        P("head", ("dp", "mlp"), None),
        P(None, ("dp", "mlp"), "head"),
        P(None, ("dp", "mlp")),
        P(None, ("dp", "mlp")),
        P(),
        P(None, "head"),
        P(None, "head"),
        P(None, "head"),
        P("head", None),
        P(),
        P(None, "mlp"),
        P(None, "mlp"),
        P("mlp", None),
        P("head", ("dp", "mlp"), None),
    )
    return jax.shard_map(
        on_device,
        mesh=mesh,
        in_specs=placed,
        out_specs=(
            P("head", ("dp", "mlp"), None),
            P("head", ("dp", "mlp"), None),
            P(None, ("dp", "mlp"), "head"),
            P(),
            P(None, "head"),
            P(None, "head"),
            P(None, "head"),
            P("head", None),
            P(),
            P(None, "mlp"),
            P(None, "mlp"),
            P("mlp", None),
            P(),
        ),
        check_vma=False,
    )
```

profile of v0, /device:TPU:0, one launch (start us, length us, event | category | flops | bytes accessed | tf_op | source)
XLA Modules:
  0.0 409.3 jit_solution(15421485780155228598)
XLA Ops:
  0.7 3.0 collective-permute-start
  5.2 2.6 pad_maximum_fusion.refs_0_.refs_1_.refs_2_
  7.9 2.1 copy-done.11
  10.0 2.7 collective-permute-start.4
  19.0 5.5 %fusion.9 = (f32[2048,128]{1,0:T(8,128)}, f32[2048,128]{1,0:T(8,128)}) fusion(f32[128]{0:T(128)S(1)} %get-tuple-element.175, f32[128]{0:T(128)S(1)} %get-tuple-element.176, f32[2048]{0:T(1024)S(1)} %bitcast.90), kind=kLoop, calls=%fused_computation.45 | loop fusion | flops 524288 | bytes 2106368 | tf_op jit(solution)/shard_map/mul | solution.py:839
  24.6 2.6 collective-permute-done.refs_2_
  32.7 13.4 %project.2 = (bf16[2048,1024]{1,0:T(8,128)(2,1)}, bf16[2048,256]{1,0:T(8,128)(2,1)}, bf16[2048,256]{1,0:T(8,128)(2,1)}, bf16[2048,256]{1,0:T(8,128)(2,1)}, f32[8,128]{1,0:T(8,128)}) custom-call(s32[1]{0:T(128)} %bitcast.2.rank_ref, bf16[512,1024]{1,0:T(8,128)(2,1)} %bitcast.79, bf16[512,1024]{1,0:T(8,128)(2,1)} %collective-permute-done.2.refs_1_, ...), custom_call_target="tpu_custom_call" | custom-call | flops 14849999872 | bytes 1350000 | tf_op jit(solution)/shard_map/project/pallas_call | solution.py:359
  49.2 2.7 collective-permute-start.7
  51.9 4.7 %project.3 = (bf16[2048,1024]{1,0:T(8,128)(2,1)}, bf16[2048,256]{1,0:T(8,128)(2,1)}, bf16[2048,256]{1,0:T(8,128)(2,1)}, bf16[2048,256]{1,0:T(8,128)(2,1)}, f32[8,128]{1,0:T(8,128)}) custom-call(s32[1]{0:T(128)} %bitcast.2.rank_ref, bf16[256,1024]{1,0:T(8,128)(2,1)} %copy-done.37, ...), custom_call_target="tpu_custom_call", output_to_operand_aliasing={{0}: (8, {}), {1}: (9, {}), {2}: (10, {}), {3}: (11, {})} | custom-call | flops 4950000128 | bytes 450000 | tf_op jit(solution)/shard_map/project/pallas_call | solution.py:359
  56.6 12.0 %attend_forward.2 = (bf16[2048,128]{1,0:T(8,128)(2,1)}, f32[1,8,2048]{2,1,0:T(8,128)}) custom-call(s32[2]{0:T(128)} %slice.174.firsts, s32[2]{0:T(128)} %slice.175.lasts, bf16[2048,256]{1,0:T(8,128)(2,1)} %get-tuple-element.100.q_ref, bf16[2048,256]{1,0:T(8,128)(2,1)} %get-tuple-element.101.k_ref, bf16[2048,256]{1,0:T(8,128)(2,1)} %get-tuple-element.102.v_ref, ...), custom_call_target="tpu_custom_call" | custom-call | flops 15569256448 | bytes 2097152 | tf_op jit(solution)/shard_map/attend_forward/pallas_call | solution.py:89
  68.6 3.7 all-to-all-start
  72.4 11.8 %attend_forward.3 = (bf16[2048,128]{1,0:T(8,128)(2,1)}, f32[1,8,2048]{2,1,0:T(8,128)}) custom-call(s32[2]{0:T(128)} %slice.174.firsts, s32[2]{0:T(128)} %slice.175.lasts, bf16[2048,256]{1,0:T(8,128)(2,1)} %get-tuple-element.100.q_ref, bf16[2048,256]{1,0:T(8,128)(2,1)} %get-tuple-element.101.k_ref, bf16[2048,256]{1,0:T(8,128)(2,1)} %get-tuple-element.102.v_ref, ...), custom_call_target="tpu_custom_call" | custom-call | flops 15569256448 | bytes 2097152 | tf_op jit(solution)/shard_map/attend_forward/pallas_call | solution.py:89
  84.2 5.5 %all-to-all-done.refs_4_ = bf16[4,512,128]{2,1,0:T(8,128)(2,1)S(1)} async-done(((bf16[4,512,128]{2,1,0:T(8,128)(2,1)}), bf16[4,512,128]{2,1,0:T(8,128)(2,1)S(1)}, u32[]{:S(2)}, u32[]{:S(2)}) %all-to-all-start) | async-done | bytes 524320 | tf_op jit(solution)/shard_map/all_to_all | solution.py:856
  91.0 4.0 assemble.1
  97.7 3.9 all-to-all-start.1
  105.4 4.3 %all-to-all-done.1 = bf16[4,512,128]{2,1,0:T(8,128)(2,1)S(1)} async-done(((bf16[4,512,128]{2,1,0:T(8,128)(2,1)}), bf16[4,512,128]{2,1,0:T(8,128)(2,1)S(1)}, u32[]{:S(2)}, u32[]{:S(2)}) %all-to-all-start.1) | async-done | bytes 524320 | tf_op jit(solution)/shard_map/all_to_all | solution.py:856
  109.7 2.7 multiply_reduce_fusion
  113.9 16.5 %feed.2 = (bf16[4,3,352,512]{3,2,1,0:T(8,128)(2,1)}, f32[512,1024]{1,0:T(8,128)}) custom-call(bf16[512,1024]{1,0:T(8,128)(2,1)} %copy-done.31, bf16[512,1024]{1,0:T(8,128)(2,1)} %bitcast.17.g_ref.grad_ref.refs_4_, bf16[2112,1024]{1,0:T(8,128)(2,1)} %copy-done.11, bf16[2112,1024]{1,0:T(8,128)(2,1)} %copy-done.11, bf16[2112,1024]{1,0:T(8,128)(2,1)} %copy-done.11, ...), custom_call_target="tpu_custom_call" | custom-call | flops 17600000000 | bytes 1600000 | tf_op jit(solution)/shard_map/feed/pallas_call | solution.py:445
  130.4 12.9 %collective-permute-done.10.x_ref.xn_ref.refs_3_ = bf16[512,1024]{1,0:T(8,128)(2,1)S(1)} collective-permute-done((bf16[512,1024]{1,0:T(8,128)(2,1)S(1)}, bf16[512,1024]{1,0:T(8,128)(2,1)S(1)}, u32[]{:S(2)}, u32[]{:S(2)}) %collective-permute-start.10) | collective-permute-done | bytes 1048608 | tf_op jit(solution)/shard_map/ppermute | solution.py:182
  144.2 16.3 %feed.3 = (bf16[4,3,352,512]{3,2,1,0:T(8,128)(2,1)}, bf16[512,1024]{1,0:T(8,128)(2,1)}) custom-call(bf16[512,1024]{1,0:T(8,128)(2,1)} %copy-done.50, bf16[512,1024]{1,0:T(8,128)(2,1)} %collective-permute-done.11.g_ref.gn_ref.refs_5_, bf16[2112,1024]{1,0:T(8,128)(2,1)} %copy-done.11, bf16[2112,1024]{1,0:T(8,128)(2,1)} %copy-done.11, ...), custom_call_target="tpu_custom_call" | custom-call | flops 17600000000 | bytes 1600000 | tf_op jit(solution)/shard_map/feed/pallas_call | solution.py:445
  162.2 18.9 %others.1 = (bf16[1056,1024]{1,0:T(8,128)(2,1)}, bf16[1056,1024]{1,0:T(8,128)(2,1)}, f32[512,1024]{1,0:T(8,128)}, bf16[512,1024]{1,0:T(8,128)(2,1)}) custom-call(s32[2]{0:T(128)} %pad_add_fusion.scalars, bf16[4,3,352,512]{3,2,1,0:T(8,128)(2,1)} %get-tuple-element.107.act_ref.refs_0_, bf16[4,3,352,512]{3,2,1,0:T(8,128)(2,1)} %get-tuple-element.109.near_ref.refs_1_, ...), custom_call_target="tpu_custom_call" | custom-call | flops 20899999744 | bytes 1900000 | tf_op jit(solution)/shard_map/others/pallas_call | solution.py:627
  181.1 4.1 collective-permute-done.12.refs_0_
  187.1 2.6 collective-permute-done.13.refs_1_.refs_0_
  189.9 8.2 %state_back.1 = (f32[512,1024]{1,0:T(8,128)}, bf16[512,1024]{1,0:T(8,128)(2,1)}, bf16[4,512,256]{2,1,0:T(8,128)(2,1)}, f32[1,1024]{1,0:T(1,128)}) custom-call(bf16[512,1024]{1,0:T(8,128)(2,1)} %after.26.back_ref.refs_1_, f32[512,1024]{1,0:T(8,128)} %get-tuple-element.108.refs_9_.terms_ref, f32[512,1024]{1,0:T(8,128)} %copy-done.3, ...), custom_call_target="tpu_custom_call" | custom-call | flops 6600000000 | bytes 600000 | tf_op jit(solution)/shard_map/state_back/pallas_call | solution.py:763
  203.6 3.8 all-to-all-start.2
  207.3 8.0 %far_sum.1 = (bf16[3,88,1024]{2,1,0:T(8,128)(2,1)}, bf16[3,88,1024]{2,1,0:T(8,128)(2,1)}, bf16[3,88,1024]{2,1,0:T(8,128)(2,1)}, bf16[3,88,1024]{2,1,0:T(8,128)(2,1)}) custom-call(s32[2]{0:T(128)} %pad_add_fusion.scalars, bf16[4,3,352,512]{3,2,1,0:T(8,128)(2,1)} %get-tuple-element.107.act_ref.refs_0_, ...), custom_call_target="tpu_custom_call" | custom-call | flops 8800000000 | bytes 800000 | tf_op jit(solution)/shard_map/far_sum/pallas_call | solution.py:561
  218.8 9.5 %own_sum.1 = (bf16[392,1024]{1,0:T(8,128)(2,1)}, bf16[392,1024]{1,0:T(8,128)(2,1)}, bf16[392,1024]{1,0:T(8,128)(2,1)}, bf16[392,1024]{1,0:T(8,128)(2,1)}) custom-call(s32[2]{0:T(128)} %pad_add_fusion.scalars, bf16[4,3,352,512]{3,2,1,0:T(8,128)(2,1)} %get-tuple-element.107.act_ref.refs_0_, bf16[4,3,352,512]{3,2,1,0:T(8,128)(2,1)} %get-tuple-element.109.near_ref.refs_1_, ...), custom_call_target="tpu_custom_call" | custom-call | flops 8800000000 | bytes 800000 | tf_op jit(solution)/shard_map/own_sum/pallas_call | solution.py:561
  230.9 21.8 %attend_backward.2 = (bf16[2048,768]{1,0:T(8,128)(2,1)}, bf16[2048,256]{1,0:T(8,128)(2,1)}) custom-call(s32[4]{0:T(128)} %get-tuple-element.172.full_end, s32[4]{0:T(128)} %get-tuple-element.171.some_end, bf16[2048,256]{1,0:T(8,128)(2,1)} %get-tuple-element.100.q_ref, bf16[2048,256]{1,0:T(8,128)(2,1)} %get-tuple-element.101.k_ref, ...), custom_call_target="tpu_custom_call" | custom-call | flops 27917287424 | bytes 5767168 | tf_op jit(solution)/shard_map/attend_backward/pallas_call | solution.py:168
  261.8 22.5 %attend_backward.3 = (bf16[2048,768]{1,0:T(8,128)(2,1)}, bf16[2048,256]{1,0:T(8,128)(2,1)}) custom-call(s32[4]{0:T(128)} %get-tuple-element.172.full_end, s32[4]{0:T(128)} %get-tuple-element.171.some_end, bf16[2048,256]{1,0:T(8,128)(2,1)} %get-tuple-element.100.q_ref, ...), custom_call_target="tpu_custom_call", output_to_operand_aliasing={{0}: (16, {}), {1}: (17, {})} | custom-call | flops 27917287424 | bytes 5767168 | tf_op jit(solution)/shard_map/attend_backward/pallas_call | solution.py:168
  284.3 6.7 %convolution_convert_fusion.refs_4_ = bf16[1024,768]{1,0:T(8,128)(2,1)S(1)} fusion(bf16[2048,1024]{1,0:T(8,128)(2,1)} %get-tuple-element.118, bf16[2048,768]{1,0:T(8,128)(2,1)} %get-tuple-element.129.refs_3_.refs_4_), kind=kOutput, calls=%fused_computation.31 | convolution fusion | flops 3222011904 | bytes 8912896 | tf_op jit(solution)/shard_map/dot_general | solution.py:18
  292.4 3.9 unproject.2
  305.3 3.4 collective-permute-done.29.refs_2_
  311.4 2.1 collective-permute-start.32
  317.1 9.3 %unproject.3 = (bf16[512,1024]{1,0:T(8,128)(2,1)}, bf16[512,1024]{1,0:T(8,128)(2,1)}, bf16[512,1024]{1,0:T(8,128)(2,1)}, f32[1,1024]{1,0:T(1,128)}) custom-call(s32[1]{0:T(128)} %bitcast.2.rank_ref, bf16[512,1024]{1,0:T(8,128)(2,1)} %bitcast.80, bf16[512,1024]{1,0:T(8,128)(2,1)} %collective-permute-done.2.refs_1_, ...), custom_call_target="tpu_custom_call" | custom-call | flops 11550000128 | bytes 1050000 | tf_op jit(solution)/shard_map/unproject/pallas_call | solution.py:728
  326.5 2.2 fusion.13.refs_0_
  328.7 4.4 %collective-permute-start.26 = (bf16[128,1024]{1,0:T(8,128)(2,1)S(1)}, bf16[128,1024]{1,0:T(8,128)(2,1)S(1)}, u32[]{:S(2)}, u32[]{:S(2)}) collective-permute-start(bf16[128,1024]{1,0:T(8,128)(2,1)S(1)} %get-tuple-element.166), channel_id=1, source_target_pairs={{0,3},{1,2},{2,1},{3,0},{4,7},{5,6},{6,5},{7,4},{8,11},{9,10},{10,... | collective-permute-start | bytes 786440 | tf_op jit(solution)/shard_map/ppermute | solution.py:182
  338.8 3.6 regroup.1.refs_3_
  342.4 3.0 collective-permute-done.25
  347.2 4.8 %collective-permute-start.36 = (bf16[128,1024]{1,0:T(8,128)(2,1)S(1)}, bf16[128,1024]{1,0:T(8,128)(2,1)S(1)}, u32[]{:S(2)}, u32[]{:S(2)}) collective-permute-start(bf16[128,1024]{1,0:T(8,128)(2,1)S(1)} %copy-done.5), channel_id=1, source_target_pairs={{0,1},{1,0},{2,3},{3,2},{4,5},{5,4},{6,7},{7,6},{8,9},{9,8},{10,11... | collective-permute-start | bytes 786440 | tf_op jit(solution)/shard_map/ppermute | solution.py:182
  352.8 5.4 %collective-permute-done.36.refs_1_ = bf16[128,1024]{1,0:T(8,128)(2,1)S(1)} collective-permute-done((bf16[128,1024]{1,0:T(8,128)(2,1)S(1)}, bf16[128,1024]{1,0:T(8,128)(2,1)S(1)}, u32[]{:S(2)}, u32[]{:S(2)}) %collective-permute-start.36) | collective-permute-done | bytes 262176 | tf_op jit(solution)/shard_map/ppermute | solution.py:182
  360.6 2.2 collective-permute-done.37
  365.0 3.2 collective-permute-done.38
  370.3 3.6 add_convert_fusion.refs_1_
  378.3 2.5 fusion
  380.9 3.7 fusion.6.refs_2_
  384.5 2.2 broadcast_select_fusion.1
  387.9 3.7 slice_bitcast_fusion
  392.7 8.4 %collective-permute-done.43 = bf16[256,1024]{1,0:T(8,128)(2,1)S(1)} collective-permute-done((bf16[256,1024]{1,0:T(8,128)(2,1)S(1)}, bf16[256,1024]{1,0:T(8,128)(2,1)S(1)}, u32[]{:S(2)}, u32[]{:S(2)}) %collective-permute-start.43) | collective-permute-done | bytes 524320 | tf_op jit(solution)/shard_map/ppermute | solution.py:182
  (282 shorter events, 97.1 us)
Async XLA Ops:
  0.7 26.5 %collective-permute-start = (bf16[512,1024]{1,0:T(8,128)(2,1)}, bf16[512,1024]{1,0:T(8,128)(2,1)}, u32[]{:S(2)}, u32[]{:S(2)}) collective-permute-start(bf16[512,1024]{1,0:T(8,128)(2,1)} %bitcast.77), channel_id=1, source_target_pairs={{0,8},{4,12},{8,0},{12,4},{1,9},{5,13},{9,1},{13,5},{2,10},{6,14},... | collective-permute-start | bytes 3145736 | tf_op jit(solution)/shard_map/ppermute | solution.py:182
  3.7 26.3 %collective-permute-start.2 = (bf16[512,1024]{1,0:T(8,128)(2,1)}, bf16[512,1024]{1,0:T(8,128)(2,1)}, u32[]{:S(2)}, u32[]{:S(2)}) collective-permute-start(bf16[512,1024]{1,0:T(8,128)(2,1)} %bitcast.78), channel_id=1, source_target_pairs={{0,4},{4,0},{8,12},{12,8},{1,5},{5,1},{9,13},{13,9},{2,6},{6,2},{1... | collective-permute-start | bytes 3145736 | tf_op jit(solution)/shard_map/ppermute | solution.py:182
  10.0 36.1 %collective-permute-start.4 = (bf16[3,88,1024]{2,1,0:T(8,128)(2,1)S(1)}, bf16[3,88,1024]{2,1,0:T(8,128)(2,1)S(1)}, u32[]{:S(2)}, u32[]{:S(2)}) collective-permute-start(bf16[3,88,1024]{2,1,0:T(8,128)(2,1)S(1)} %dynamic-slice_bitcast_fusion.2), channel_id=1, source_target_pairs={{0,2},{1,3},{2,0},{3,1},{4,6},{5,7},{6,4},{7,5},{8,10},{9,11},{10,... | collective-permute-start | bytes 1622024 | tf_op jit(solution)/shard_map/ppermute | solution.py:182
  28.3 17.8 %collective-permute-start.1 = (bf16[256,1024]{1,0:T(8,128)(2,1)S(1)}, bf16[256,1024]{1,0:T(8,128)(2,1)S(1)}, u32[]{:S(2)}, u32[]{:S(2)}) collective-permute-start(bf16[256,1024]{1,0:T(8,128)(2,1)S(1)} %slice.216), channel_id=1, source_target_pairs={{0,4},{4,0},{8,12},{12,8},{1,5},{5,1},{9,13},{13,9},{2,6},{6,2},{1... | collective-permute-start | bytes 1572872 | tf_op jit(solution)/shard_map/ppermute | solution.py:182
  31.1 15.0 %collective-permute-start.3 = (bf16[256,1024]{1,0:T(8,128)(2,1)S(1)}, bf16[256,1024]{1,0:T(8,128)(2,1)S(1)}, u32[]{:S(2)}, u32[]{:S(2)}) collective-permute-start(bf16[256,1024]{1,0:T(8,128)(2,1)S(1)} %slice.217), channel_id=1, source_target_pairs={{0,8},{4,12},{8,0},{12,4},{1,9},{5,13},{9,1},{13,5},{2,10},{6,14},... | collective-permute-start | bytes 1572872 | tf_op jit(solution)/shard_map/ppermute | solution.py:182
  48.3 41.4 %collective-permute-start.5 = (bf16[392,1024]{1,0:T(8,128)(2,1)S(1)}, bf16[392,1024]{1,0:T(8,128)(2,1)S(1)}, u32[]{:S(2)}, u32[]{:S(2)}) collective-permute-start(bf16[392,1024]{1,0:T(8,128)(2,1)S(1)} %pad_maximum_fusion.7.refs_0_), channel_id=1, source_target_pairs={{0,4},{4,0},{8,12},{12,8},{1,5},{5,1},{9,13},{13,9},{2,6},{6,2},{1... | collective-permute-start | bytes 2408456 | tf_op jit(solution)/shard_map/ppermute | solution.py:182
  48.9 40.8 %collective-permute-start.6 = (bf16[392,1024]{1,0:T(8,128)(2,1)S(1)}, bf16[392,1024]{1,0:T(8,128)(2,1)S(1)}, u32[]{:S(2)}, u32[]{:S(2)}) collective-permute-start(bf16[392,1024]{1,0:T(8,128)(2,1)S(1)} %pad_maximum_fusion.7.refs_0_), channel_id=1, source_target_pairs={{0,8},{4,12},{8,0},{12,4},{1,9},{5,13},{9,1},{13,5},{2,10},{6,14},... | collective-permute-start | bytes 2408456 | tf_op jit(solution)/shard_map/ppermute | solution.py:182
  49.2 40.5 %collective-permute-start.7 = (bf16[392,1024]{1,0:T(8,128)(2,1)S(1)}, bf16[392,1024]{1,0:T(8,128)(2,1)}, u32[]{:S(2)}, u32[]{:S(2)}) collective-permute-start(bf16[392,1024]{1,0:T(8,128)(2,1)S(1)} %pad_maximum_fusion.7.refs_0_), channel_id=1, source_target_pairs={{0,12},{4,8},{8,4},{12,0},{1,13},{5,9},{9,5},{13,1},{2,14},{6,10},... | collective-permute-start | bytes 2408456 | tf_op jit(solution)/shard_map/ppermute | solution.py:182
  68.6 21.1 %all-to-all-start = ((bf16[4,512,128]{2,1,0:T(8,128)(2,1)}), bf16[4,512,128]{2,1,0:T(8,128)(2,1)S(1)}, u32[]{:S(2)}, u32[]{:S(2)}) async-start(bf16[4,512,128]{2,1,0:T(8,128)(2,1)} %bitcast.88), calls=%async_computation | async-start | bytes 1048576 | tf_op jit(solution)/shard_map/all_to_all | solution.py:856
  95.0 6.6 %collective-permute-start.8 = (bf16[4,128,1024]{2,1,0:T(8,128)(2,1)}, bf16[4,128,1024]{2,1,0:T(8,128)(2,1)}, u32[]{:S(2)}, u32[]{:S(2)}) collective-permute-start(bf16[4,128,1024]{2,1,0:T(8,128)(2,1)} %get-tuple-element.105), channel_id=1, source_target_pairs={{0,16},{16,0},{1,17},{17,1},{2,18},{18,2},{3,19},{19,3},{4,20},{20... | collective-permute-start | bytes 3145736 | tf_op jit(solution)/shard_map/ppermute | solution.py:182
  95.0 18.3 %collective-permute-start.9 = (bf16[1056,1024]{1,0:T(8,128)(2,1)}, bf16[1056,1024]{1,0:T(8,128)(2,1)}, u32[]{:S(2)}, u32[]{:S(2)}) collective-permute-start(bf16[1056,1024]{1,0:T(8,128)(2,1)} %bitcast.97), channel_id=1, source_target_pairs={{0,16},{16,0},{1,17},{17,1},{2,18},{18,2},{3,19},{19,3},{4,20},{20... | collective-permute-start | bytes 6488072 | tf_op jit(solution)/shard_map/ppermute | solution.py:182
  95.5 34.9 %collective-permute-start.11 = (bf16[512,1024]{1,0:T(8,128)(2,1)}, bf16[512,1024]{1,0:T(8,128)(2,1)}, u32[]{:S(2)}, u32[]{:S(2)}) collective-permute-start(bf16[512,1024]{1,0:T(8,128)(2,1)} %bitcast.17.g_ref.grad_ref.refs_4_), channel_id=1, source_target_pairs={{0,1},{1,0},{2,3},{3,2},{4,5},{5,4},{6,7},{7,6},{8,9},{9,8},{10,11... | collective-permute-start | bytes 3145736 | tf_op jit(solution)/shard_map/ppermute | solution.py:182
  97.7 12.1 %all-to-all-start.1 = ((bf16[4,512,128]{2,1,0:T(8,128)(2,1)}), bf16[4,512,128]{2,1,0:T(8,128)(2,1)S(1)}, u32[]{:S(2)}, u32[]{:S(2)}) async-start(bf16[4,512,128]{2,1,0:T(8,128)(2,1)} %bitcast.14), calls=%async_computation.1 | async-start | bytes 1048576 | tf_op jit(solution)/shard_map/all_to_all | solution.py:856
  112.8 30.5 %collective-permute-start.10 = (bf16[512,1024]{1,0:T(8,128)(2,1)S(1)}, bf16[512,1024]{1,0:T(8,128)(2,1)S(1)}, u32[]{:S(2)}, u32[]{:S(2)}) collective-permute-start(bf16[512,1024]{1,0:T(8,128)(2,1)S(1)} %multiply_convert_fusion.x_ref.refs_2_), channel_id=1, source_target_pairs={{0,1},{1,0},{2,3},{3,2},{4,5},{5,4},{6,7},{7,6},{8,9},{9,8},{10,11... | collective-permute-start | bytes 3145736 | tf_op jit(solution)/shard_map/ppermute | solution.py:182
  160.6 24.6 %collective-permute-start.12 = (bf16[512,1024]{1,0:T(8,128)(2,1)}, bf16[512,1024]{1,0:T(8,128)(2,1)}, u32[]{:S(2)}, u32[]{:S(2)}) collective-permute-start(bf16[512,1024]{1,0:T(8,128)(2,1)} %get-tuple-element.111), channel_id=1, source_target_pairs={{0,1},{1,0},{2,3},{3,2},{4,5},{5,4},{6,7},{7,6},{8,9},{9,8},{10,11... | collective-permute-start | bytes 3145736 | tf_op jit(solution)/shard_map/ppermute | solution.py:182
  185.2 4.6 %collective-permute-start.13 = (bf16[1056,1024]{1,0:T(8,128)(2,1)}, bf16[1056,1024]{1,0:T(8,128)(2,1)}, u32[]{:S(2)}, u32[]{:S(2)}) collective-permute-start(bf16[1056,1024]{1,0:T(8,128)(2,1)} %after.27), channel_id=1, source_target_pairs={{0,16},{16,0},{1,17},{17,1},{2,18},{18,2},{3,19},{19,3},{4,20},{20... | collective-permute-start | bytes 6488072 | tf_op jit(solution)/shard_map/ppermute | solution.py:182
  189.8 29.1 %collective-permute-start.14 = (bf16[1056,1024]{1,0:T(8,128)(2,1)}, bf16[1056,1024]{1,0:T(8,128)(2,1)}, u32[]{:S(2)}, u32[]{:S(2)}) collective-permute-start(bf16[1056,1024]{1,0:T(8,128)(2,1)} %after.28), channel_id=1, source_target_pairs={{0,16},{16,0},{1,17},{17,1},{2,18},{18,2},{3,19},{19,3},{4,20},{20... | collective-permute-start | bytes 6488072 | tf_op jit(solution)/shard_map/ppermute | solution.py:182
  202.6 16.2 %collective-permute-start.15 = (bf16[4,128,1024]{2,1,0:T(8,128)(2,1)}, bf16[4,128,1024]{2,1,0:T(8,128)(2,1)}, u32[]{:S(2)}, u32[]{:S(2)}) collective-permute-start(bf16[4,128,1024]{2,1,0:T(8,128)(2,1)} %get-tuple-element.160), channel_id=1, source_target_pairs={{0,16},{16,0},{1,17},{17,1},{2,18},{18,2},{3,19},{19,3},{4,20},{20... | collective-permute-start | bytes 3145736 | tf_op jit(solution)/shard_map/ppermute | solution.py:182
  203.6 24.8 %all-to-all-start.2 = ((bf16[4,512,256]{2,1,0:T(8,128)(2,1)}), bf16[4,512,256]{2,1,0:T(8,128)(2,1)S(1)}, u32[]{:S(2)}, u32[]{:S(2)}) async-start(bf16[4,512,256]{2,1,0:T(8,128)(2,1)} %get-tuple-element.112.refs_1_), calls=%async_computation.2 | async-start | bytes 2097152 | tf_op jit(solution)/shard_map/all_to_all | solution.py:893
  215.3 37.5 %collective-permute-start.17 = (bf16[3,88,1024]{2,1,0:T(8,128)(2,1)}, bf16[3,88,1024]{2,1,0:T(8,128)(2,1)}, u32[]{:S(2)}, u32[]{:S(2)}) collective-permute-start(bf16[3,88,1024]{2,1,0:T(8,128)(2,1)} %get-tuple-element.120), channel_id=1, source_target_pairs={{0,4},{4,0},{8,12},{12,8},{1,5},{5,1},{9,13},{13,9},{2,6},{6,2},{1... | collective-permute-start | bytes 1622024 | tf_op jit(solution)/shard_map/ppermute | solution.py:182
  217.3 35.5 %collective-permute-start.18 = (bf16[3,88,1024]{2,1,0:T(8,128)(2,1)}, bf16[3,88,1024]{2,1,0:T(8,128)(2,1)S(1)}, u32[]{:S(2)}, u32[]{:S(2)}) collective-permute-start(bf16[3,88,1024]{2,1,0:T(8,128)(2,1)} %get-tuple-element.123), channel_id=1, source_target_pairs={{0,8},{4,12},{8,0},{12,4},{1,9},{5,13},{9,1},{13,5},{2,10},{6,14},... | collective-permute-start | bytes 1622024 | tf_op jit(solution)/shard_map/ppermute | solution.py:182
  218.8 34.8 %collective-permute-start.19 = (bf16[3,88,1024]{2,1,0:T(8,128)(2,1)}, bf16[3,88,1024]{2,1,0:T(8,128)(2,1)S(1)}, u32[]{:S(2)}, u32[]{:S(2)}) collective-permute-start(bf16[3,88,1024]{2,1,0:T(8,128)(2,1)} %get-tuple-element.124), channel_id=1, source_target_pairs={{0,12},{4,8},{8,4},{12,0},{1,13},{5,9},{9,5},{13,1},{2,14},{6,10},... | collective-permute-start | bytes 1622024 | tf_op jit(solution)/shard_map/ppermute | solution.py:182
  229.3 31.5 %collective-permute-start.16 = (bf16[512,1024]{1,0:T(8,128)(2,1)}, bf16[512,1024]{1,0:T(8,128)(2,1)S(1)}, u32[]{:S(2)}, u32[]{:S(2)}) collective-permute-start(bf16[512,1024]{1,0:T(8,128)(2,1)} %after.33), channel_id=1, source_target_pairs={{0,1},{1,0},{2,3},{3,2},{4,5},{5,4},{6,7},{7,6},{8,9},{9,8},{10,11... | collective-permute-start | bytes 3145736 | tf_op jit(solution)/shard_map/ppermute | solution.py:182
  256.6 40.6 %collective-permute-start.27 = (bf16[3,88,1024]{2,1,0:T(8,128)(2,1)S(1)}, bf16[3,88,1024]{2,1,0:T(8,128)(2,1)S(1)}, u32[]{:S(2)}, u32[]{:S(2)}) collective-permute-start(bf16[3,88,1024]{2,1,0:T(8,128)(2,1)S(1)} %add_convert_fusion.2.refs_1_.rest_0_), channel_id=1, source_target_pairs={{0,2},{1,3},{2,0},{3,1},{4,6},{5,7},{6,4},{7,5},{8,10},{9,11},{10,... | collective-permute-start | bytes 1622024 | tf_op jit(solution)/shard_map/ppermute | solution.py:182
  257.4 38.9 %collective-permute-start.21 = (bf16[392,1024]{1,0:T(8,128)(2,1)}, bf16[392,1024]{1,0:T(8,128)(2,1)}, u32[]{:S(2)}, u32[]{:S(2)}) collective-permute-start(bf16[392,1024]{1,0:T(8,128)(2,1)} %after.37.rest_2_), channel_id=1, source_target_pairs={{0,4},{4,0},{8,12},{12,8},{1,5},{5,1},{9,13},{13,9},{2,6},{6,2},{1... | collective-permute-start | bytes 2408456 | tf_op jit(solution)/shard_map/ppermute | solution.py:182
  259.3 36.9 %collective-permute-start.22 = (bf16[392,1024]{1,0:T(8,128)(2,1)}, bf16[392,1024]{1,0:T(8,128)(2,1)}, u32[]{:S(2)}, u32[]{:S(2)}) collective-permute-start(bf16[392,1024]{1,0:T(8,128)(2,1)} %after.38.rest_3_), channel_id=1, source_target_pairs={{0,8},{4,12},{8,0},{12,4},{1,9},{5,13},{9,1},{13,5},{2,10},{6,14},... | collective-permute-start | bytes 2408456 | tf_op jit(solution)/shard_map/ppermute | solution.py:182
  260.8 35.5 %collective-permute-start.23 = (bf16[392,1024]{1,0:T(8,128)(2,1)}, bf16[392,1024]{1,0:T(8,128)(2,1)S(1)}, u32[]{:S(2)}, u32[]{:S(2)}) collective-permute-start(bf16[392,1024]{1,0:T(8,128)(2,1)} %after.39.rest_4_), channel_id=1, source_target_pairs={{0,12},{4,8},{8,4},{12,0},{1,13},{5,9},{9,5},{13,1},{2,14},{6,10},... | collective-permute-start | bytes 2408456 | tf_op jit(solution)/shard_map/ppermute | solution.py:182
  292.0 21.4 %collective-permute-start.20 = (bf16[512,768]{1,0:T(8,128)(2,1)}, bf16[512,768]{1,0:T(8,128)(2,1)}, u32[]{:S(2)}, u32[]{:S(2)}) collective-permute-start(bf16[512,768]{1,0:T(8,128)(2,1)} %constant_dynamic-slice_fusion), channel_id=1, source_target_pairs={{0,16},{16,0},{1,17},{17,1},{2,18},{18,2},{3,19},{19,3},{4,20},{20... | collective-permute-start | bytes 2359304 | tf_op jit(solution)/shard_map/ppermute | solution.py:182
  299.6 9.2 %collective-permute-start.29 = (bf16[128,1024]{1,0:T(8,128)(2,1)S(1)}, bf16[128,1024]{1,0:T(8,128)(2,1)S(1)}, u32[]{:S(2)}, u32[]{:S(2)}) collective-permute-start(bf16[128,1024]{1,0:T(8,128)(2,1)S(1)} %slice.224.refs_0_), channel_id=1, source_target_pairs={{0,4},{4,0},{8,12},{12,8},{1,5},{5,1},{9,13},{13,9},{2,6},{6,2},{1... | collective-permute-start | bytes 786440 | tf_op jit(solution)/shard_map/ppermute | solution.py:182
  301.7 24.8 %collective-permute-start.33 = (bf16[256,1024]{1,0:T(8,128)(2,1)S(1)}, bf16[256,1024]{1,0:T(8,128)(2,1)}, u32[]{:S(2)}, u32[]{:S(2)}) collective-permute-start(bf16[256,1024]{1,0:T(8,128)(2,1)S(1)} %copy-done.14), channel_id=1, source_target_pairs={{0,4},{4,0},{8,12},{12,8},{1,5},{5,1},{9,13},{13,9},{2,6},{6,2},{1... | collective-permute-start | bytes 1572872 | tf_op jit(solution)/shard_map/ppermute | solution.py:182
  301.8 9.5 %collective-permute-start.31 = (bf16[136,1024]{1,0:T(8,128)(2,1)S(1)}, bf16[136,1024]{1,0:T(8,128)(2,1)S(1)}, u32[]{:S(2)}, u32[]{:S(2)}) collective-permute-start(bf16[136,1024]{1,0:T(8,128)(2,1)S(1)} %slice.225.refs_1_), channel_id=1, source_target_pairs={{0,8},{4,12},{8,0},{12,4},{1,9},{5,13},{9,1},{13,5},{2,10},{6,14},... | collective-permute-start | bytes 835592 | tf_op jit(solution)/shard_map/ppermute | solution.py:182
  305.2 23.5 %collective-permute-start.28 = (bf16[256,1024]{1,0:T(8,128)(2,1)}, bf16[256,1024]{1,0:T(8,128)(2,1)S(1)}, u32[]{:S(2)}, u32[]{:S(2)}) collective-permute-start(bf16[256,1024]{1,0:T(8,128)(2,1)} %get-tuple-element.132), channel_id=1, source_target_pairs={{0,8},{4,12},{8,0},{12,4},{1,9},{5,13},{9,1},{13,5},{2,10},{6,14},... | collective-permute-start | bytes 1572872 | tf_op jit(solution)/shard_map/ppermute | solution.py:182
  308.8 26.3 %collective-permute-start.30 = (bf16[256,1024]{1,0:T(8,128)(2,1)S(1)}, bf16[256,1024]{1,0:T(8,128)(2,1)S(1)}, u32[]{:S(2)}, u32[]{:S(2)}) collective-permute-start(bf16[256,1024]{1,0:T(8,128)(2,1)S(1)} %pad_maximum_fusion.9), channel_id=1, source_target_pairs={{0,8},{4,12},{8,0},{12,4},{1,9},{5,13},{9,1},{13,5},{2,10},{6,14},... | collective-permute-start | bytes 1572872 | tf_op jit(solution)/shard_map/ppermute | solution.py:182
  311.4 23.7 %collective-permute-start.32 = (bf16[272,1024]{1,0:T(8,128)(2,1)S(1)}, bf16[272,1024]{1,0:T(8,128)(2,1)S(1)}, u32[]{:S(2)}, u32[]{:S(2)}) collective-permute-start(bf16[272,1024]{1,0:T(8,128)(2,1)S(1)} %pad_maximum_fusion.8), channel_id=1, source_target_pairs={{0,4},{4,0},{8,12},{12,8},{1,5},{5,1},{9,13},{13,9},{2,6},{6,2},{1... | collective-permute-start | bytes 1671176 | tf_op jit(solution)/shard_map/ppermute | solution.py:182
  317.1 25.2 %collective-permute-start.24 = (bf16[128,1024]{1,0:T(8,128)(2,1)}, bf16[128,1024]{1,0:T(8,128)(2,1)S(1)}, u32[]{:S(2)}, u32[]{:S(2)}) collective-permute-start(bf16[128,1024]{1,0:T(8,128)(2,1)} %get-tuple-element.164), channel_id=1, source_target_pairs={{0,1},{1,0},{2,3},{3,2},{4,5},{5,4},{6,7},{7,6},{8,9},{9,8},{10,11... | collective-permute-start | bytes 786440 | tf_op jit(solution)/shard_map/ppermute | solution.py:182
  326.5 18.9 %collective-permute-start.25 = (bf16[128,1024]{1,0:T(8,128)(2,1)}, bf16[128,1024]{1,0:T(8,128)(2,1)S(1)}, u32[]{:S(2)}, u32[]{:S(2)}) collective-permute-start(bf16[128,1024]{1,0:T(8,128)(2,1)} %get-tuple-element.165), channel_id=1, source_target_pairs={{0,2},{1,3},{2,0},{3,1},{4,6},{5,7},{6,4},{7,5},{8,10},{9,11},{10,... | collective-permute-start | bytes 786440 | tf_op jit(solution)/shard_map/ppermute | solution.py:182
  328.7 16.6 %collective-permute-start.26 = (bf16[128,1024]{1,0:T(8,128)(2,1)S(1)}, bf16[128,1024]{1,0:T(8,128)(2,1)S(1)}, u32[]{:S(2)}, u32[]{:S(2)}) collective-permute-start(bf16[128,1024]{1,0:T(8,128)(2,1)S(1)} %get-tuple-element.166), channel_id=1, source_target_pairs={{0,3},{1,2},{2,1},{3,0},{4,7},{5,6},{6,5},{7,4},{8,11},{9,10},{10,... | collective-permute-start | bytes 786440 | tf_op jit(solution)/shard_map/ppermute | solution.py:182
  336.7 41.5 %collective-permute-start.35 = (bf16[512,1024]{1,0:T(8,128)(2,1)}, bf16[512,1024]{1,0:T(8,128)(2,1)}, u32[]{:S(2)}, u32[]{:S(2)}) collective-permute-start(bf16[512,1024]{1,0:T(8,128)(2,1)} %after.44.refs_2_), channel_id=1, source_target_pairs={{0,8},{4,12},{8,0},{12,4},{1,9},{5,13},{9,1},{13,5},{2,10},{6,14},... | collective-permute-start | bytes 3145736 | tf_op jit(solution)/shard_map/ppermute | solution.py:182
  338.2 40.1 %collective-permute-start.34 = (bf16[512,1024]{1,0:T(8,128)(2,1)}, bf16[512,1024]{1,0:T(8,128)(2,1)}, u32[]{:S(2)}, u32[]{:S(2)}) collective-permute-start(bf16[512,1024]{1,0:T(8,128)(2,1)} %after.43.refs_1_), channel_id=1, source_target_pairs={{0,4},{4,0},{8,12},{12,8},{1,5},{5,1},{9,13},{13,9},{2,6},{6,2},{1... | collective-permute-start | bytes 3145736 | tf_op jit(solution)/shard_map/ppermute | solution.py:182
  346.3 38.2 %collective-permute-start.42 = (bf16[3,352,1024]{2,1,0:T(8,128)(2,1)}, bf16[3,352,1024]{2,1,0:T(8,128)(2,1)}, u32[]{:S(2)}, u32[]{:S(2)}) collective-permute-start(bf16[3,352,1024]{2,1,0:T(8,128)(2,1)} %after.48), channel_id=1, source_target_pairs={{0,16},{16,0},{1,17},{17,1},{2,18},{18,2},{3,19},{19,3},{4,20},{20... | collective-permute-start | bytes 6488072 | tf_op jit(solution)/shard_map/ppermute | solution.py:182
  347.2 11.0 %collective-permute-start.36 = (bf16[128,1024]{1,0:T(8,128)(2,1)S(1)}, bf16[128,1024]{1,0:T(8,128)(2,1)S(1)}, u32[]{:S(2)}, u32[]{:S(2)}) collective-permute-start(bf16[128,1024]{1,0:T(8,128)(2,1)S(1)} %copy-done.5), channel_id=1, source_target_pairs={{0,1},{1,0},{2,3},{3,2},{4,5},{5,4},{6,7},{7,6},{8,9},{9,8},{10,11... | collective-permute-start | bytes 786440 | tf_op jit(solution)/shard_map/ppermute | solution.py:182
  358.9 3.9 collective-permute-start.37
  363.6 4.6 %collective-permute-start.38 = (f32[3,1024]{1,0:T(4,128)S(1)}, f32[3,1024]{1,0:T(4,128)S(1)}, u32[]{:S(2)}, u32[]{:S(2)}) collective-permute-start(f32[3,1024]{1,0:T(4,128)S(1)} %add.235), channel_id=1, source_target_pairs={{0,2},{1,3},{2,0},{3,1},{4,6},{5,7},{6,4},{7,5},{8,10},{9,11},{10,... | collective-permute-start | bytes 36872 | tf_op jit(solution)/shard_map/ppermute | solution.py:182
  368.2 1.2 collective-permute-start.39
  369.4 4.5 %collective-permute-start.40 = (f32[3,1024]{1,0:T(4,128)S(1)}, f32[3,1024]{1,0:T(4,128)S(1)}, u32[]{:S(2)}, u32[]{:S(2)}) collective-permute-start(f32[3,1024]{1,0:T(4,128)S(1)} %add.237), channel_id=1, source_target_pairs={{0,4},{4,0},{8,12},{12,8},{1,5},{5,1},{9,13},{13,9},{2,6},{6,2},{1... | collective-permute-start | bytes 36872 | tf_op jit(solution)/shard_map/ppermute | solution.py:182
  373.9 3.8 collective-permute-start.41
  375.4 25.6 %collective-permute-start.43 = (bf16[256,1024]{1,0:T(8,128)(2,1)S(1)}, bf16[256,1024]{1,0:T(8,128)(2,1)S(1)}, u32[]{:S(2)}, u32[]{:S(2)}) collective-permute-start(bf16[256,1024]{1,0:T(8,128)(2,1)S(1)} %pad_maximum_fusion.10), channel_id=1, source_target_pairs={{0,2},{1,3},{2,0},{3,1},{4,6},{5,7},{6,4},{7,5},{8,10},{9,11},{10,... | collective-permute-start | bytes 1572872 | tf_op jit(solution)/shard_map/ppermute | solution.py:182
  401.1 2.7 collective-permute-start.44
  (53 other events, 257.7 us)
where the time goes:
time: 416 us; the launch traced here: 409 us
  Pallas kernels  184 us (44%)
  starting transfers between devices  65.8 us (16%)
  waiting for transfers between devices  61.5 us (15%)
  other arithmetic  49 us (12%)
  local copies, waits for them, and re-layouts  32.5 us (8%)
  matrix products  14.2 us (3%)
    ppermute x45, starting transfers between devices, swap(): lax.ppermute(x, axis, [(i, i ^ mask) for i in range(lax.axis_size(axis))])  54.4 us
    ppermute x45, waiting for transfers between devices, swap(): lax.ppermute(x, axis, [(i, i ^ mask) for i in range(lax.axis_size(axis))])  51.7 us
    pallas_call x2, Pallas kernels, attend_backward(): pl.pallas_call(functools.partial(backward_kernel, block), grid_spec=spec,...  44.3 us
    pallas_call x2, Pallas kernels, feed(): pl.pallas_call(feed_kernel, grid=(4,), in_specs=[spec_whole(x), spec_whol...  32.8 us
    pallas_call x2, Pallas kernels, attend_forward2(): pl.pallas_call(functools.partial(fwd2_kernel, block), grid_spec=spec, out...  23.9 us
    unnamed x111, local copies, waits for them, and re-layouts  19.6 us
    pallas_call x1, Pallas kernels, others(): pl.pallas_call(others_kernel, grid_spec=spec, out_shape=[half, half] + [j...  18.9 us
    pallas_call x2, Pallas kernels, project(): pl.pallas_call(functools.partial(project_kernel, counts), grid_spec=spec,...  18.1 us
  transfers between devices with their start and end apart: 48, of which 16 were waited for; matrix products, arithmetic and copies ran while one was open for 18% of the time, Pallas kernels for 40%

commit v1 on v0

--- a/solution.py
+++ b/solution.py
@@ -241,8 +241,12 @@
 
 def sum_over_all(x):
     for axis in ("mlp", "dp", "head"):
+        count = lax.axis_size(axis)
+        if count == 4:
+            x = (x + swap(x, axis, 1)) + (swap(x, axis, 2) + swap(x, axis, 3))
+            continue
         mask = 1
-        while mask < lax.axis_size(axis):
+        while mask < count:
             x = x + swap(x, axis, mask)
             mask *= 2
     return x
@@ -903,30 +907,29 @@
     far_half_got = after(far_half_got, mixed_grad)
     far_chip = shard_grads(scalars, ranks, True, *tokens_two, [far_half_got])
     far_got = [swap(f, "head", e) for e, f in enumerate(far_chip) if e]
-    own_half_got = after(own_half_got, far_chip[0])
-    own_chip = shard_grads(scalars, ranks, False, *tokens_two, [own_half_got, out_own, out_got])
-    mixed_grad_rows = after(mixed_grad_rows, own_chip[0])
-
-    down_back = swap(after(down_near, mixed_grad_rows), "mlp", 1)
+    mixed_grad_rows = after(mixed_grad_rows, far_chip[0])
+
     back_args = (queries, keys, values, mixed_grad_rows, start, cosine, sine, block)
     grads = attend_backward(*back_args, 0, mixed[0], log_total[0])
-    far_got = [after(f, grads[0]) for f in far_got]
+    own_half_got = after(own_half_got, grads[0])
+    own_chip = shard_grads(scalars, ranks, False, *tokens_two, [own_half_got, out_own, out_got])
+    far_got = [after(f, own_chip[0]) for f in far_got]
     far_sum = add_low(far_chip[0], *far_got)
     far_here = swap(far_sum, "mlp", 2)
     own_chip = [own_chip[0]] + [after(f, far_sum) for f in own_chip[1:]]
     own_got = [swap(f, "head", e) for e, f in enumerate(own_chip) if e]
+    down_back = swap(after(down_near, own_chip[0]), "mlp", 1)
     for g in range(1, width // lanes):
         grads = attend_backward(
-            *back_args, g, mixed[g], log_total[g], grads, (far_sum, down_back, *own_chip[1:])
+            *back_args, g, mixed[g], log_total[g], grads, (far_sum, *own_chip[1:])
         )
     proj_grad, first_values_grad = grads
     cut = cut_of(chunk)
     half_proj = model // 2
     proj_wgrad = dot(gathered, proj_grad, TN).astype(bf16)
-    proj_got = swap(block_of(proj_wgrad, 1 - core, half_proj), "dp", 1)
     if ranks == 4:
         (low, high), gain_last = unproject(
-            rank, row_parts[3:], 3, ((cut, chunk - cut),), w_project, proj_grad, (proj_wgrad,)
+            rank, row_parts[3:], 3, ((cut, chunk - cut),), w_project, proj_grad, (proj_wgrad, down_back)
         )
         for_two, for_one = swap(low, "head", 1), swap(high, "head", 2)
         own_got = [after(f, low) for f in own_got]
@@ -935,6 +938,7 @@
     own_all = (own_chip[0], *own_got)
     piece_sum = add_low(*(f[: 3 * rows] for f in own_all), far_here.reshape(3 * rows, model))
     out_sum = add_low(*(f[3 * rows :] for f in own_all))
+    proj_got = swap(after(block_of(proj_wgrad, 1 - core, half_proj), own_got[-1]), "dp", 1)
     proj_mine = add_low(block_of(proj_wgrad, core, half_proj), proj_got)
     both_mine = jnp.concatenate([proj_mine, out_sum.reshape(half_proj, -1)], axis=1)
     line, count = lax.axis_index("mlp"), lax.axis_size("mlp")
@@ -946,10 +950,6 @@
     if ranks == 4:
         cut_p = cut_of(3 * rows)
         cut_q = 3 * rows - cut_p
-        low_p, high_p = piece_sum[:cut_p], piece_sum[cut_p:]
-        low_x, high_y = swap(low_p, "head", 1), swap(high_p, "head", 2)
-        low_yy = swap(jnp.concatenate([low_p, low_x]), "head", 2)
-        high_xx = swap(jnp.concatenate([high_p, high_y]), "head", 1)
         (own, one, two), gain_rest = unproject(
             rank,
             row_parts[:3],
@@ -957,11 +957,16 @@
             ((chunk,),) * 3,
             w_project,
             proj_grad,
-            (piece_sum, both_mine),
+            (both_mine,),
         )
         attn_gain_grad = gain_last + gain_rest
-        one = after(one.at[cut:].set(add_low(one[cut:], for_one)), low_yy, high_xx)
-        two = after(two.at[:cut].set(add_low(two[:cut], for_two)), low_yy, high_xx)
+        piece_sum = after(piece_sum, own)
+        low_p, high_p = piece_sum[:cut_p], piece_sum[cut_p:]
+        low_x, high_y = swap(low_p, "head", 1), swap(high_p, "head", 2)
+        low_yy = swap(jnp.concatenate([low_p, low_x]), "head", 2)
+        high_xx = swap(jnp.concatenate([high_p, high_y]), "head", 1)
+        one = one.at[cut:].set(add_low(one[cut:], for_one))
+        two = two.at[:cut].set(add_low(two[:cut], for_two))
         one_got, two_got = swap(one, "head", 1), swap(two, "head", 2)
         half_sum = regroup(
             rank,
@@ -973,7 +978,7 @@
             ],
             rows,
         )
-        line_piece = after(line_sum(both_mine), one, two, half_sum)
+        line_piece = after(line_sum(both_mine), one, two)
         attn_normed_grad = own.astype(f32) + one_got.astype(f32) + two_got.astype(f32)
         ended = (one_got, two_got)
     else:

time: 416 us -> 412 us (level)
    ppermute x45 -> x47, waiting for transfers between devices: 51.7 us -> 48.2 us  [swap(): lax.ppermute(x, axis, [(i, i ^ mask) for i in range(lax.axis_size(axis))])]
    ppermute x45 -> x47, starting transfers between devices: 54.4 us -> 52.4 us  [swap(): lax.ppermute(x, axis, [(i, i ^ mask) for i in range(lax.axis_size(axis))])]
    unnamed x111 -> x123, local copies, waits for them, and re-layouts: 19.6 us -> 20.2 us
  transfers between devices with their start and end apart: 48 -> 50, of which waited for: 16 -> 14; matrix products, arithmetic and copies ran while one was open for 18% -> 18% of each run, Pallas kernels for 40% -> 41%
where the time goes in v1:
time: 412 us; the launch traced here: 405 us
  Pallas kernels  185 us (45%)
  starting transfers between devices  63.4 us (15%)
  waiting for transfers between devices  57.9 us (14%)
  other arithmetic  47.8 us (12%)
  local copies, waits for them, and re-layouts  35.2 us (9%)
  matrix products  14.2 us (3%)
    ppermute x47, starting transfers between devices, swap(): lax.ppermute(x, axis, [(i, i ^ mask) for i in range(lax.axis_size(axis))])  52.4 us
    ppermute x47, waiting for transfers between devices, swap(): lax.ppermute(x, axis, [(i, i ^ mask) for i in range(lax.axis_size(axis))])  48.2 us
    pallas_call x2, Pallas kernels, attend_backward(): pl.pallas_call(functools.partial(backward_kernel, block), grid_spec=spec,...  44 us
    pallas_call x2, Pallas kernels, feed(): pl.pallas_call(feed_kernel, grid=(4,), in_specs=[spec_whole(x), spec_whol...  32.8 us
    pallas_call x2, Pallas kernels, attend_forward2(): pl.pallas_call(functools.partial(fwd2_kernel, block), grid_spec=spec, out...  24.1 us
    unnamed x123, local copies, waits for them, and re-layouts  20.2 us
    pallas_call x1, Pallas kernels, others(): pl.pallas_call(others_kernel, grid_spec=spec, out_shape=[half, half] + [j...  19.1 us
    pallas_call x2, Pallas kernels, project(): pl.pallas_call(functools.partial(project_kernel, counts), grid_spec=spec,...  18.1 us
  transfers between devices with their start and end apart: 50, of which 14 were waited for; matrix products, arithmetic and copies ran while one was open for 18% of the time, Pallas kernels for 41%

profile of v1, /device:TPU:0, one launch (start us, length us, event | category | flops | bytes accessed | tf_op | source)
XLA Modules:
  0.0 405.0 jit_solution(18319440178327366242)
XLA Ops:
  0.7 3.0 collective-permute-start
  5.2 2.6 pad_maximum_fusion.refs_0_.refs_1_.refs_2_
  7.9 2.1 copy-done.13
  10.0 2.7 collective-permute-start.4
  19.1 5.5 %fusion.9 = (f32[2048,128]{1,0:T(8,128)}, f32[2048,128]{1,0:T(8,128)}) fusion(f32[128]{0:T(128)S(1)} %get-tuple-element.175, f32[128]{0:T(128)S(1)} %get-tuple-element.176, f32[2048]{0:T(1024)S(1)} %bitcast.90), kind=kLoop, calls=%fused_computation.45 | loop fusion | flops 524288 | bytes 2106368 | tf_op jit(solution)/shard_map/mul | solution.py:843
  24.6 2.6 collective-permute-done.refs_2_
  32.7 13.4 %project.2 = (bf16[2048,1024]{1,0:T(8,128)(2,1)}, bf16[2048,256]{1,0:T(8,128)(2,1)}, bf16[2048,256]{1,0:T(8,128)(2,1)}, bf16[2048,256]{1,0:T(8,128)(2,1)}, f32[8,128]{1,0:T(8,128)}) custom-call(s32[1]{0:T(128)} %bitcast.2.rank_ref, bf16[512,1024]{1,0:T(8,128)(2,1)} %bitcast.77, bf16[512,1024]{1,0:T(8,128)(2,1)} %collective-permute-done.2.refs_1_, ...), custom_call_target="tpu_custom_call" | custom-call | flops 14849999872 | bytes 1350000 | tf_op jit(solution)/shard_map/project/pallas_call | solution.py:363
  49.2 2.7 collective-permute-start.7
  51.9 4.7 %project.3 = (bf16[2048,1024]{1,0:T(8,128)(2,1)}, bf16[2048,256]{1,0:T(8,128)(2,1)}, bf16[2048,256]{1,0:T(8,128)(2,1)}, bf16[2048,256]{1,0:T(8,128)(2,1)}, f32[8,128]{1,0:T(8,128)}) custom-call(s32[1]{0:T(128)} %bitcast.2.rank_ref, bf16[256,1024]{1,0:T(8,128)(2,1)} %copy-done.42, ...), custom_call_target="tpu_custom_call", output_to_operand_aliasing={{0}: (8, {}), {1}: (9, {}), {2}: (10, {}), {3}: (11, {})} | custom-call | flops 4950000128 | bytes 450000 | tf_op jit(solution)/shard_map/project/pallas_call | solution.py:363
  56.6 12.3 %attend_forward.2 = (bf16[2048,128]{1,0:T(8,128)(2,1)}, f32[1,8,2048]{2,1,0:T(8,128)}) custom-call(s32[2]{0:T(128)} %slice.174.firsts, s32[2]{0:T(128)} %slice.175.lasts, bf16[2048,256]{1,0:T(8,128)(2,1)} %get-tuple-element.100.q_ref, bf16[2048,256]{1,0:T(8,128)(2,1)} %get-tuple-element.101.k_ref, bf16[2048,256]{1,0:T(8,128)(2,1)} %get-tuple-element.102.v_ref, ...), custom_call_target="tpu_custom_call" | custom-call | flops 15569256448 | bytes 2097152 | tf_op jit(solution)/shard_map/attend_forward/pallas_call | solution.py:89
  68.9 3.6 all-to-all-start
  72.6 11.8 %attend_forward.3 = (bf16[2048,128]{1,0:T(8,128)(2,1)}, f32[1,8,2048]{2,1,0:T(8,128)}) custom-call(s32[2]{0:T(128)} %slice.174.firsts, s32[2]{0:T(128)} %slice.175.lasts, bf16[2048,256]{1,0:T(8,128)(2,1)} %get-tuple-element.100.q_ref, bf16[2048,256]{1,0:T(8,128)(2,1)} %get-tuple-element.101.k_ref, bf16[2048,256]{1,0:T(8,128)(2,1)} %get-tuple-element.102.v_ref, ...), custom_call_target="tpu_custom_call" | custom-call | flops 15569256448 | bytes 2097152 | tf_op jit(solution)/shard_map/attend_forward/pallas_call | solution.py:89
  84.4 5.3 %all-to-all-done.refs_4_ = bf16[4,512,128]{2,1,0:T(8,128)(2,1)S(1)} async-done(((bf16[4,512,128]{2,1,0:T(8,128)(2,1)}), bf16[4,512,128]{2,1,0:T(8,128)(2,1)S(1)}, u32[]{:S(2)}, u32[]{:S(2)}) %all-to-all-start) | async-done | bytes 524320 | tf_op jit(solution)/shard_map/all_to_all | solution.py:860
  91.0 4.0 assemble.1
  97.8 3.7 all-to-all-start.1
  103.2 2.0 fusion.26
  105.3 4.3 %all-to-all-done.1 = bf16[4,512,128]{2,1,0:T(8,128)(2,1)S(1)} async-done(((bf16[4,512,128]{2,1,0:T(8,128)(2,1)}), bf16[4,512,128]{2,1,0:T(8,128)(2,1)S(1)}, u32[]{:S(2)}, u32[]{:S(2)}) %all-to-all-start.1) | async-done | bytes 524320 | tf_op jit(solution)/shard_map/all_to_all | solution.py:860
  109.6 2.7 multiply_reduce_fusion
  113.8 16.4 %feed.2 = (bf16[4,3,352,512]{3,2,1,0:T(8,128)(2,1)}, f32[512,1024]{1,0:T(8,128)}) custom-call(bf16[512,1024]{1,0:T(8,128)(2,1)} %copy-done.35, bf16[512,1024]{1,0:T(8,128)(2,1)} %bitcast.17.g_ref.grad_ref.refs_4_, bf16[2112,1024]{1,0:T(8,128)(2,1)} %copy-done.13, bf16[2112,1024]{1,0:T(8,128)(2,1)} %copy-done.13, bf16[2112,1024]{1,0:T(8,128)(2,1)} %copy-done.13, ...), custom_call_target="tpu_custom_call" | custom-call | flops 17600000000 | bytes 1600000 | tf_op jit(solution)/shard_map/feed/pallas_call | solution.py:449
  130.3 13.0 %collective-permute-done.10.x_ref.xn_ref.refs_3_ = bf16[512,1024]{1,0:T(8,128)(2,1)S(1)} collective-permute-done((bf16[512,1024]{1,0:T(8,128)(2,1)S(1)}, bf16[512,1024]{1,0:T(8,128)(2,1)S(1)}, u32[]{:S(2)}, u32[]{:S(2)}) %collective-permute-start.10) | collective-permute-done | bytes 1048608 | tf_op jit(solution)/shard_map/ppermute | solution.py:182
  144.2 16.4 %feed.3 = (bf16[4,3,352,512]{3,2,1,0:T(8,128)(2,1)}, bf16[512,1024]{1,0:T(8,128)(2,1)}) custom-call(bf16[512,1024]{1,0:T(8,128)(2,1)} %copy-done.56, bf16[512,1024]{1,0:T(8,128)(2,1)} %collective-permute-done.11.g_ref.gn_ref.refs_5_, bf16[2112,1024]{1,0:T(8,128)(2,1)} %copy-done.13, bf16[2112,1024]{1,0:T(8,128)(2,1)} %copy-done.13, ...), custom_call_target="tpu_custom_call" | custom-call | flops 17600000000 | bytes 1600000 | tf_op jit(solution)/shard_map/feed/pallas_call | solution.py:449
  162.2 19.1 %others.1 = (bf16[1056,1024]{1,0:T(8,128)(2,1)}, bf16[1056,1024]{1,0:T(8,128)(2,1)}, f32[512,1024]{1,0:T(8,128)}, bf16[512,1024]{1,0:T(8,128)(2,1)}) custom-call(s32[2]{0:T(128)} %pad_add_fusion.scalars, bf16[4,3,352,512]{3,2,1,0:T(8,128)(2,1)} %get-tuple-element.107.act_ref.refs_0_, bf16[4,3,352,512]{3,2,1,0:T(8,128)(2,1)} %get-tuple-element.109.near_ref.refs_1_, ...), custom_call_target="tpu_custom_call" | custom-call | flops 20899999744 | bytes 1900000 | tf_op jit(solution)/shard_map/others/pallas_call | solution.py:631
  181.4 3.8 collective-permute-done.12.refs_0_
  187.8 8.2 %state_back.1 = (f32[512,1024]{1,0:T(8,128)}, bf16[512,1024]{1,0:T(8,128)(2,1)}, bf16[4,512,256]{2,1,0:T(8,128)(2,1)}, f32[1,1024]{1,0:T(1,128)}) custom-call(bf16[512,1024]{1,0:T(8,128)(2,1)} %after.26.refs_1_.back_ref, f32[512,1024]{1,0:T(8,128)} %get-tuple-element.108.refs_9_.terms_ref, f32[512,1024]{1,0:T(8,128)} %copy-done.3, ...), custom_call_target="tpu_custom_call" | custom-call | flops 6600000000 | bytes 600000 | tf_op jit(solution)/shard_map/state_back/pallas_call | solution.py:767
  195.9 3.7 all-to-all-start.2
  199.7 2.0 convolution_convert_fusion.2
  204.9 7.9 %far_sum.1 = (bf16[3,88,1024]{2,1,0:T(8,128)(2,1)}, bf16[3,88,1024]{2,1,0:T(8,128)(2,1)}, bf16[3,88,1024]{2,1,0:T(8,128)(2,1)}, bf16[3,88,1024]{2,1,0:T(8,128)(2,1)}) custom-call(s32[2]{0:T(128)} %pad_add_fusion.scalars, bf16[4,3,352,512]{3,2,1,0:T(8,128)(2,1)} %get-tuple-element.107.act_ref.refs_0_, ...), custom_call_target="tpu_custom_call" | custom-call | flops 8800000000 | bytes 800000 | tf_op jit(solution)/shard_map/far_sum/pallas_call | solution.py:565
  217.2 21.8 %attend_backward.2 = (bf16[2048,768]{1,0:T(8,128)(2,1)}, bf16[2048,256]{1,0:T(8,128)(2,1)}) custom-call(s32[4]{0:T(128)} %get-tuple-element.172.full_end, s32[4]{0:T(128)} %get-tuple-element.171.some_end, bf16[2048,256]{1,0:T(8,128)(2,1)} %get-tuple-element.100.q_ref, bf16[2048,256]{1,0:T(8,128)(2,1)} %get-tuple-element.101.k_ref, ...), custom_call_target="tpu_custom_call" | custom-call | flops 27917287424 | bytes 5767168 | tf_op jit(solution)/shard_map/attend_backward/pallas_call | solution.py:168
  239.1 9.5 %own_sum.1 = (bf16[392,1024]{1,0:T(8,128)(2,1)}, bf16[392,1024]{1,0:T(8,128)(2,1)}, bf16[392,1024]{1,0:T(8,128)(2,1)}, bf16[392,1024]{1,0:T(8,128)(2,1)}) custom-call(s32[2]{0:T(128)} %pad_add_fusion.scalars, bf16[4,3,352,512]{3,2,1,0:T(8,128)(2,1)} %get-tuple-element.107.act_ref.refs_0_, bf16[4,3,352,512]{3,2,1,0:T(8,128)(2,1)} %get-tuple-element.109.near_ref.refs_1_, ...), custom_call_target="tpu_custom_call" | custom-call | flops 8800000000 | bytes 800000 | tf_op jit(solution)/shard_map/own_sum/pallas_call | solution.py:565
  258.4 22.1 %attend_backward.3 = (bf16[2048,768]{1,0:T(8,128)(2,1)}, bf16[2048,256]{1,0:T(8,128)(2,1)}) custom-call(s32[4]{0:T(128)} %get-tuple-element.172.full_end, s32[4]{0:T(128)} %get-tuple-element.171.some_end, bf16[2048,256]{1,0:T(8,128)(2,1)} %get-tuple-element.100.q_ref, ...), custom_call_target="tpu_custom_call", output_to_operand_aliasing={{0}: (15, {}), {1}: (16, {})} | custom-call | flops 27917287424 | bytes 5767168 | tf_op jit(solution)/shard_map/attend_backward/pallas_call | solution.py:168
  280.6 6.7 %convolution_convert_fusion.refs_4_ = bf16[1024,768]{1,0:T(8,128)(2,1)S(1)} fusion(bf16[2048,1024]{1,0:T(8,128)(2,1)} %get-tuple-element.120, bf16[2048,768]{1,0:T(8,128)(2,1)} %get-tuple-element.129.refs_3_.refs_4_), kind=kOutput, calls=%fused_computation.31 | convolution fusion | flops 3222011904 | bytes 8912896 | tf_op jit(solution)/shard_map/dot_general | solution.py:18
  289.7 3.9 unproject.2
  301.2 2.7 fusion.8.refs_0_
  306.3 9.6 %unproject.3 = (bf16[512,1024]{1,0:T(8,128)(2,1)}, bf16[512,1024]{1,0:T(8,128)(2,1)}, bf16[512,1024]{1,0:T(8,128)(2,1)}, f32[1,1024]{1,0:T(1,128)}) custom-call(s32[1]{0:T(128)} %bitcast.2.rank_ref, bf16[512,1024]{1,0:T(8,128)(2,1)} %bitcast.78, bf16[512,1024]{1,0:T(8,128)(2,1)} %collective-permute-done.2.refs_1_, ...), custom_call_target="tpu_custom_call" | custom-call | flops 11550000128 | bytes 1050000 | tf_op jit(solution)/shard_map/unproject/pallas_call | solution.py:732
  320.8 2.2 fusion.13.refs_2_
  323.0 2.2 collective-permute-done.40.refs_2_
  331.2 9.6 %collective-permute-done.25 = bf16[128,1024]{1,0:T(8,128)(2,1)S(1)} collective-permute-done((bf16[128,1024]{1,0:T(8,128)(2,1)S(1)}, bf16[128,1024]{1,0:T(8,128)(2,1)S(1)}, u32[]{:S(2)}, u32[]{:S(2)}) %collective-permute-start.25) | collective-permute-done | bytes 262176 | tf_op jit(solution)/shard_map/ppermute | solution.py:182
  341.7 4.1 %collective-permute-start.31 = (bf16[128,1024]{1,0:T(8,128)(2,1)}, bf16[128,1024]{1,0:T(8,128)(2,1)S(1)}, u32[]{:S(2)}, u32[]{:S(2)}) collective-permute-start(bf16[128,1024]{1,0:T(8,128)(2,1)} %after.44.refs_1_.refs_0_), channel_id=1, source_target_pairs={{0,1},{1,0},{2,3},{3,2},{4,5},{5,4},{6,7},{7,6},{8,9},{9,8},{10,11... | collective-permute-start | bytes 786440 | tf_op jit(solution)/shard_map/ppermute | solution.py:182
  353.1 2.5 collective-permute-start.34
  355.6 3.4 regroup.1
  359.9 3.5 collective-permute-done.35
  364.5 3.6 add_convert_fusion.refs_1_
  372.6 2.6 collective-permute-done.38
  375.8 2.5 fusion
  378.4 3.7 fusion.6.refs_2_
  382.1 2.2 broadcast_select_fusion.1
  385.4 3.7 slice_bitcast_fusion
  390.2 6.4 %collective-permute-done.45 = bf16[256,1024]{1,0:T(8,128)(2,1)S(1)} collective-permute-done((bf16[256,1024]{1,0:T(8,128)(2,1)S(1)}, bf16[256,1024]{1,0:T(8,128)(2,1)S(1)}, u32[]{:S(2)}, u32[]{:S(2)}) %collective-permute-start.45) | collective-permute-done | bytes 524320 | tf_op jit(solution)/shard_map/ppermute | solution.py:182
  (296 shorter events, 94.9 us)
Async XLA Ops:
  0.7 26.5 %collective-permute-start = (bf16[512,1024]{1,0:T(8,128)(2,1)}, bf16[512,1024]{1,0:T(8,128)(2,1)}, u32[]{:S(2)}, u32[]{:S(2)}) collective-permute-start(bf16[512,1024]{1,0:T(8,128)(2,1)} %bitcast.75), channel_id=1, source_target_pairs={{0,8},{4,12},{8,0},{12,4},{1,9},{5,13},{9,1},{13,5},{2,10},{6,14},... | collective-permute-start | bytes 3145736 | tf_op jit(solution)/shard_map/ppermute | solution.py:182
  3.7 26.3 %collective-permute-start.2 = (bf16[512,1024]{1,0:T(8,128)(2,1)}, bf16[512,1024]{1,0:T(8,128)(2,1)}, u32[]{:S(2)}, u32[]{:S(2)}) collective-permute-start(bf16[512,1024]{1,0:T(8,128)(2,1)} %bitcast.76), channel_id=1, source_target_pairs={{0,4},{4,0},{8,12},{12,8},{1,5},{5,1},{9,13},{13,9},{2,6},{6,2},{1... | collective-permute-start | bytes 3145736 | tf_op jit(solution)/shard_map/ppermute | solution.py:182
  10.0 36.1 %collective-permute-start.4 = (bf16[3,88,1024]{2,1,0:T(8,128)(2,1)S(1)}, bf16[3,88,1024]{2,1,0:T(8,128)(2,1)S(1)}, u32[]{:S(2)}, u32[]{:S(2)}) collective-permute-start(bf16[3,88,1024]{2,1,0:T(8,128)(2,1)S(1)} %dynamic-slice_bitcast_fusion.2), channel_id=1, source_target_pairs={{0,2},{1,3},{2,0},{3,1},{4,6},{5,7},{6,4},{7,5},{8,10},{9,11},{10,... | collective-permute-start | bytes 1622024 | tf_op jit(solution)/shard_map/ppermute | solution.py:182
  28.3 17.8 %collective-permute-start.1 = (bf16[256,1024]{1,0:T(8,128)(2,1)S(1)}, bf16[256,1024]{1,0:T(8,128)(2,1)S(1)}, u32[]{:S(2)}, u32[]{:S(2)}) collective-permute-start(bf16[256,1024]{1,0:T(8,128)(2,1)S(1)} %slice.216), channel_id=1, source_target_pairs={{0,4},{4,0},{8,12},{12,8},{1,5},{5,1},{9,13},{13,9},{2,6},{6,2},{1... | collective-permute-start | bytes 1572872 | tf_op jit(solution)/shard_map/ppermute | solution.py:182
  31.1 15.0 %collective-permute-start.3 = (bf16[256,1024]{1,0:T(8,128)(2,1)S(1)}, bf16[256,1024]{1,0:T(8,128)(2,1)S(1)}, u32[]{:S(2)}, u32[]{:S(2)}) collective-permute-start(bf16[256,1024]{1,0:T(8,128)(2,1)S(1)} %slice.217), channel_id=1, source_target_pairs={{0,8},{4,12},{8,0},{12,4},{1,9},{5,13},{9,1},{13,5},{2,10},{6,14},... | collective-permute-start | bytes 1572872 | tf_op jit(solution)/shard_map/ppermute | solution.py:182
  48.3 41.3 %collective-permute-start.5 = (bf16[392,1024]{1,0:T(8,128)(2,1)S(1)}, bf16[392,1024]{1,0:T(8,128)(2,1)S(1)}, u32[]{:S(2)}, u32[]{:S(2)}) collective-permute-start(bf16[392,1024]{1,0:T(8,128)(2,1)S(1)} %pad_maximum_fusion.7.refs_0_), channel_id=1, source_target_pairs={{0,4},{4,0},{8,12},{12,8},{1,5},{5,1},{9,13},{13,9},{2,6},{6,2},{1... | collective-permute-start | bytes 2408456 | tf_op jit(solution)/shard_map/ppermute | solution.py:182
  48.9 40.8 %collective-permute-start.6 = (bf16[392,1024]{1,0:T(8,128)(2,1)S(1)}, bf16[392,1024]{1,0:T(8,128)(2,1)S(1)}, u32[]{:S(2)}, u32[]{:S(2)}) collective-permute-start(bf16[392,1024]{1,0:T(8,128)(2,1)S(1)} %pad_maximum_fusion.7.refs_0_), channel_id=1, source_target_pairs={{0,8},{4,12},{8,0},{12,4},{1,9},{5,13},{9,1},{13,5},{2,10},{6,14},... | collective-permute-start | bytes 2408456 | tf_op jit(solution)/shard_map/ppermute | solution.py:182
  49.2 40.5 %collective-permute-start.7 = (bf16[392,1024]{1,0:T(8,128)(2,1)S(1)}, bf16[392,1024]{1,0:T(8,128)(2,1)}, u32[]{:S(2)}, u32[]{:S(2)}) collective-permute-start(bf16[392,1024]{1,0:T(8,128)(2,1)S(1)} %pad_maximum_fusion.7.refs_0_), channel_id=1, source_target_pairs={{0,12},{4,8},{8,4},{12,0},{1,13},{5,9},{9,5},{13,1},{2,14},{6,10},... | collective-permute-start | bytes 2408456 | tf_op jit(solution)/shard_map/ppermute | solution.py:182
  68.9 20.8 %all-to-all-start = ((bf16[4,512,128]{2,1,0:T(8,128)(2,1)}), bf16[4,512,128]{2,1,0:T(8,128)(2,1)S(1)}, u32[]{:S(2)}, u32[]{:S(2)}) async-start(bf16[4,512,128]{2,1,0:T(8,128)(2,1)} %bitcast.88), calls=%async_computation | async-start | bytes 1048576 | tf_op jit(solution)/shard_map/all_to_all | solution.py:860
  95.0 6.4 %collective-permute-start.8 = (bf16[4,128,1024]{2,1,0:T(8,128)(2,1)}, bf16[4,128,1024]{2,1,0:T(8,128)(2,1)}, u32[]{:S(2)}, u32[]{:S(2)}) collective-permute-start(bf16[4,128,1024]{2,1,0:T(8,128)(2,1)} %get-tuple-element.105), channel_id=1, source_target_pairs={{0,16},{16,0},{1,17},{17,1},{2,18},{18,2},{3,19},{19,3},{4,20},{20... | collective-permute-start | bytes 3145736 | tf_op jit(solution)/shard_map/ppermute | solution.py:182
  95.0 18.1 %collective-permute-start.9 = (bf16[1056,1024]{1,0:T(8,128)(2,1)}, bf16[1056,1024]{1,0:T(8,128)(2,1)}, u32[]{:S(2)}, u32[]{:S(2)}) collective-permute-start(bf16[1056,1024]{1,0:T(8,128)(2,1)} %bitcast.97), channel_id=1, source_target_pairs={{0,16},{16,0},{1,17},{17,1},{2,18},{18,2},{3,19},{19,3},{4,20},{20... | collective-permute-start | bytes 6488072 | tf_op jit(solution)/shard_map/ppermute | solution.py:182
  95.5 34.7 %collective-permute-start.11 = (bf16[512,1024]{1,0:T(8,128)(2,1)}, bf16[512,1024]{1,0:T(8,128)(2,1)}, u32[]{:S(2)}, u32[]{:S(2)}) collective-permute-start(bf16[512,1024]{1,0:T(8,128)(2,1)} %bitcast.17.g_ref.grad_ref.refs_4_), channel_id=1, source_target_pairs={{0,1},{1,0},{2,3},{3,2},{4,5},{5,4},{6,7},{7,6},{8,9},{9,8},{10,11... | collective-permute-start | bytes 3145736 | tf_op jit(solution)/shard_map/ppermute | solution.py:182
  97.8 11.8 %all-to-all-start.1 = ((bf16[4,512,128]{2,1,0:T(8,128)(2,1)}), bf16[4,512,128]{2,1,0:T(8,128)(2,1)S(1)}, u32[]{:S(2)}, u32[]{:S(2)}) async-start(bf16[4,512,128]{2,1,0:T(8,128)(2,1)} %bitcast.14), calls=%async_computation.1 | async-start | bytes 1048576 | tf_op jit(solution)/shard_map/all_to_all | solution.py:860
  112.6 30.7 %collective-permute-start.10 = (bf16[512,1024]{1,0:T(8,128)(2,1)S(1)}, bf16[512,1024]{1,0:T(8,128)(2,1)S(1)}, u32[]{:S(2)}, u32[]{:S(2)}) collective-permute-start(bf16[512,1024]{1,0:T(8,128)(2,1)S(1)} %multiply_convert_fusion.x_ref.refs_2_), channel_id=1, source_target_pairs={{0,1},{1,0},{2,3},{3,2},{4,5},{5,4},{6,7},{7,6},{8,9},{9,8},{10,11... | collective-permute-start | bytes 3145736 | tf_op jit(solution)/shard_map/ppermute | solution.py:182
  160.6 24.6 %collective-permute-start.12 = (bf16[512,1024]{1,0:T(8,128)(2,1)}, bf16[512,1024]{1,0:T(8,128)(2,1)}, u32[]{:S(2)}, u32[]{:S(2)}) collective-permute-start(bf16[512,1024]{1,0:T(8,128)(2,1)} %get-tuple-element.113), channel_id=1, source_target_pairs={{0,1},{1,0},{2,3},{3,2},{4,5},{5,4},{6,7},{7,6},{8,9},{9,8},{10,11... | collective-permute-start | bytes 3145736 | tf_op jit(solution)/shard_map/ppermute | solution.py:182
  185.2 19.6 %collective-permute-start.13 = (bf16[1056,1024]{1,0:T(8,128)(2,1)}, bf16[1056,1024]{1,0:T(8,128)(2,1)}, u32[]{:S(2)}, u32[]{:S(2)}) collective-permute-start(bf16[1056,1024]{1,0:T(8,128)(2,1)} %after.27), channel_id=1, source_target_pairs={{0,16},{16,0},{1,17},{17,1},{2,18},{18,2},{3,19},{19,3},{4,20},{20... | collective-permute-start | bytes 6488072 | tf_op jit(solution)/shard_map/ppermute | solution.py:182
  195.9 20.3 %all-to-all-start.2 = ((bf16[4,512,256]{2,1,0:T(8,128)(2,1)}), bf16[4,512,256]{2,1,0:T(8,128)(2,1)S(1)}, u32[]{:S(2)}, u32[]{:S(2)}) async-start(bf16[4,512,256]{2,1,0:T(8,128)(2,1)} %get-tuple-element.114.refs_1_), calls=%async_computation.2 | async-start | bytes 2097152 | tf_op jit(solution)/shard_map/all_to_all | solution.py:897
  204.3 34.8 %collective-permute-start.15 = (bf16[4,128,1024]{2,1,0:T(8,128)(2,1)}, bf16[4,128,1024]{2,1,0:T(8,128)(2,1)}, u32[]{:S(2)}, u32[]{:S(2)}) collective-permute-start(bf16[4,128,1024]{2,1,0:T(8,128)(2,1)} %get-tuple-element.160), channel_id=1, source_target_pairs={{0,16},{16,0},{1,17},{17,1},{2,18},{18,2},{3,19},{19,3},{4,20},{20... | collective-permute-start | bytes 3145736 | tf_op jit(solution)/shard_map/ppermute | solution.py:182
  204.8 34.3 %collective-permute-start.14 = (bf16[1056,1024]{1,0:T(8,128)(2,1)}, bf16[1056,1024]{1,0:T(8,128)(2,1)}, u32[]{:S(2)}, u32[]{:S(2)}) collective-permute-start(bf16[1056,1024]{1,0:T(8,128)(2,1)} %after.28), channel_id=1, source_target_pairs={{0,16},{16,0},{1,17},{17,1},{2,18},{18,2},{3,19},{19,3},{4,20},{20... | collective-permute-start | bytes 6488072 | tf_op jit(solution)/shard_map/ppermute | solution.py:182
  212.8 35.8 %collective-permute-start.17 = (bf16[3,88,1024]{2,1,0:T(8,128)(2,1)}, bf16[3,88,1024]{2,1,0:T(8,128)(2,1)S(1)}, u32[]{:S(2)}, u32[]{:S(2)}) collective-permute-start(bf16[3,88,1024]{2,1,0:T(8,128)(2,1)} %get-tuple-element.122), channel_id=1, source_target_pairs={{0,4},{4,0},{8,12},{12,8},{1,5},{5,1},{9,13},{13,9},{2,6},{6,2},{1... | collective-permute-start | bytes 1622024 | tf_op jit(solution)/shard_map/ppermute | solution.py:182
  214.7 34.7 %collective-permute-start.18 = (bf16[3,88,1024]{2,1,0:T(8,128)(2,1)}, bf16[3,88,1024]{2,1,0:T(8,128)(2,1)S(1)}, u32[]{:S(2)}, u32[]{:S(2)}) collective-permute-start(bf16[3,88,1024]{2,1,0:T(8,128)(2,1)} %get-tuple-element.123), channel_id=1, source_target_pairs={{0,8},{4,12},{8,0},{12,4},{1,9},{5,13},{9,1},{13,5},{2,10},{6,14},... | collective-permute-start | bytes 1622024 | tf_op jit(solution)/shard_map/ppermute | solution.py:182
  216.2 34.1 %collective-permute-start.19 = (bf16[3,88,1024]{2,1,0:T(8,128)(2,1)}, bf16[3,88,1024]{2,1,0:T(8,128)(2,1)S(1)}, u32[]{:S(2)}, u32[]{:S(2)}) collective-permute-start(bf16[3,88,1024]{2,1,0:T(8,128)(2,1)} %get-tuple-element.124), channel_id=1, source_target_pairs={{0,12},{4,8},{8,4},{12,0},{1,13},{5,9},{9,5},{13,1},{2,14},{6,10},... | collective-permute-start | bytes 1622024 | tf_op jit(solution)/shard_map/ppermute | solution.py:182
  253.0 48.2 %collective-permute-start.39 = (bf16[3,88,1024]{2,1,0:T(8,128)(2,1)S(1)}, bf16[3,88,1024]{2,1,0:T(8,128)(2,1)}, u32[]{:S(2)}, u32[]{:S(2)}) collective-permute-start(bf16[3,88,1024]{2,1,0:T(8,128)(2,1)S(1)} %add_convert_fusion.2.refs_1_.rest_0_), channel_id=1, source_target_pairs={{0,2},{1,3},{2,0},{3,1},{4,6},{5,7},{6,4},{7,5},{8,10},{9,11},{10,... | collective-permute-start | bytes 1622024 | tf_op jit(solution)/shard_map/ppermute | solution.py:182
  253.8 34.5 %collective-permute-start.16 = (bf16[512,1024]{1,0:T(8,128)(2,1)}, bf16[512,1024]{1,0:T(8,128)(2,1)S(1)}, u32[]{:S(2)}, u32[]{:S(2)}) collective-permute-start(bf16[512,1024]{1,0:T(8,128)(2,1)} %after.33), channel_id=1, source_target_pairs={{0,1},{1,0},{2,3},{3,2},{4,5},{5,4},{6,7},{7,6},{8,9},{9,8},{10,11... | collective-permute-start | bytes 3145736 | tf_op jit(solution)/shard_map/ppermute | solution.py:182
  255.0 42.4 %collective-permute-start.22 = (bf16[392,1024]{1,0:T(8,128)(2,1)}, bf16[392,1024]{1,0:T(8,128)(2,1)}, u32[]{:S(2)}, u32[]{:S(2)}) collective-permute-start(bf16[392,1024]{1,0:T(8,128)(2,1)} %after.37.rest_1_), channel_id=1, source_target_pairs={{0,4},{4,0},{8,12},{12,8},{1,5},{5,1},{9,13},{13,9},{2,6},{6,2},{1... | collective-permute-start | bytes 2408456 | tf_op jit(solution)/shard_map/ppermute | solution.py:182
  256.9 40.5 %collective-permute-start.23 = (bf16[392,1024]{1,0:T(8,128)(2,1)}, bf16[392,1024]{1,0:T(8,128)(2,1)S(1)}, u32[]{:S(2)}, u32[]{:S(2)}) collective-permute-start(bf16[392,1024]{1,0:T(8,128)(2,1)} %after.38.rest_2_), channel_id=1, source_target_pairs={{0,8},{4,12},{8,0},{12,4},{1,9},{5,13},{9,1},{13,5},{2,10},{6,14},... | collective-permute-start | bytes 2408456 | tf_op jit(solution)/shard_map/ppermute | solution.py:182
  258.4 35.2 %collective-permute-start.20 = (bf16[392,1024]{1,0:T(8,128)(2,1)S(1)}, bf16[392,1024]{1,0:T(8,128)(2,1)S(1)}, u32[]{:S(2)}, u32[]{:S(2)}) collective-permute-start(bf16[392,1024]{1,0:T(8,128)(2,1)S(1)} %copy-done.38), channel_id=1, source_target_pairs={{0,12},{4,8},{8,4},{12,0},{1,13},{5,9},{9,5},{13,1},{2,14},{6,10},... | collective-permute-start | bytes 2408456 | tf_op jit(solution)/shard_map/ppermute | solution.py:182
  294.4 9.4 %collective-permute-start.21 = (bf16[512,768]{1,0:T(8,128)(2,1)}, bf16[512,768]{1,0:T(8,128)(2,1)}, u32[]{:S(2)}, u32[]{:S(2)}) collective-permute-start(bf16[512,768]{1,0:T(8,128)(2,1)} %after.41), channel_id=1, source_target_pairs={{0,16},{16,0},{1,17},{17,1},{2,18},{18,2},{3,19},{19,3},{4,20},{20... | collective-permute-start | bytes 2359304 | tf_op jit(solution)/shard_map/ppermute | solution.py:182
  295.5 24.1 %collective-permute-start.28 = (bf16[256,1024]{1,0:T(8,128)(2,1)S(1)}, bf16[256,1024]{1,0:T(8,128)(2,1)}, u32[]{:S(2)}, u32[]{:S(2)}) collective-permute-start(bf16[256,1024]{1,0:T(8,128)(2,1)S(1)} %copy-done.16), channel_id=1, source_target_pairs={{0,4},{4,0},{8,12},{12,8},{1,5},{5,1},{9,13},{13,9},{2,6},{6,2},{1... | collective-permute-start | bytes 1572872 | tf_op jit(solution)/shard_map/ppermute | solution.py:182
  299.7 28.7 %collective-permute-start.27 = (bf16[256,1024]{1,0:T(8,128)(2,1)}, bf16[256,1024]{1,0:T(8,128)(2,1)}, u32[]{:S(2)}, u32[]{:S(2)}) collective-permute-start(bf16[256,1024]{1,0:T(8,128)(2,1)} %get-tuple-element.132), channel_id=1, source_target_pairs={{0,8},{4,12},{8,0},{12,4},{1,9},{5,13},{9,1},{13,5},{2,10},{6,14},... | collective-permute-start | bytes 1572872 | tf_op jit(solution)/shard_map/ppermute | solution.py:182
  318.0 7.2 %collective-permute-start.40 = (bf16[128,1024]{1,0:T(8,128)(2,1)S(1)}, bf16[128,1024]{1,0:T(8,128)(2,1)S(1)}, u32[]{:S(2)}, u32[]{:S(2)}) collective-permute-start(bf16[128,1024]{1,0:T(8,128)(2,1)S(1)} %slice.225.refs_0_), channel_id=1, source_target_pairs={{0,4},{4,0},{8,12},{12,8},{1,5},{5,1},{9,13},{13,9},{2,6},{6,2},{1... | collective-permute-start | bytes 786440 | tf_op jit(solution)/shard_map/ppermute | solution.py:182
  318.6 8.4 %collective-permute-start.41 = (bf16[136,1024]{1,0:T(8,128)(2,1)S(1)}, bf16[136,1024]{1,0:T(8,128)(2,1)S(1)}, u32[]{:S(2)}, u32[]{:S(2)}) collective-permute-start(bf16[136,1024]{1,0:T(8,128)(2,1)S(1)} %slice.226.refs_1_), channel_id=1, source_target_pairs={{0,8},{4,12},{8,0},{12,4},{1,9},{5,13},{9,1},{13,5},{2,10},{6,14},... | collective-permute-start | bytes 835592 | tf_op jit(solution)/shard_map/ppermute | solution.py:182
  319.5 11.7 %collective-permute-start.24 = (bf16[128,1024]{1,0:T(8,128)(2,1)S(1)}, bf16[128,1024]{1,0:T(8,128)(2,1)S(1)}, u32[]{:S(2)}, u32[]{:S(2)}) collective-permute-start(bf16[128,1024]{1,0:T(8,128)(2,1)S(1)} %get-tuple-element.164), channel_id=1, source_target_pairs={{0,1},{1,0},{2,3},{3,2},{4,5},{5,4},{6,7},{7,6},{8,9},{9,8},{10,11... | collective-permute-start | bytes 786440 | tf_op jit(solution)/shard_map/ppermute | solution.py:182
  319.6 21.3 %collective-permute-start.25 = (bf16[128,1024]{1,0:T(8,128)(2,1)S(1)}, bf16[128,1024]{1,0:T(8,128)(2,1)S(1)}, u32[]{:S(2)}, u32[]{:S(2)}) collective-permute-start(bf16[128,1024]{1,0:T(8,128)(2,1)S(1)} %get-tuple-element.165), channel_id=1, source_target_pairs={{0,2},{1,3},{2,0},{3,1},{4,6},{5,7},{6,4},{7,5},{8,10},{9,11},{10,... | collective-permute-start | bytes 786440 | tf_op jit(solution)/shard_map/ppermute | solution.py:182
  325.2 15.7 %collective-permute-start.26 = (bf16[128,1024]{1,0:T(8,128)(2,1)S(1)}, bf16[128,1024]{1,0:T(8,128)(2,1)S(1)}, u32[]{:S(2)}, u32[]{:S(2)}) collective-permute-start(bf16[128,1024]{1,0:T(8,128)(2,1)S(1)} %get-tuple-element.166), channel_id=1, source_target_pairs={{0,3},{1,2},{2,1},{3,0},{4,7},{5,6},{6,5},{7,4},{8,11},{9,10},{10,... | collective-permute-start | bytes 786440 | tf_op jit(solution)/shard_map/ppermute | solution.py:182
  327.0 26.1 %collective-permute-start.43 = (bf16[256,1024]{1,0:T(8,128)(2,1)}, bf16[256,1024]{1,0:T(8,128)(2,1)}, u32[]{:S(2)}, u32[]{:S(2)}) collective-permute-start(bf16[256,1024]{1,0:T(8,128)(2,1)} %pad_maximum_fusion.9), channel_id=1, source_target_pairs={{0,8},{4,12},{8,0},{12,4},{1,9},{5,13},{9,1},{13,5},{2,10},{6,14},... | collective-permute-start | bytes 1572872 | tf_op jit(solution)/shard_map/ppermute | solution.py:182
  328.3 24.8 %collective-permute-start.42 = (bf16[272,1024]{1,0:T(8,128)(2,1)S(1)}, bf16[272,1024]{1,0:T(8,128)(2,1)}, u32[]{:S(2)}, u32[]{:S(2)}) collective-permute-start(bf16[272,1024]{1,0:T(8,128)(2,1)S(1)} %pad_maximum_fusion.8), channel_id=1, source_target_pairs={{0,4},{4,0},{8,12},{12,8},{1,5},{5,1},{9,13},{13,9},{2,6},{6,2},{1... | collective-permute-start | bytes 1671176 | tf_op jit(solution)/shard_map/ppermute | solution.py:182
  341.7 8.9 %collective-permute-start.31 = (bf16[128,1024]{1,0:T(8,128)(2,1)}, bf16[128,1024]{1,0:T(8,128)(2,1)S(1)}, u32[]{:S(2)}, u32[]{:S(2)}) collective-permute-start(bf16[128,1024]{1,0:T(8,128)(2,1)} %after.44.refs_1_.refs_0_), channel_id=1, source_target_pairs={{0,1},{1,0},{2,3},{3,2},{4,5},{5,4},{6,7},{7,6},{8,9},{9,8},{10,11... | collective-permute-start | bytes 786440 | tf_op jit(solution)/shard_map/ppermute | solution.py:182
  345.9 29.9 %collective-permute-start.30 = (bf16[512,1024]{1,0:T(8,128)(2,1)}, bf16[512,1024]{1,0:T(8,128)(2,1)}, u32[]{:S(2)}, u32[]{:S(2)}) collective-permute-start(bf16[512,1024]{1,0:T(8,128)(2,1)} %fusion.13.refs_2_), channel_id=1, source_target_pairs={{0,8},{4,12},{8,0},{12,4},{1,9},{5,13},{9,1},{13,5},{2,10},{6,14},... | collective-permute-start | bytes 3145736 | tf_op jit(solution)/shard_map/ppermute | solution.py:182
  347.3 28.5 %collective-permute-start.29 = (bf16[512,1024]{1,0:T(8,128)(2,1)}, bf16[512,1024]{1,0:T(8,128)(2,1)}, u32[]{:S(2)}, u32[]{:S(2)}) collective-permute-start(bf16[512,1024]{1,0:T(8,128)(2,1)} %copy-done.21), channel_id=1, source_target_pairs={{0,4},{4,0},{8,12},{12,8},{1,5},{5,1},{9,13},{13,9},{2,6},{6,2},{1... | collective-permute-start | bytes 3145736 | tf_op jit(solution)/shard_map/ppermute | solution.py:182
  351.3 7.8 %collective-permute-start.32 = (f32[3,1024]{1,0:T(4,128)}, f32[3,1024]{1,0:T(4,128)S(1)}, u32[]{:S(2)}, u32[]{:S(2)}) collective-permute-start(f32[3,1024]{1,0:T(4,128)} %after.46), channel_id=1, source_target_pairs={{0,1},{1,0},{2,3},{3,2},{4,5},{5,4},{6,7},{7,6},{8,9},{9,8},{10,11... | collective-permute-start | bytes 36872 | tf_op jit(solution)/shard_map/ppermute | solution.py:182
  353.1 6.0 %collective-permute-start.33 = (f32[3,1024]{1,0:T(4,128)}, f32[3,1024]{1,0:T(4,128)S(1)}, u32[]{:S(2)}, u32[]{:S(2)}) collective-permute-start(f32[3,1024]{1,0:T(4,128)} %after.46), channel_id=1, source_target_pairs={{0,2},{1,3},{2,0},{3,1},{4,6},{5,7},{6,4},{7,5},{8,10},{9,11},{10,... | collective-permute-start | bytes 36872 | tf_op jit(solution)/shard_map/ppermute | solution.py:182
  353.1 6.0 %collective-permute-start.34 = (f32[3,1024]{1,0:T(4,128)}, f32[3,1024]{1,0:T(4,128)S(1)}, u32[]{:S(2)}, u32[]{:S(2)}) collective-permute-start(f32[3,1024]{1,0:T(4,128)} %after.46), channel_id=1, source_target_pairs={{0,3},{1,2},{2,1},{3,0},{4,7},{5,6},{6,5},{7,4},{8,11},{9,10},{10,... | collective-permute-start | bytes 36872 | tf_op jit(solution)/shard_map/ppermute | solution.py:182
  359.1 23.0 %collective-permute-start.44 = (bf16[3,352,1024]{2,1,0:T(8,128)(2,1)}, bf16[3,352,1024]{2,1,0:T(8,128)(2,1)}, u32[]{:S(2)}, u32[]{:S(2)}) collective-permute-start(bf16[3,352,1024]{2,1,0:T(8,128)(2,1)} %after.48), channel_id=1, source_target_pairs={{0,16},{16,0},{1,17},{17,1},{2,18},{18,2},{3,19},{19,3},{4,20},{20... | collective-permute-start | bytes 6488072 | tf_op jit(solution)/shard_map/ppermute | solution.py:182
  363.4 7.1 %collective-permute-start.36 = (f32[3,1024]{1,0:T(4,128)S(1)}, f32[3,1024]{1,0:T(4,128)S(1)}, u32[]{:S(2)}, u32[]{:S(2)}) collective-permute-start(f32[3,1024]{1,0:T(4,128)S(1)} %add.240), channel_id=1, source_target_pairs={{0,4},{4,0},{8,12},{12,8},{1,5},{5,1},{9,13},{13,9},{2,6},{6,2},{1... | collective-permute-start | bytes 36872 | tf_op jit(solution)/shard_map/ppermute | solution.py:182
  368.1 3.7 collective-permute-start.37
  370.5 4.6 %collective-permute-start.38 = (f32[3,1024]{1,0:T(4,128)S(1)}, f32[3,1024]{1,0:T(4,128)S(1)}, u32[]{:S(2)}, u32[]{:S(2)}) collective-permute-start(f32[3,1024]{1,0:T(4,128)S(1)} %add.240), channel_id=1, source_target_pairs={{0,12},{4,8},{8,4},{12,0},{1,13},{5,9},{9,5},{13,1},{2,14},{6,10},... | collective-permute-start | bytes 36872 | tf_op jit(solution)/shard_map/ppermute | solution.py:182
  371.8 24.8 %collective-permute-start.45 = (bf16[256,1024]{1,0:T(8,128)(2,1)S(1)}, bf16[256,1024]{1,0:T(8,128)(2,1)S(1)}, u32[]{:S(2)}, u32[]{:S(2)}) collective-permute-start(bf16[256,1024]{1,0:T(8,128)(2,1)S(1)} %pad_maximum_fusion.10), channel_id=1, source_target_pairs={{0,2},{1,3},{2,0},{3,1},{4,6},{5,7},{6,4},{7,5},{8,10},{9,11},{10,... | collective-permute-start | bytes 1572872 | tf_op jit(solution)/shard_map/ppermute | solution.py:182
  (61 other events, 341.8 us)

commit v2 on v1

--- a/solution.py
+++ b/solution.py
@@ -139,15 +139,12 @@
     carry=lax.fori_loop(j+1,full_end[j],functools.partial(step,False),carry)
     dk,dv=lax.fori_loop(full_end[j],some_end[j],functools.partial(step,True),carry)
     here=pl.ds(pl.multiple_of(j*block,block),block)
-    p_ref[here,lanes:2*lanes]=turned(dk*scale,cos_ref[here,:],-sin_ref[here,:]).astype(jnp.bfloat16)
+    cosine,sine=cos_ref[here,:],-sin_ref[here,:]
+    p_ref[:,:lanes]=turned(dq_ref[here,:],cosine,sine).astype(jnp.bfloat16)
+    p_ref[:,lanes:2*lanes]=turned(dk*scale,cosine,sine).astype(jnp.bfloat16)
     blend=dv.astype(jnp.bfloat16).astype(jnp.float32)
-    p_ref[here,2*lanes:]=(blend_weight*blend).astype(jnp.bfloat16)
+    p_ref[:,2*lanes:]=(blend_weight*blend).astype(jnp.bfloat16)
     first_ref[...]=((1.0-blend_weight)*blend).astype(jnp.bfloat16)
-    @pl.when(j==pl.num_programs(1)-1)
-    def _():
-        for i in range(length//block):
-            rows=pl.ds(i*block,block)
-            p_ref[rows,:lanes]=turned(dq_ref[rows,:],cos_ref[rows,:],-sin_ref[rows,:]).astype(jnp.bfloat16)
 
 def attend_backward(q,k,v,d,start,cosine,sine,block,group,o,lse,before=(),earlier=()):
     length,width=q.shape
@@ -163,7 +160,7 @@
     more=list(earlier)+list(before)
     spec=pltpu.PrefetchScalarGridSpec(num_scalar_prefetch=2,grid=(1,n),
         in_specs=[whole,part,part,whole,table,pl.BlockSpec((1,8,length),lambda g,j,*_:(0,0,0)),pl.BlockSpec((1,length),lambda g,j,*_:(0,0)),table,table]+[pl.BlockSpec(memory_space=pl.ANY)]*len(more),
-        out_specs=[pl.BlockSpec((length,3*lanes),lambda g,j,*_:(0,group)),part],
+        out_specs=[pl.BlockSpec((block,3*lanes),lambda g,j,*_:(j,group)),part],
         scratch_shapes=[pltpu.VMEM((length,lanes),jnp.float32),pltpu.VMEM((8,length),jnp.float32)])
     return pl.pallas_call(functools.partial(backward_kernel,block),grid_spec=spec,
         out_shape=[jax.ShapeDtypeStruct((length,3*width),jnp.bfloat16),jax.ShapeDtypeStruct((length,width),jnp.bfloat16)],
@@ -304,12 +301,13 @@
     cosine, sine = cos_ref[...], sin_ref[...]
     joined = dot(a, w_ref[...], NN)
     of = lax.broadcasted_iota(jnp.int32, (lanes, 128), 0) // HEAD_DIM
-    one_hot = (of == lax.broadcasted_iota(jnp.int32, (lanes, 128), 1)).astype(f32)
+    one_hot = (of == lax.broadcasted_iota(jnp.int32, (lanes, 128), 1)).astype(bf16)
 
     def norms(value):
-        squares = lax.dot_general(
-            value * value, one_hot, NN, precision=lax.Precision.HIGHEST, preferred_element_type=f32
-        )
+        wide = value * value
+        high = wide.astype(bf16)
+        low = (wide - high.astype(f32)).astype(bf16)
+        squares = dot(high, one_hot, NN) + dot(low, one_hot, NN)
         return jnp.sum(jnp.sqrt(jnp.maximum(squares, 0.0)), axis=0, keepdims=True)
 
     @pl.when(i == 0)

time: 412 us -> 411 us (level)
  starting transfers between devices: 63.4 us -> 70.2 us
  Pallas kernels: 185 us -> 180 us
    ppermute x47, starting transfers between devices: 52.4 us -> 58.5 us  [swap(): lax.ppermute(x, axis, [(i, i ^ mask) for i in range(lax.axis_size(axis))])]
  transfers between devices with their start and end apart: 50 -> 50, of which waited for: 14 -> 15; matrix products, arithmetic and copies ran while one was open for 18% -> 18% of each run, Pallas kernels for 41% -> 39%
where the time goes in v2:
time: 411 us; the launch traced here: 406 us
  Pallas kernels  180 us (44%)
  starting transfers between devices  70.2 us (17%)
  waiting for transfers between devices  58 us (14%)
  other arithmetic  47.8 us (12%)
  local copies, waits for them, and re-layouts  34.2 us (8%)
  matrix products  14.2 us (3%)
    ppermute x47, starting transfers between devices, swap(): lax.ppermute(x, axis, [(i, i ^ mask) for i in range(lax.axis_size(axis))])  58.5 us
    ppermute x47, waiting for transfers between devices, swap(): lax.ppermute(x, axis, [(i, i ^ mask) for i in range(lax.axis_size(axis))])  47.9 us
    pallas_call x2, Pallas kernels, attend_backward(): pl.pallas_call(functools.partial(backward_kernel, block), grid_spec=spec,...  43 us
    pallas_call x2, Pallas kernels, feed(): pl.pallas_call(feed_kernel, grid=(4,), in_specs=[spec_whole(x), spec_whol...  32.8 us
    pallas_call x2, Pallas kernels, attend_forward2(): pl.pallas_call(functools.partial(fwd2_kernel, block), grid_spec=spec, out...  23.9 us
    unnamed x123, local copies, waits for them, and re-layouts  19.2 us
    pallas_call x1, Pallas kernels, others(): pl.pallas_call(others_kernel, grid_spec=spec, out_shape=[half, half] + [j...  18.9 us
    pallas_call x2, Pallas kernels, shard_grads(): pl.pallas_call(kernel, grid_spec=spec, out_shape=out_shape, compiler_para...  17.4 us
  transfers between devices with their start and end apart: 50, of which 15 were waited for; matrix products, arithmetic and copies ran while one was open for 18% of the time, Pallas kernels for 39%

profile of v2, /device:TPU:0, one launch (start us, length us, event | category | flops | bytes accessed | tf_op | source)
XLA Modules:
  0.0 406.3 jit_solution(7986653426474089567)
XLA Ops:
  0.7 3.0 collective-permute-start
  5.2 2.6 pad_maximum_fusion.refs_0_.refs_1_.refs_2_
  7.9 2.1 copy-done.13
  10.0 2.7 collective-permute-start.4
  19.1 5.5 %fusion.9 = (f32[2048,128]{1,0:T(8,128)}, f32[2048,128]{1,0:T(8,128)}) fusion(f32[128]{0:T(128)S(1)} %get-tuple-element.175, f32[128]{0:T(128)S(1)} %get-tuple-element.176, f32[2048]{0:T(1024)S(1)} %bitcast.90), kind=kLoop, calls=%fused_computation.45 | loop fusion | flops 524288 | bytes 2106368 | tf_op jit(solution)/shard_map/mul | solution.py:841
  24.6 2.6 collective-permute-done.refs_2_
  32.7 10.9 %project.2 = (bf16[2048,1024]{1,0:T(8,128)(2,1)}, bf16[2048,256]{1,0:T(8,128)(2,1)}, bf16[2048,256]{1,0:T(8,128)(2,1)}, bf16[2048,256]{1,0:T(8,128)(2,1)}, f32[8,128]{1,0:T(8,128)}) custom-call(s32[1]{0:T(128)} %bitcast.2.rank_ref, bf16[512,1024]{1,0:T(8,128)(2,1)} %bitcast.77, bf16[512,1024]{1,0:T(8,128)(2,1)} %collective-permute-done.2.refs_1_, ...), custom_call_target="tpu_custom_call" | custom-call | flops 14849999872 | bytes 1350000 | tf_op jit(solution)/shard_map/project/pallas_call | solution.py:361
  49.4 4.2 %project.3 = (bf16[2048,1024]{1,0:T(8,128)(2,1)}, bf16[2048,256]{1,0:T(8,128)(2,1)}, bf16[2048,256]{1,0:T(8,128)(2,1)}, bf16[2048,256]{1,0:T(8,128)(2,1)}, f32[8,128]{1,0:T(8,128)}) custom-call(s32[1]{0:T(128)} %bitcast.2.rank_ref, bf16[256,1024]{1,0:T(8,128)(2,1)} %copy-done.42, ...), custom_call_target="tpu_custom_call", output_to_operand_aliasing={{0}: (8, {}), {1}: (9, {}), {2}: (10, {}), {3}: (11, {})} | custom-call | flops 4950000128 | bytes 450000 | tf_op jit(solution)/shard_map/project/pallas_call | solution.py:361
  53.6 12.1 %attend_forward.2 = (bf16[2048,128]{1,0:T(8,128)(2,1)}, f32[1,8,2048]{2,1,0:T(8,128)}) custom-call(s32[2]{0:T(128)} %slice.174.firsts, s32[2]{0:T(128)} %slice.175.lasts, bf16[2048,256]{1,0:T(8,128)(2,1)} %get-tuple-element.100.q_ref, bf16[2048,256]{1,0:T(8,128)(2,1)} %get-tuple-element.101.k_ref, bf16[2048,256]{1,0:T(8,128)(2,1)} %get-tuple-element.102.v_ref, ...), custom_call_target="tpu_custom_call" | custom-call | flops 15569256448 | bytes 2097152 | tf_op jit(solution)/shard_map/attend_forward/pallas_call | solution.py:89
  65.7 4.0 all-to-all-start
  69.7 11.8 %attend_forward.3 = (bf16[2048,128]{1,0:T(8,128)(2,1)}, f32[1,8,2048]{2,1,0:T(8,128)}) custom-call(s32[2]{0:T(128)} %slice.174.firsts, s32[2]{0:T(128)} %slice.175.lasts, bf16[2048,256]{1,0:T(8,128)(2,1)} %get-tuple-element.100.q_ref, bf16[2048,256]{1,0:T(8,128)(2,1)} %get-tuple-element.101.k_ref, bf16[2048,256]{1,0:T(8,128)(2,1)} %get-tuple-element.102.v_ref, ...), custom_call_target="tpu_custom_call" | custom-call | flops 15569256448 | bytes 2097152 | tf_op jit(solution)/shard_map/attend_forward/pallas_call | solution.py:89
  81.6 5.6 %all-to-all-done.refs_4_ = bf16[4,512,128]{2,1,0:T(8,128)(2,1)S(1)} async-done(((bf16[4,512,128]{2,1,0:T(8,128)(2,1)}), bf16[4,512,128]{2,1,0:T(8,128)(2,1)S(1)}, u32[]{:S(2)}, u32[]{:S(2)}) %all-to-all-start) | async-done | bytes 524320 | tf_op jit(solution)/shard_map/all_to_all | solution.py:858
  88.5 4.0 assemble.1
  95.3 3.6 all-to-all-start.1
  100.7 2.0 fusion.26
  102.8 4.4 %all-to-all-done.1 = bf16[4,512,128]{2,1,0:T(8,128)(2,1)S(1)} async-done(((bf16[4,512,128]{2,1,0:T(8,128)(2,1)}), bf16[4,512,128]{2,1,0:T(8,128)(2,1)S(1)}, u32[]{:S(2)}, u32[]{:S(2)}) %all-to-all-start.1) | async-done | bytes 524320 | tf_op jit(solution)/shard_map/all_to_all | solution.py:858
  107.1 2.7 multiply_reduce_fusion
  111.4 16.4 %feed.2 = (bf16[4,3,352,512]{3,2,1,0:T(8,128)(2,1)}, f32[512,1024]{1,0:T(8,128)}) custom-call(bf16[512,1024]{1,0:T(8,128)(2,1)} %copy-done.35, bf16[512,1024]{1,0:T(8,128)(2,1)} %bitcast.17.g_ref.grad_ref.refs_4_, bf16[2112,1024]{1,0:T(8,128)(2,1)} %copy-done.13, bf16[2112,1024]{1,0:T(8,128)(2,1)} %copy-done.13, bf16[2112,1024]{1,0:T(8,128)(2,1)} %copy-done.13, ...), custom_call_target="tpu_custom_call" | custom-call | flops 17600000000 | bytes 1600000 | tf_op jit(solution)/shard_map/feed/pallas_call | solution.py:447
  127.8 13.0 %collective-permute-done.10.x_ref.xn_ref.refs_3_ = bf16[512,1024]{1,0:T(8,128)(2,1)S(1)} collective-permute-done((bf16[512,1024]{1,0:T(8,128)(2,1)S(1)}, bf16[512,1024]{1,0:T(8,128)(2,1)S(1)}, u32[]{:S(2)}, u32[]{:S(2)}) %collective-permute-start.10) | collective-permute-done | bytes 1048608 | tf_op jit(solution)/shard_map/ppermute | solution.py:179
  141.8 16.3 %feed.3 = (bf16[4,3,352,512]{3,2,1,0:T(8,128)(2,1)}, bf16[512,1024]{1,0:T(8,128)(2,1)}) custom-call(bf16[512,1024]{1,0:T(8,128)(2,1)} %copy-done.56, bf16[512,1024]{1,0:T(8,128)(2,1)} %collective-permute-done.11.g_ref.gn_ref.refs_5_, bf16[2112,1024]{1,0:T(8,128)(2,1)} %copy-done.13, bf16[2112,1024]{1,0:T(8,128)(2,1)} %copy-done.13, ...), custom_call_target="tpu_custom_call" | custom-call | flops 17600000000 | bytes 1600000 | tf_op jit(solution)/shard_map/feed/pallas_call | solution.py:447
  159.8 18.9 %others.1 = (bf16[1056,1024]{1,0:T(8,128)(2,1)}, bf16[1056,1024]{1,0:T(8,128)(2,1)}, f32[512,1024]{1,0:T(8,128)}, bf16[512,1024]{1,0:T(8,128)(2,1)}) custom-call(s32[2]{0:T(128)} %pad_add_fusion.scalars, bf16[4,3,352,512]{3,2,1,0:T(8,128)(2,1)} %get-tuple-element.107.act_ref.refs_0_, bf16[4,3,352,512]{3,2,1,0:T(8,128)(2,1)} %get-tuple-element.109.near_ref.refs_1_, ...), custom_call_target="tpu_custom_call" | custom-call | flops 20899999744 | bytes 1900000 | tf_op jit(solution)/shard_map/others/pallas_call | solution.py:629
  178.7 4.1 %collective-permute-done.12.refs_0_ = bf16[512,1024]{1,0:T(8,128)(2,1)} collective-permute-done((bf16[512,1024]{1,0:T(8,128)(2,1)}, bf16[512,1024]{1,0:T(8,128)(2,1)}, u32[]{:S(2)}, u32[]{:S(2)}) %collective-permute-start.12) | collective-permute-done | bytes 1048608 | tf_op jit(solution)/shard_map/ppermute | solution.py:179
  185.4 8.2 %state_back.1 = (f32[512,1024]{1,0:T(8,128)}, bf16[512,1024]{1,0:T(8,128)(2,1)}, bf16[4,512,256]{2,1,0:T(8,128)(2,1)}, f32[1,1024]{1,0:T(1,128)}) custom-call(bf16[512,1024]{1,0:T(8,128)(2,1)} %after.26.refs_1_.back_ref, f32[512,1024]{1,0:T(8,128)} %get-tuple-element.108.refs_9_.terms_ref, f32[512,1024]{1,0:T(8,128)} %copy-done.3, ...), custom_call_target="tpu_custom_call" | custom-call | flops 6600000000 | bytes 600000 | tf_op jit(solution)/shard_map/state_back/pallas_call | solution.py:765
  193.6 4.0 all-to-all-start.2
  197.6 2.0 convolution_convert_fusion.2
  202.8 7.9 %far_sum.1 = (bf16[3,88,1024]{2,1,0:T(8,128)(2,1)}, bf16[3,88,1024]{2,1,0:T(8,128)(2,1)}, bf16[3,88,1024]{2,1,0:T(8,128)(2,1)}, bf16[3,88,1024]{2,1,0:T(8,128)(2,1)}) custom-call(s32[2]{0:T(128)} %pad_add_fusion.scalars, bf16[4,3,352,512]{3,2,1,0:T(8,128)(2,1)} %get-tuple-element.107.act_ref.refs_0_, ...), custom_call_target="tpu_custom_call" | custom-call | flops 8800000000 | bytes 800000 | tf_op jit(solution)/shard_map/far_sum/pallas_call | solution.py:563
  215.1 21.4 %attend_backward.2 = (bf16[2048,768]{1,0:T(8,128)(2,1)}, bf16[2048,256]{1,0:T(8,128)(2,1)}) custom-call(s32[4]{0:T(128)} %get-tuple-element.172.full_end, s32[4]{0:T(128)} %get-tuple-element.171.some_end, bf16[2048,256]{1,0:T(8,128)(2,1)} %get-tuple-element.100.q_ref, bf16[2048,256]{1,0:T(8,128)(2,1)} %get-tuple-element.101.k_ref, ...), custom_call_target="tpu_custom_call" | custom-call | flops 27917287424 | bytes 5767168 | tf_op jit(solution)/shard_map/attend_backward/pallas_call | solution.py:165
  236.6 9.5 %own_sum.1 = (bf16[392,1024]{1,0:T(8,128)(2,1)}, bf16[392,1024]{1,0:T(8,128)(2,1)}, bf16[392,1024]{1,0:T(8,128)(2,1)}, bf16[392,1024]{1,0:T(8,128)(2,1)}) custom-call(s32[2]{0:T(128)} %pad_add_fusion.scalars, bf16[4,3,352,512]{3,2,1,0:T(8,128)(2,1)} %get-tuple-element.107.act_ref.refs_0_, bf16[4,3,352,512]{3,2,1,0:T(8,128)(2,1)} %get-tuple-element.109.near_ref.refs_1_, ...), custom_call_target="tpu_custom_call" | custom-call | flops 8800000000 | bytes 800000 | tf_op jit(solution)/shard_map/own_sum/pallas_call | solution.py:563
  251.3 2.0 collective-permute-start.22
  255.3 21.6 %attend_backward.3 = (bf16[2048,768]{1,0:T(8,128)(2,1)}, bf16[2048,256]{1,0:T(8,128)(2,1)}) custom-call(s32[4]{0:T(128)} %get-tuple-element.172.full_end, s32[4]{0:T(128)} %get-tuple-element.171.some_end, bf16[2048,256]{1,0:T(8,128)(2,1)} %get-tuple-element.100.q_ref, ...), custom_call_target="tpu_custom_call", output_to_operand_aliasing={{0}: (15, {}), {1}: (16, {})} | custom-call | flops 27917287424 | bytes 5767168 | tf_op jit(solution)/shard_map/attend_backward/pallas_call | solution.py:165
  276.9 6.7 %convolution_convert_fusion.refs_4_ = bf16[1024,768]{1,0:T(8,128)(2,1)S(1)} fusion(bf16[2048,1024]{1,0:T(8,128)(2,1)} %get-tuple-element.120, bf16[2048,768]{1,0:T(8,128)(2,1)} %get-tuple-element.129.refs_3_.refs_4_), kind=kOutput, calls=%fused_computation.31 | convolution fusion | flops 3222011904 | bytes 8912896 | tf_op jit(solution)/shard_map/dot_general | solution.py:18
  287.3 3.9 unproject.2
  298.3 2.7 fusion.8.refs_0_
  303.4 9.5 %unproject.3 = (bf16[512,1024]{1,0:T(8,128)(2,1)}, bf16[512,1024]{1,0:T(8,128)(2,1)}, bf16[512,1024]{1,0:T(8,128)(2,1)}, f32[1,1024]{1,0:T(1,128)}) custom-call(s32[1]{0:T(128)} %bitcast.2.rank_ref, bf16[512,1024]{1,0:T(8,128)(2,1)} %bitcast.78, bf16[512,1024]{1,0:T(8,128)(2,1)} %collective-permute-done.2.refs_1_, ...), custom_call_target="tpu_custom_call" | custom-call | flops 11550000128 | bytes 1050000 | tf_op jit(solution)/shard_map/unproject/pallas_call | solution.py:730
  317.4 3.9 collective-permute-start.25
  321.4 2.2 fusion.13.refs_2_
  323.6 4.3 %collective-permute-start.26 = (bf16[128,1024]{1,0:T(8,128)(2,1)S(1)}, bf16[128,1024]{1,0:T(8,128)(2,1)S(1)}, u32[]{:S(2)}, u32[]{:S(2)}) collective-permute-start(bf16[128,1024]{1,0:T(8,128)(2,1)S(1)} %get-tuple-element.166), channel_id=1, source_target_pairs={{0,3},{1,2},{2,1},{3,0},{4,7},{5,6},{6,5},{7,4},{8,11},{9,10},{10,... | collective-permute-start | bytes 786440 | tf_op jit(solution)/shard_map/ppermute | solution.py:179
  331.9 7.9 %collective-permute-done.25 = bf16[128,1024]{1,0:T(8,128)(2,1)S(1)} collective-permute-done((bf16[128,1024]{1,0:T(8,128)(2,1)S(1)}, bf16[128,1024]{1,0:T(8,128)(2,1)S(1)}, u32[]{:S(2)}, u32[]{:S(2)}) %collective-permute-start.25) | collective-permute-done | bytes 262176 | tf_op jit(solution)/shard_map/ppermute | solution.py:179
  340.7 5.4 %collective-permute-start.31 = (bf16[128,1024]{1,0:T(8,128)(2,1)}, bf16[128,1024]{1,0:T(8,128)(2,1)S(1)}, u32[]{:S(2)}, u32[]{:S(2)}) collective-permute-start(bf16[128,1024]{1,0:T(8,128)(2,1)} %after.44.refs_1_.refs_0_), channel_id=1, source_target_pairs={{0,1},{1,0},{2,3},{3,2},{4,5},{5,4},{6,7},{7,6},{8,9},{9,8},{10,11... | collective-permute-start | bytes 786440 | tf_op jit(solution)/shard_map/ppermute | solution.py:179
  349.2 2.9 collective-permute-done.31.refs_1_
  357.2 3.4 regroup.1
  361.7 3.3 collective-permute-done.35
  365.8 3.6 add_convert_fusion.refs_1_
  377.4 2.5 fusion
  379.9 3.7 fusion.6.refs_2_
  383.6 2.2 broadcast_select_fusion.1
  386.9 3.7 slice_bitcast_fusion
  391.7 6.4 %collective-permute-done.45 = bf16[256,1024]{1,0:T(8,128)(2,1)S(1)} collective-permute-done((bf16[256,1024]{1,0:T(8,128)(2,1)S(1)}, bf16[256,1024]{1,0:T(8,128)(2,1)S(1)}, u32[]{:S(2)}, u32[]{:S(2)}) %collective-permute-start.45) | collective-permute-done | bytes 524320 | tf_op jit(solution)/shard_map/ppermute | solution.py:179
  (296 shorter events, 97.2 us)
Async XLA Ops:
  0.7 26.5 %collective-permute-start = (bf16[512,1024]{1,0:T(8,128)(2,1)}, bf16[512,1024]{1,0:T(8,128)(2,1)}, u32[]{:S(2)}, u32[]{:S(2)}) collective-permute-start(bf16[512,1024]{1,0:T(8,128)(2,1)} %bitcast.75), channel_id=1, source_target_pairs={{0,8},{4,12},{8,0},{12,4},{1,9},{5,13},{9,1},{13,5},{2,10},{6,14},... | collective-permute-start | bytes 3145736 | tf_op jit(solution)/shard_map/ppermute | solution.py:179
  3.7 26.3 %collective-permute-start.2 = (bf16[512,1024]{1,0:T(8,128)(2,1)}, bf16[512,1024]{1,0:T(8,128)(2,1)}, u32[]{:S(2)}, u32[]{:S(2)}) collective-permute-start(bf16[512,1024]{1,0:T(8,128)(2,1)} %bitcast.76), channel_id=1, source_target_pairs={{0,4},{4,0},{8,12},{12,8},{1,5},{5,1},{9,13},{13,9},{2,6},{6,2},{1... | collective-permute-start | bytes 3145736 | tf_op jit(solution)/shard_map/ppermute | solution.py:179
  10.0 33.6 %collective-permute-start.4 = (bf16[3,88,1024]{2,1,0:T(8,128)(2,1)S(1)}, bf16[3,88,1024]{2,1,0:T(8,128)(2,1)S(1)}, u32[]{:S(2)}, u32[]{:S(2)}) collective-permute-start(bf16[3,88,1024]{2,1,0:T(8,128)(2,1)S(1)} %dynamic-slice_bitcast_fusion.2), channel_id=1, source_target_pairs={{0,2},{1,3},{2,0},{3,1},{4,6},{5,7},{6,4},{7,5},{8,10},{9,11},{10,... | collective-permute-start | bytes 1622024 | tf_op jit(solution)/shard_map/ppermute | solution.py:179
  28.3 15.4 %collective-permute-start.1 = (bf16[256,1024]{1,0:T(8,128)(2,1)S(1)}, bf16[256,1024]{1,0:T(8,128)(2,1)S(1)}, u32[]{:S(2)}, u32[]{:S(2)}) collective-permute-start(bf16[256,1024]{1,0:T(8,128)(2,1)S(1)} %slice.216), channel_id=1, source_target_pairs={{0,4},{4,0},{8,12},{12,8},{1,5},{5,1},{9,13},{13,9},{2,6},{6,2},{1... | collective-permute-start | bytes 1572872 | tf_op jit(solution)/shard_map/ppermute | solution.py:179
  31.1 12.6 %collective-permute-start.3 = (bf16[256,1024]{1,0:T(8,128)(2,1)S(1)}, bf16[256,1024]{1,0:T(8,128)(2,1)S(1)}, u32[]{:S(2)}, u32[]{:S(2)}) collective-permute-start(bf16[256,1024]{1,0:T(8,128)(2,1)S(1)} %slice.217), channel_id=1, source_target_pairs={{0,8},{4,12},{8,0},{12,4},{1,9},{5,13},{9,1},{13,5},{2,10},{6,14},... | collective-permute-start | bytes 1572872 | tf_op jit(solution)/shard_map/ppermute | solution.py:179
  45.9 41.3 %collective-permute-start.5 = (bf16[392,1024]{1,0:T(8,128)(2,1)S(1)}, bf16[392,1024]{1,0:T(8,128)(2,1)S(1)}, u32[]{:S(2)}, u32[]{:S(2)}) collective-permute-start(bf16[392,1024]{1,0:T(8,128)(2,1)S(1)} %pad_maximum_fusion.7.refs_0_), channel_id=1, source_target_pairs={{0,4},{4,0},{8,12},{12,8},{1,5},{5,1},{9,13},{13,9},{2,6},{6,2},{1... | collective-permute-start | bytes 2408456 | tf_op jit(solution)/shard_map/ppermute | solution.py:179
  46.5 40.8 %collective-permute-start.6 = (bf16[392,1024]{1,0:T(8,128)(2,1)S(1)}, bf16[392,1024]{1,0:T(8,128)(2,1)S(1)}, u32[]{:S(2)}, u32[]{:S(2)}) collective-permute-start(bf16[392,1024]{1,0:T(8,128)(2,1)S(1)} %pad_maximum_fusion.7.refs_0_), channel_id=1, source_target_pairs={{0,8},{4,12},{8,0},{12,4},{1,9},{5,13},{9,1},{13,5},{2,10},{6,14},... | collective-permute-start | bytes 2408456 | tf_op jit(solution)/shard_map/ppermute | solution.py:179
  47.7 39.5 %collective-permute-start.7 = (bf16[392,1024]{1,0:T(8,128)(2,1)S(1)}, bf16[392,1024]{1,0:T(8,128)(2,1)}, u32[]{:S(2)}, u32[]{:S(2)}) collective-permute-start(bf16[392,1024]{1,0:T(8,128)(2,1)S(1)} %pad_maximum_fusion.7.refs_0_), channel_id=1, source_target_pairs={{0,12},{4,8},{8,4},{12,0},{1,13},{5,9},{9,5},{13,1},{2,14},{6,10},... | collective-permute-start | bytes 2408456 | tf_op jit(solution)/shard_map/ppermute | solution.py:179
  65.7 21.5 %all-to-all-start = ((bf16[4,512,128]{2,1,0:T(8,128)(2,1)}), bf16[4,512,128]{2,1,0:T(8,128)(2,1)S(1)}, u32[]{:S(2)}, u32[]{:S(2)}) async-start(bf16[4,512,128]{2,1,0:T(8,128)(2,1)} %bitcast.88), calls=%async_computation | async-start | bytes 1048576 | tf_op jit(solution)/shard_map/all_to_all | solution.py:858
  92.6 6.4 %collective-permute-start.8 = (bf16[4,128,1024]{2,1,0:T(8,128)(2,1)}, bf16[4,128,1024]{2,1,0:T(8,128)(2,1)}, u32[]{:S(2)}, u32[]{:S(2)}) collective-permute-start(bf16[4,128,1024]{2,1,0:T(8,128)(2,1)} %get-tuple-element.105), channel_id=1, source_target_pairs={{0,16},{16,0},{1,17},{17,1},{2,18},{18,2},{3,19},{19,3},{4,20},{20... | collective-permute-start | bytes 3145736 | tf_op jit(solution)/shard_map/ppermute | solution.py:179
  92.6 18.1 %collective-permute-start.9 = (bf16[1056,1024]{1,0:T(8,128)(2,1)}, bf16[1056,1024]{1,0:T(8,128)(2,1)}, u32[]{:S(2)}, u32[]{:S(2)}) collective-permute-start(bf16[1056,1024]{1,0:T(8,128)(2,1)} %bitcast.97), channel_id=1, source_target_pairs={{0,16},{16,0},{1,17},{17,1},{2,18},{18,2},{3,19},{19,3},{4,20},{20... | collective-permute-start | bytes 6488072 | tf_op jit(solution)/shard_map/ppermute | solution.py:179
  93.1 34.8 %collective-permute-start.11 = (bf16[512,1024]{1,0:T(8,128)(2,1)}, bf16[512,1024]{1,0:T(8,128)(2,1)}, u32[]{:S(2)}, u32[]{:S(2)}) collective-permute-start(bf16[512,1024]{1,0:T(8,128)(2,1)} %bitcast.17.g_ref.grad_ref.refs_4_), channel_id=1, source_target_pairs={{0,1},{1,0},{2,3},{3,2},{4,5},{5,4},{6,7},{7,6},{8,9},{9,8},{10,11... | collective-permute-start | bytes 3145736 | tf_op jit(solution)/shard_map/ppermute | solution.py:179
  95.3 11.8 %all-to-all-start.1 = ((bf16[4,512,128]{2,1,0:T(8,128)(2,1)}), bf16[4,512,128]{2,1,0:T(8,128)(2,1)S(1)}, u32[]{:S(2)}, u32[]{:S(2)}) async-start(bf16[4,512,128]{2,1,0:T(8,128)(2,1)} %bitcast.14), calls=%async_computation.1 | async-start | bytes 1048576 | tf_op jit(solution)/shard_map/all_to_all | solution.py:858
  110.2 30.7 %collective-permute-start.10 = (bf16[512,1024]{1,0:T(8,128)(2,1)S(1)}, bf16[512,1024]{1,0:T(8,128)(2,1)S(1)}, u32[]{:S(2)}, u32[]{:S(2)}) collective-permute-start(bf16[512,1024]{1,0:T(8,128)(2,1)S(1)} %multiply_convert_fusion.x_ref.refs_2_), channel_id=1, source_target_pairs={{0,1},{1,0},{2,3},{3,2},{4,5},{5,4},{6,7},{7,6},{8,9},{9,8},{10,11... | collective-permute-start | bytes 3145736 | tf_op jit(solution)/shard_map/ppermute | solution.py:179
  158.2 24.7 %collective-permute-start.12 = (bf16[512,1024]{1,0:T(8,128)(2,1)}, bf16[512,1024]{1,0:T(8,128)(2,1)}, u32[]{:S(2)}, u32[]{:S(2)}) collective-permute-start(bf16[512,1024]{1,0:T(8,128)(2,1)} %get-tuple-element.113), channel_id=1, source_target_pairs={{0,1},{1,0},{2,3},{3,2},{4,5},{5,4},{6,7},{7,6},{8,9},{9,8},{10,11... | collective-permute-start | bytes 3145736 | tf_op jit(solution)/shard_map/ppermute | solution.py:179
  182.8 19.9 %collective-permute-start.13 = (bf16[1056,1024]{1,0:T(8,128)(2,1)}, bf16[1056,1024]{1,0:T(8,128)(2,1)}, u32[]{:S(2)}, u32[]{:S(2)}) collective-permute-start(bf16[1056,1024]{1,0:T(8,128)(2,1)} %after.27), channel_id=1, source_target_pairs={{0,16},{16,0},{1,17},{17,1},{2,18},{18,2},{3,19},{19,3},{4,20},{20... | collective-permute-start | bytes 6488072 | tf_op jit(solution)/shard_map/ppermute | solution.py:179
  193.6 20.6 %all-to-all-start.2 = ((bf16[4,512,256]{2,1,0:T(8,128)(2,1)}), bf16[4,512,256]{2,1,0:T(8,128)(2,1)S(1)}, u32[]{:S(2)}, u32[]{:S(2)}) async-start(bf16[4,512,256]{2,1,0:T(8,128)(2,1)} %get-tuple-element.114.refs_1_), calls=%async_computation.2 | async-start | bytes 2097152 | tf_op jit(solution)/shard_map/all_to_all | solution.py:895
  202.2 34.4 %collective-permute-start.15 = (bf16[4,128,1024]{2,1,0:T(8,128)(2,1)}, bf16[4,128,1024]{2,1,0:T(8,128)(2,1)}, u32[]{:S(2)}, u32[]{:S(2)}) collective-permute-start(bf16[4,128,1024]{2,1,0:T(8,128)(2,1)} %get-tuple-element.160), channel_id=1, source_target_pairs={{0,16},{16,0},{1,17},{17,1},{2,18},{18,2},{3,19},{19,3},{4,20},{20... | collective-permute-start | bytes 3145736 | tf_op jit(solution)/shard_map/ppermute | solution.py:179
  202.7 33.9 %collective-permute-start.14 = (bf16[1056,1024]{1,0:T(8,128)(2,1)}, bf16[1056,1024]{1,0:T(8,128)(2,1)}, u32[]{:S(2)}, u32[]{:S(2)}) collective-permute-start(bf16[1056,1024]{1,0:T(8,128)(2,1)} %after.28), channel_id=1, source_target_pairs={{0,16},{16,0},{1,17},{17,1},{2,18},{18,2},{3,19},{19,3},{4,20},{20... | collective-permute-start | bytes 6488072 | tf_op jit(solution)/shard_map/ppermute | solution.py:179
  210.7 35.4 %collective-permute-start.17 = (bf16[3,88,1024]{2,1,0:T(8,128)(2,1)}, bf16[3,88,1024]{2,1,0:T(8,128)(2,1)S(1)}, u32[]{:S(2)}, u32[]{:S(2)}) collective-permute-start(bf16[3,88,1024]{2,1,0:T(8,128)(2,1)} %get-tuple-element.122), channel_id=1, source_target_pairs={{0,4},{4,0},{8,12},{12,8},{1,5},{5,1},{9,13},{13,9},{2,6},{6,2},{1... | collective-permute-start | bytes 1622024 | tf_op jit(solution)/shard_map/ppermute | solution.py:179
  212.6 34.3 %collective-permute-start.18 = (bf16[3,88,1024]{2,1,0:T(8,128)(2,1)}, bf16[3,88,1024]{2,1,0:T(8,128)(2,1)S(1)}, u32[]{:S(2)}, u32[]{:S(2)}) collective-permute-start(bf16[3,88,1024]{2,1,0:T(8,128)(2,1)} %get-tuple-element.123), channel_id=1, source_target_pairs={{0,8},{4,12},{8,0},{12,4},{1,9},{5,13},{9,1},{13,5},{2,10},{6,14},... | collective-permute-start | bytes 1622024 | tf_op jit(solution)/shard_map/ppermute | solution.py:179
  214.1 33.7 %collective-permute-start.19 = (bf16[3,88,1024]{2,1,0:T(8,128)(2,1)}, bf16[3,88,1024]{2,1,0:T(8,128)(2,1)S(1)}, u32[]{:S(2)}, u32[]{:S(2)}) collective-permute-start(bf16[3,88,1024]{2,1,0:T(8,128)(2,1)} %get-tuple-element.124), channel_id=1, source_target_pairs={{0,12},{4,8},{8,4},{12,0},{1,13},{5,9},{9,5},{13,1},{2,14},{6,10},... | collective-permute-start | bytes 1622024 | tf_op jit(solution)/shard_map/ppermute | solution.py:179
  250.5 47.8 %collective-permute-start.39 = (bf16[3,88,1024]{2,1,0:T(8,128)(2,1)S(1)}, bf16[3,88,1024]{2,1,0:T(8,128)(2,1)}, u32[]{:S(2)}, u32[]{:S(2)}) collective-permute-start(bf16[3,88,1024]{2,1,0:T(8,128)(2,1)S(1)} %add_convert_fusion.2.refs_1_.rest_0_), channel_id=1, source_target_pairs={{0,2},{1,3},{2,0},{3,1},{4,6},{5,7},{6,4},{7,5},{8,10},{9,11},{10,... | collective-permute-start | bytes 1622024 | tf_op jit(solution)/shard_map/ppermute | solution.py:179
  251.3 35.0 %collective-permute-start.16 = (bf16[512,1024]{1,0:T(8,128)(2,1)}, bf16[512,1024]{1,0:T(8,128)(2,1)S(1)}, u32[]{:S(2)}, u32[]{:S(2)}) collective-permute-start(bf16[512,1024]{1,0:T(8,128)(2,1)} %after.33), channel_id=1, source_target_pairs={{0,1},{1,0},{2,3},{3,2},{4,5},{5,4},{6,7},{7,6},{8,9},{9,8},{10,11... | collective-permute-start | bytes 3145736 | tf_op jit(solution)/shard_map/ppermute | solution.py:179
  251.3 43.2 %collective-permute-start.22 = (bf16[392,1024]{1,0:T(8,128)(2,1)}, bf16[392,1024]{1,0:T(8,128)(2,1)}, u32[]{:S(2)}, u32[]{:S(2)}) collective-permute-start(bf16[392,1024]{1,0:T(8,128)(2,1)} %after.37.rest_1_), channel_id=1, source_target_pairs={{0,4},{4,0},{8,12},{12,8},{1,5},{5,1},{9,13},{13,9},{2,6},{6,2},{1... | collective-permute-start | bytes 2408456 | tf_op jit(solution)/shard_map/ppermute | solution.py:179
  253.3 41.2 %collective-permute-start.23 = (bf16[392,1024]{1,0:T(8,128)(2,1)}, bf16[392,1024]{1,0:T(8,128)(2,1)S(1)}, u32[]{:S(2)}, u32[]{:S(2)}) collective-permute-start(bf16[392,1024]{1,0:T(8,128)(2,1)} %after.38.rest_2_), channel_id=1, source_target_pairs={{0,8},{4,12},{8,0},{12,4},{1,9},{5,13},{9,1},{13,5},{2,10},{6,14},... | collective-permute-start | bytes 2408456 | tf_op jit(solution)/shard_map/ppermute | solution.py:179
  254.8 36.4 %collective-permute-start.20 = (bf16[392,1024]{1,0:T(8,128)(2,1)S(1)}, bf16[392,1024]{1,0:T(8,128)(2,1)S(1)}, u32[]{:S(2)}, u32[]{:S(2)}) collective-permute-start(bf16[392,1024]{1,0:T(8,128)(2,1)S(1)} %copy-done.38), channel_id=1, source_target_pairs={{0,12},{4,8},{8,4},{12,0},{1,13},{5,9},{9,5},{13,1},{2,14},{6,10},... | collective-permute-start | bytes 2408456 | tf_op jit(solution)/shard_map/ppermute | solution.py:179
  292.1 8.9 %collective-permute-start.21 = (bf16[512,768]{1,0:T(8,128)(2,1)}, bf16[512,768]{1,0:T(8,128)(2,1)}, u32[]{:S(2)}, u32[]{:S(2)}) collective-permute-start(bf16[512,768]{1,0:T(8,128)(2,1)} %after.41), channel_id=1, source_target_pairs={{0,16},{16,0},{1,17},{17,1},{2,18},{18,2},{3,19},{19,3},{4,20},{20... | collective-permute-start | bytes 2359304 | tf_op jit(solution)/shard_map/ppermute | solution.py:179
  293.1 24.3 %collective-permute-start.28 = (bf16[256,1024]{1,0:T(8,128)(2,1)S(1)}, bf16[256,1024]{1,0:T(8,128)(2,1)}, u32[]{:S(2)}, u32[]{:S(2)}) collective-permute-start(bf16[256,1024]{1,0:T(8,128)(2,1)S(1)} %copy-done.16), channel_id=1, source_target_pairs={{0,4},{4,0},{8,12},{12,8},{1,5},{5,1},{9,13},{13,9},{2,6},{6,2},{1... | collective-permute-start | bytes 1572872 | tf_op jit(solution)/shard_map/ppermute | solution.py:179
  296.8 32.7 %collective-permute-start.27 = (bf16[256,1024]{1,0:T(8,128)(2,1)}, bf16[256,1024]{1,0:T(8,128)(2,1)}, u32[]{:S(2)}, u32[]{:S(2)}) collective-permute-start(bf16[256,1024]{1,0:T(8,128)(2,1)} %get-tuple-element.132), channel_id=1, source_target_pairs={{0,8},{4,12},{8,0},{12,4},{1,9},{5,13},{9,1},{13,5},{2,10},{6,14},... | collective-permute-start | bytes 1572872 | tf_op jit(solution)/shard_map/ppermute | solution.py:179
  315.0 8.5 %collective-permute-start.40 = (bf16[128,1024]{1,0:T(8,128)(2,1)S(1)}, bf16[128,1024]{1,0:T(8,128)(2,1)S(1)}, u32[]{:S(2)}, u32[]{:S(2)}) collective-permute-start(bf16[128,1024]{1,0:T(8,128)(2,1)S(1)} %slice.225.refs_0_), channel_id=1, source_target_pairs={{0,4},{4,0},{8,12},{12,8},{1,5},{5,1},{9,13},{13,9},{2,6},{6,2},{1... | collective-permute-start | bytes 786440 | tf_op jit(solution)/shard_map/ppermute | solution.py:179
  315.6 13.0 %collective-permute-start.41 = (bf16[136,1024]{1,0:T(8,128)(2,1)S(1)}, bf16[136,1024]{1,0:T(8,128)(2,1)S(1)}, u32[]{:S(2)}, u32[]{:S(2)}) collective-permute-start(bf16[136,1024]{1,0:T(8,128)(2,1)S(1)} %slice.226.refs_1_), channel_id=1, source_target_pairs={{0,8},{4,12},{8,0},{12,4},{1,9},{5,13},{9,1},{13,5},{2,10},{6,14},... | collective-permute-start | bytes 835592 | tf_op jit(solution)/shard_map/ppermute | solution.py:179
  316.4 15.5 %collective-permute-start.24 = (bf16[128,1024]{1,0:T(8,128)(2,1)S(1)}, bf16[128,1024]{1,0:T(8,128)(2,1)S(1)}, u32[]{:S(2)}, u32[]{:S(2)}) collective-permute-start(bf16[128,1024]{1,0:T(8,128)(2,1)S(1)} %get-tuple-element.164), channel_id=1, source_target_pairs={{0,1},{1,0},{2,3},{3,2},{4,5},{5,4},{6,7},{7,6},{8,9},{9,8},{10,11... | collective-permute-start | bytes 786440 | tf_op jit(solution)/shard_map/ppermute | solution.py:179
  317.4 22.4 %collective-permute-start.25 = (bf16[128,1024]{1,0:T(8,128)(2,1)S(1)}, bf16[128,1024]{1,0:T(8,128)(2,1)S(1)}, u32[]{:S(2)}, u32[]{:S(2)}) collective-permute-start(bf16[128,1024]{1,0:T(8,128)(2,1)S(1)} %get-tuple-element.165), channel_id=1, source_target_pairs={{0,2},{1,3},{2,0},{3,1},{4,6},{5,7},{6,4},{7,5},{8,10},{9,11},{10,... | collective-permute-start | bytes 786440 | tf_op jit(solution)/shard_map/ppermute | solution.py:179
  323.6 16.2 %collective-permute-start.26 = (bf16[128,1024]{1,0:T(8,128)(2,1)S(1)}, bf16[128,1024]{1,0:T(8,128)(2,1)S(1)}, u32[]{:S(2)}, u32[]{:S(2)}) collective-permute-start(bf16[128,1024]{1,0:T(8,128)(2,1)S(1)} %get-tuple-element.166), channel_id=1, source_target_pairs={{0,3},{1,2},{2,1},{3,0},{4,7},{5,6},{6,5},{7,4},{8,11},{9,10},{10,... | collective-permute-start | bytes 786440 | tf_op jit(solution)/shard_map/ppermute | solution.py:179
  328.7 25.8 %collective-permute-start.43 = (bf16[256,1024]{1,0:T(8,128)(2,1)}, bf16[256,1024]{1,0:T(8,128)(2,1)}, u32[]{:S(2)}, u32[]{:S(2)}) collective-permute-start(bf16[256,1024]{1,0:T(8,128)(2,1)} %pad_maximum_fusion.9), channel_id=1, source_target_pairs={{0,8},{4,12},{8,0},{12,4},{1,9},{5,13},{9,1},{13,5},{2,10},{6,14},... | collective-permute-start | bytes 1572872 | tf_op jit(solution)/shard_map/ppermute | solution.py:179
  329.5 26.3 %collective-permute-start.42 = (bf16[272,1024]{1,0:T(8,128)(2,1)S(1)}, bf16[272,1024]{1,0:T(8,128)(2,1)}, u32[]{:S(2)}, u32[]{:S(2)}) collective-permute-start(bf16[272,1024]{1,0:T(8,128)(2,1)S(1)} %pad_maximum_fusion.8), channel_id=1, source_target_pairs={{0,4},{4,0},{8,12},{12,8},{1,5},{5,1},{9,13},{13,9},{2,6},{6,2},{1... | collective-permute-start | bytes 1671176 | tf_op jit(solution)/shard_map/ppermute | solution.py:179
  340.7 11.4 %collective-permute-start.31 = (bf16[128,1024]{1,0:T(8,128)(2,1)}, bf16[128,1024]{1,0:T(8,128)(2,1)S(1)}, u32[]{:S(2)}, u32[]{:S(2)}) collective-permute-start(bf16[128,1024]{1,0:T(8,128)(2,1)} %after.44.refs_1_.refs_0_), channel_id=1, source_target_pairs={{0,1},{1,0},{2,3},{3,2},{4,5},{5,4},{6,7},{7,6},{8,9},{9,8},{10,11... | collective-permute-start | bytes 786440 | tf_op jit(solution)/shard_map/ppermute | solution.py:179
  346.2 31.1 %collective-permute-start.30 = (bf16[512,1024]{1,0:T(8,128)(2,1)}, bf16[512,1024]{1,0:T(8,128)(2,1)}, u32[]{:S(2)}, u32[]{:S(2)}) collective-permute-start(bf16[512,1024]{1,0:T(8,128)(2,1)} %fusion.13.refs_2_), channel_id=1, source_target_pairs={{0,8},{4,12},{8,0},{12,4},{1,9},{5,13},{9,1},{13,5},{2,10},{6,14},... | collective-permute-start | bytes 3145736 | tf_op jit(solution)/shard_map/ppermute | solution.py:179
  347.6 29.8 %collective-permute-start.29 = (bf16[512,1024]{1,0:T(8,128)(2,1)}, bf16[512,1024]{1,0:T(8,128)(2,1)}, u32[]{:S(2)}, u32[]{:S(2)}) collective-permute-start(bf16[512,1024]{1,0:T(8,128)(2,1)} %copy-done.21), channel_id=1, source_target_pairs={{0,4},{4,0},{8,12},{12,8},{1,5},{5,1},{9,13},{13,9},{2,6},{6,2},{1... | collective-permute-start | bytes 3145736 | tf_op jit(solution)/shard_map/ppermute | solution.py:179
  352.8 7.8 %collective-permute-start.32 = (f32[3,1024]{1,0:T(4,128)}, f32[3,1024]{1,0:T(4,128)S(1)}, u32[]{:S(2)}, u32[]{:S(2)}) collective-permute-start(f32[3,1024]{1,0:T(4,128)} %after.46), channel_id=1, source_target_pairs={{0,1},{1,0},{2,3},{3,2},{4,5},{5,4},{6,7},{7,6},{8,9},{9,8},{10,11... | collective-permute-start | bytes 36872 | tf_op jit(solution)/shard_map/ppermute | solution.py:179
  354.5 6.1 %collective-permute-start.33 = (f32[3,1024]{1,0:T(4,128)}, f32[3,1024]{1,0:T(4,128)S(1)}, u32[]{:S(2)}, u32[]{:S(2)}) collective-permute-start(f32[3,1024]{1,0:T(4,128)} %after.46), channel_id=1, source_target_pairs={{0,2},{1,3},{2,0},{3,1},{4,6},{5,7},{6,4},{7,5},{8,10},{9,11},{10,... | collective-permute-start | bytes 36872 | tf_op jit(solution)/shard_map/ppermute | solution.py:179
  355.8 5.7 %collective-permute-start.34 = (f32[3,1024]{1,0:T(4,128)}, f32[3,1024]{1,0:T(4,128)S(1)}, u32[]{:S(2)}, u32[]{:S(2)}) collective-permute-start(f32[3,1024]{1,0:T(4,128)} %after.46), channel_id=1, source_target_pairs={{0,3},{1,2},{2,1},{3,0},{4,7},{5,6},{6,5},{7,4},{8,11},{9,10},{10,... | collective-permute-start | bytes 36872 | tf_op jit(solution)/shard_map/ppermute | solution.py:179
  360.6 23.0 %collective-permute-start.44 = (bf16[3,352,1024]{2,1,0:T(8,128)(2,1)}, bf16[3,352,1024]{2,1,0:T(8,128)(2,1)}, u32[]{:S(2)}, u32[]{:S(2)}) collective-permute-start(bf16[3,352,1024]{2,1,0:T(8,128)(2,1)} %after.48), channel_id=1, source_target_pairs={{0,16},{16,0},{1,17},{17,1},{2,18},{18,2},{3,19},{19,3},{4,20},{20... | collective-permute-start | bytes 6488072 | tf_op jit(solution)/shard_map/ppermute | solution.py:179
  364.9 7.1 %collective-permute-start.36 = (f32[3,1024]{1,0:T(4,128)S(1)}, f32[3,1024]{1,0:T(4,128)S(1)}, u32[]{:S(2)}, u32[]{:S(2)}) collective-permute-start(f32[3,1024]{1,0:T(4,128)S(1)} %add.240), channel_id=1, source_target_pairs={{0,4},{4,0},{8,12},{12,8},{1,5},{5,1},{9,13},{13,9},{2,6},{6,2},{1... | collective-permute-start | bytes 36872 | tf_op jit(solution)/shard_map/ppermute | solution.py:179
  369.4 3.7 collective-permute-start.37
  372.1 4.6 %collective-permute-start.38 = (f32[3,1024]{1,0:T(4,128)S(1)}, f32[3,1024]{1,0:T(4,128)S(1)}, u32[]{:S(2)}, u32[]{:S(2)}) collective-permute-start(f32[3,1024]{1,0:T(4,128)S(1)} %add.240), channel_id=1, source_target_pairs={{0,12},{4,8},{8,4},{12,0},{1,13},{5,9},{9,5},{13,1},{2,14},{6,10},... | collective-permute-start | bytes 36872 | tf_op jit(solution)/shard_map/ppermute | solution.py:179
  373.1 25.0 %collective-permute-start.45 = (bf16[256,1024]{1,0:T(8,128)(2,1)S(1)}, bf16[256,1024]{1,0:T(8,128)(2,1)S(1)}, u32[]{:S(2)}, u32[]{:S(2)}) collective-permute-start(bf16[256,1024]{1,0:T(8,128)(2,1)S(1)} %pad_maximum_fusion.10), channel_id=1, source_target_pairs={{0,2},{1,3},{2,0},{3,1},{4,6},{5,7},{6,4},{7,5},{8,10},{9,11},{10,... | collective-permute-start | bytes 1572872 | tf_op jit(solution)/shard_map/ppermute | solution.py:179
  (61 other events, 348.8 us)

commit v3 on v2

--- a/solution.py
+++ b/solution.py
@@ -413,11 +413,7 @@
     f = pl.program_id(0)
     steps = pl.num_programs(0)
 
-    @pl.when(f == 0)
-    def _():
-        sum_ref[...] = jnp.zeros_like(sum_ref)
-
-    def work(gate_w, up_w, down_w):
+    def work(begin, gate_w, up_w, down_w):
         x, g = x_ref[...], g_ref[...]
         gate, up = dot(gate_w[...], x, NT), dot(up_w[...], x, NT)
         hidden_grad = dot(down_w[...], g, NT)
@@ -427,13 +423,14 @@
         gate_grad = (hidden_grad * up * (sigma + gate_sigma * (1.0 - sigma))).astype(bf16)
         up_grad = (hidden_grad * gate_sigma).astype(bf16)
         act_ref[0, 0], act_ref[0, 1], act_ref[0, 2] = gate_grad, up_grad, hidden
-        sum_ref[...] += dot(gate_grad, gate_w[...], TN) + dot(up_grad, up_w[...], TN)
-
-    for k, condition in enumerate((f < 2, f == 2, f == 3)):
+        terms = dot(gate_grad, gate_w[...], TN) + dot(up_grad, up_w[...], TN)
+        sum_ref[...] = terms if begin else sum_ref[...] + terms
+
+    for number, condition in enumerate((f == 0, f == 1, f == 2, f == 3)):
 
         @pl.when(condition)
-        def _(k=k):
-            work(*sources[k])
+        def _(number=number):
+            work(number == 0, *sources[max(number - 1, 0)])
 
     @pl.when(f == steps - 1)
     def _():

time: 411 us -> 408 us (level)
  transfers between devices with their start and end apart: 50 -> 50, of which waited for: 15 -> 14; matrix products, arithmetic and copies ran while one was open for 18% -> 18% of each run, Pallas kernels for 39% -> 40%
where the time goes in v3:
time: 408 us; the launch traced here: 402 us
  Pallas kernels  180 us (44%)
  starting transfers between devices  68.4 us (17%)
  waiting for transfers between devices  55.6 us (14%)
  other arithmetic  47.8 us (12%)
  local copies, waits for them, and re-layouts  34.6 us (8%)
  matrix products  14.2 us (3%)
    ppermute x47, starting transfers between devices, swap(): lax.ppermute(x, axis, [(i, i ^ mask) for i in range(lax.axis_size(axis))])  56.9 us
    ppermute x47, waiting for transfers between devices, swap(): lax.ppermute(x, axis, [(i, i ^ mask) for i in range(lax.axis_size(axis))])  45.1 us
    pallas_call x2, Pallas kernels, attend_backward(): pl.pallas_call(functools.partial(backward_kernel, block), grid_spec=spec,...  43 us
    pallas_call x2, Pallas kernels, feed(): pl.pallas_call(feed_kernel, grid=(4,), in_specs=[spec_whole(x), spec_whol...  32.4 us
    pallas_call x2, Pallas kernels, attend_forward2(): pl.pallas_call(functools.partial(fwd2_kernel, block), grid_spec=spec, out...  23.8 us
    unnamed x123, local copies, waits for them, and re-layouts  19.6 us
    pallas_call x1, Pallas kernels, others(): pl.pallas_call(others_kernel, grid_spec=spec, out_shape=[half, half] + [j...  18.9 us
    pallas_call x2, Pallas kernels, shard_grads(): pl.pallas_call(kernel, grid_spec=spec, out_shape=out_shape, compiler_para...  17.4 us
  transfers between devices with their start and end apart: 50, of which 14 were waited for; matrix products, arithmetic and copies ran while one was open for 18% of the time, Pallas kernels for 40%

profile of v3, /device:TPU:0, one launch (start us, length us, event | category | flops | bytes accessed | tf_op | source)
XLA Modules:
  0.0 402.0 jit_solution(4818953910020798835)
XLA Ops:
  0.7 3.0 collective-permute-start
  5.2 2.6 pad_maximum_fusion.refs_0_.refs_1_.refs_2_
  7.9 2.1 copy-done.13
  10.0 2.7 collective-permute-start.4
  19.1 5.5 %fusion.9 = (f32[2048,128]{1,0:T(8,128)}, f32[2048,128]{1,0:T(8,128)}) fusion(f32[128]{0:T(128)S(1)} %get-tuple-element.175, f32[128]{0:T(128)S(1)} %get-tuple-element.176, f32[2048]{0:T(1024)S(1)} %bitcast.90), kind=kLoop, calls=%fused_computation.45 | loop fusion | flops 524288 | bytes 2106368 | tf_op jit(solution)/shard_map/mul | solution.py:838
  24.6 2.6 collective-permute-done.refs_2_
  32.7 10.9 %project.2 = (bf16[2048,1024]{1,0:T(8,128)(2,1)}, bf16[2048,256]{1,0:T(8,128)(2,1)}, bf16[2048,256]{1,0:T(8,128)(2,1)}, bf16[2048,256]{1,0:T(8,128)(2,1)}, f32[8,128]{1,0:T(8,128)}) custom-call(s32[1]{0:T(128)} %bitcast.2.rank_ref, bf16[512,1024]{1,0:T(8,128)(2,1)} %bitcast.77, bf16[512,1024]{1,0:T(8,128)(2,1)} %collective-permute-done.2.refs_1_, ...), custom_call_target="tpu_custom_call" | custom-call | flops 14849999872 | bytes 1350000 | tf_op jit(solution)/shard_map/project/pallas_call | solution.py:361
  49.4 4.2 %project.3 = (bf16[2048,1024]{1,0:T(8,128)(2,1)}, bf16[2048,256]{1,0:T(8,128)(2,1)}, bf16[2048,256]{1,0:T(8,128)(2,1)}, bf16[2048,256]{1,0:T(8,128)(2,1)}, f32[8,128]{1,0:T(8,128)}) custom-call(s32[1]{0:T(128)} %bitcast.2.rank_ref, bf16[256,1024]{1,0:T(8,128)(2,1)} %copy-done.42, ...), custom_call_target="tpu_custom_call", output_to_operand_aliasing={{0}: (8, {}), {1}: (9, {}), {2}: (10, {}), {3}: (11, {})} | custom-call | flops 4950000128 | bytes 450000 | tf_op jit(solution)/shard_map/project/pallas_call | solution.py:361
  53.6 12.0 %attend_forward.2 = (bf16[2048,128]{1,0:T(8,128)(2,1)}, f32[1,8,2048]{2,1,0:T(8,128)}) custom-call(s32[2]{0:T(128)} %slice.174.firsts, s32[2]{0:T(128)} %slice.175.lasts, bf16[2048,256]{1,0:T(8,128)(2,1)} %get-tuple-element.100.q_ref, bf16[2048,256]{1,0:T(8,128)(2,1)} %get-tuple-element.101.k_ref, bf16[2048,256]{1,0:T(8,128)(2,1)} %get-tuple-element.102.v_ref, ...), custom_call_target="tpu_custom_call" | custom-call | flops 15569256448 | bytes 2097152 | tf_op jit(solution)/shard_map/attend_forward/pallas_call | solution.py:89
  65.6 3.7 all-to-all-start
  69.3 11.8 %attend_forward.3 = (bf16[2048,128]{1,0:T(8,128)(2,1)}, f32[1,8,2048]{2,1,0:T(8,128)}) custom-call(s32[2]{0:T(128)} %slice.174.firsts, s32[2]{0:T(128)} %slice.175.lasts, bf16[2048,256]{1,0:T(8,128)(2,1)} %get-tuple-element.100.q_ref, bf16[2048,256]{1,0:T(8,128)(2,1)} %get-tuple-element.101.k_ref, bf16[2048,256]{1,0:T(8,128)(2,1)} %get-tuple-element.102.v_ref, ...), custom_call_target="tpu_custom_call" | custom-call | flops 15569256448 | bytes 2097152 | tf_op jit(solution)/shard_map/attend_forward/pallas_call | solution.py:89
  81.1 6.1 %all-to-all-done.refs_4_ = bf16[4,512,128]{2,1,0:T(8,128)(2,1)S(1)} async-done(((bf16[4,512,128]{2,1,0:T(8,128)(2,1)}), bf16[4,512,128]{2,1,0:T(8,128)(2,1)S(1)}, u32[]{:S(2)}, u32[]{:S(2)}) %all-to-all-start) | async-done | bytes 524320 | tf_op jit(solution)/shard_map/all_to_all | solution.py:855
  88.5 4.0 assemble.1
  95.3 3.9 all-to-all-start.1
  101.0 2.0 fusion.26
  103.0 4.4 %all-to-all-done.1 = bf16[4,512,128]{2,1,0:T(8,128)(2,1)S(1)} async-done(((bf16[4,512,128]{2,1,0:T(8,128)(2,1)}), bf16[4,512,128]{2,1,0:T(8,128)(2,1)S(1)}, u32[]{:S(2)}, u32[]{:S(2)}) %all-to-all-start.1) | async-done | bytes 524320 | tf_op jit(solution)/shard_map/all_to_all | solution.py:855
  107.4 2.7 multiply_reduce_fusion
  111.6 16.3 %feed.2 = (bf16[4,3,352,512]{3,2,1,0:T(8,128)(2,1)}, f32[512,1024]{1,0:T(8,128)}) custom-call(bf16[512,1024]{1,0:T(8,128)(2,1)} %copy-done.35, bf16[512,1024]{1,0:T(8,128)(2,1)} %bitcast.17.g_ref.grad_ref.refs_4_, bf16[2112,1024]{1,0:T(8,128)(2,1)} %copy-done.13, bf16[2112,1024]{1,0:T(8,128)(2,1)} %copy-done.13, bf16[2112,1024]{1,0:T(8,128)(2,1)} %copy-done.13, ...), custom_call_target="tpu_custom_call" | custom-call | flops 17600000000 | bytes 1600000 | tf_op jit(solution)/shard_map/feed/pallas_call | solution.py:444
  127.9 13.0 %collective-permute-done.10.x_ref.xn_ref.refs_3_ = bf16[512,1024]{1,0:T(8,128)(2,1)S(1)} collective-permute-done((bf16[512,1024]{1,0:T(8,128)(2,1)S(1)}, bf16[512,1024]{1,0:T(8,128)(2,1)S(1)}, u32[]{:S(2)}, u32[]{:S(2)}) %collective-permute-start.10) | collective-permute-done | bytes 1048608 | tf_op jit(solution)/shard_map/ppermute | solution.py:179
  141.8 16.1 %feed.3 = (bf16[4,3,352,512]{3,2,1,0:T(8,128)(2,1)}, bf16[512,1024]{1,0:T(8,128)(2,1)}) custom-call(bf16[512,1024]{1,0:T(8,128)(2,1)} %copy-done.56, bf16[512,1024]{1,0:T(8,128)(2,1)} %collective-permute-done.11.g_ref.gn_ref.refs_5_, bf16[2112,1024]{1,0:T(8,128)(2,1)} %copy-done.13, bf16[2112,1024]{1,0:T(8,128)(2,1)} %copy-done.13, ...), custom_call_target="tpu_custom_call" | custom-call | flops 17600000000 | bytes 1600000 | tf_op jit(solution)/shard_map/feed/pallas_call | solution.py:444
  159.6 18.9 %others.1 = (bf16[1056,1024]{1,0:T(8,128)(2,1)}, bf16[1056,1024]{1,0:T(8,128)(2,1)}, f32[512,1024]{1,0:T(8,128)}, bf16[512,1024]{1,0:T(8,128)(2,1)}) custom-call(s32[2]{0:T(128)} %pad_add_fusion.scalars, bf16[4,3,352,512]{3,2,1,0:T(8,128)(2,1)} %get-tuple-element.107.act_ref.refs_0_, bf16[4,3,352,512]{3,2,1,0:T(8,128)(2,1)} %get-tuple-element.109.near_ref.refs_1_, ...), custom_call_target="tpu_custom_call" | custom-call | flops 20899999744 | bytes 1900000 | tf_op jit(solution)/shard_map/others/pallas_call | solution.py:626
  178.5 4.2 %collective-permute-done.12.refs_0_ = bf16[512,1024]{1,0:T(8,128)(2,1)} collective-permute-done((bf16[512,1024]{1,0:T(8,128)(2,1)}, bf16[512,1024]{1,0:T(8,128)(2,1)}, u32[]{:S(2)}, u32[]{:S(2)}) %collective-permute-start.12) | collective-permute-done | bytes 1048608 | tf_op jit(solution)/shard_map/ppermute | solution.py:179
  185.2 8.2 %state_back.1 = (f32[512,1024]{1,0:T(8,128)}, bf16[512,1024]{1,0:T(8,128)(2,1)}, bf16[4,512,256]{2,1,0:T(8,128)(2,1)}, f32[1,1024]{1,0:T(1,128)}) custom-call(bf16[512,1024]{1,0:T(8,128)(2,1)} %after.26.refs_1_.back_ref, f32[512,1024]{1,0:T(8,128)} %get-tuple-element.108.refs_9_.terms_ref, f32[512,1024]{1,0:T(8,128)} %copy-done.3, ...), custom_call_target="tpu_custom_call" | custom-call | flops 6600000000 | bytes 600000 | tf_op jit(solution)/shard_map/state_back/pallas_call | solution.py:762
  193.4 3.9 all-to-all-start.2
  197.3 2.0 convolution_convert_fusion.2
  202.5 7.9 %far_sum.1 = (bf16[3,88,1024]{2,1,0:T(8,128)(2,1)}, bf16[3,88,1024]{2,1,0:T(8,128)(2,1)}, bf16[3,88,1024]{2,1,0:T(8,128)(2,1)}, bf16[3,88,1024]{2,1,0:T(8,128)(2,1)}) custom-call(s32[2]{0:T(128)} %pad_add_fusion.scalars, bf16[4,3,352,512]{3,2,1,0:T(8,128)(2,1)} %get-tuple-element.107.act_ref.refs_0_, ...), custom_call_target="tpu_custom_call" | custom-call | flops 8800000000 | bytes 800000 | tf_op jit(solution)/shard_map/far_sum/pallas_call | solution.py:560
  214.9 21.4 %attend_backward.2 = (bf16[2048,768]{1,0:T(8,128)(2,1)}, bf16[2048,256]{1,0:T(8,128)(2,1)}) custom-call(s32[4]{0:T(128)} %get-tuple-element.172.full_end, s32[4]{0:T(128)} %get-tuple-element.171.some_end, bf16[2048,256]{1,0:T(8,128)(2,1)} %get-tuple-element.100.q_ref, bf16[2048,256]{1,0:T(8,128)(2,1)} %get-tuple-element.101.k_ref, ...), custom_call_target="tpu_custom_call" | custom-call | flops 27917287424 | bytes 5767168 | tf_op jit(solution)/shard_map/attend_backward/pallas_call | solution.py:165
  236.4 9.5 %own_sum.1 = (bf16[392,1024]{1,0:T(8,128)(2,1)}, bf16[392,1024]{1,0:T(8,128)(2,1)}, bf16[392,1024]{1,0:T(8,128)(2,1)}, bf16[392,1024]{1,0:T(8,128)(2,1)}) custom-call(s32[2]{0:T(128)} %pad_add_fusion.scalars, bf16[4,3,352,512]{3,2,1,0:T(8,128)(2,1)} %get-tuple-element.107.act_ref.refs_0_, bf16[4,3,352,512]{3,2,1,0:T(8,128)(2,1)} %get-tuple-element.109.near_ref.refs_1_, ...), custom_call_target="tpu_custom_call" | custom-call | flops 8800000000 | bytes 800000 | tf_op jit(solution)/shard_map/own_sum/pallas_call | solution.py:560
  251.1 2.0 collective-permute-start.22
  255.1 21.6 %attend_backward.3 = (bf16[2048,768]{1,0:T(8,128)(2,1)}, bf16[2048,256]{1,0:T(8,128)(2,1)}) custom-call(s32[4]{0:T(128)} %get-tuple-element.172.full_end, s32[4]{0:T(128)} %get-tuple-element.171.some_end, bf16[2048,256]{1,0:T(8,128)(2,1)} %get-tuple-element.100.q_ref, ...), custom_call_target="tpu_custom_call", output_to_operand_aliasing={{0}: (15, {}), {1}: (16, {})} | custom-call | flops 27917287424 | bytes 5767168 | tf_op jit(solution)/shard_map/attend_backward/pallas_call | solution.py:165
  276.7 6.7 %convolution_convert_fusion.refs_4_ = bf16[1024,768]{1,0:T(8,128)(2,1)S(1)} fusion(bf16[2048,1024]{1,0:T(8,128)(2,1)} %get-tuple-element.120, bf16[2048,768]{1,0:T(8,128)(2,1)} %get-tuple-element.129.refs_3_.refs_4_), kind=kOutput, calls=%fused_computation.31 | convolution fusion | flops 3222011904 | bytes 8912896 | tf_op jit(solution)/shard_map/dot_general | solution.py:18
  285.8 3.9 unproject.2
  296.9 2.7 fusion.8.refs_0_
  302.0 9.5 %unproject.3 = (bf16[512,1024]{1,0:T(8,128)(2,1)}, bf16[512,1024]{1,0:T(8,128)(2,1)}, bf16[512,1024]{1,0:T(8,128)(2,1)}, f32[1,1024]{1,0:T(1,128)}) custom-call(s32[1]{0:T(128)} %bitcast.2.rank_ref, bf16[512,1024]{1,0:T(8,128)(2,1)} %bitcast.78, bf16[512,1024]{1,0:T(8,128)(2,1)} %collective-permute-done.2.refs_1_, ...), custom_call_target="tpu_custom_call" | custom-call | flops 11550000128 | bytes 1050000 | tf_op jit(solution)/shard_map/unproject/pallas_call | solution.py:727
  315.6 4.2 %collective-permute-start.25 = (bf16[128,1024]{1,0:T(8,128)(2,1)S(1)}, bf16[128,1024]{1,0:T(8,128)(2,1)S(1)}, u32[]{:S(2)}, u32[]{:S(2)}) collective-permute-start(bf16[128,1024]{1,0:T(8,128)(2,1)S(1)} %get-tuple-element.165), channel_id=1, source_target_pairs={{0,2},{1,3},{2,0},{3,1},{4,6},{5,7},{6,4},{7,5},{8,10},{9,11},{10,... | collective-permute-start | bytes 786440 | tf_op jit(solution)/shard_map/ppermute | solution.py:179
  319.7 2.2 fusion.13.refs_2_
  321.9 2.9 collective-permute-start.26
  329.0 9.2 %collective-permute-done.25 = bf16[128,1024]{1,0:T(8,128)(2,1)S(1)} collective-permute-done((bf16[128,1024]{1,0:T(8,128)(2,1)S(1)}, bf16[128,1024]{1,0:T(8,128)(2,1)S(1)}, u32[]{:S(2)}, u32[]{:S(2)}) %collective-permute-start.25) | collective-permute-done | bytes 262176 | tf_op jit(solution)/shard_map/ppermute | solution.py:179
  339.1 4.0 collective-permute-start.31
  348.4 2.0 collective-permute-start.32
  353.2 3.4 regroup.1
  357.8 3.1 collective-permute-done.35
  361.8 3.6 add_convert_fusion.refs_1_
  372.9 2.5 fusion
  375.5 3.7 fusion.6.refs_2_
  379.1 2.2 broadcast_select_fusion.1
  382.5 3.7 slice_bitcast_fusion
  387.3 6.5 %collective-permute-done.45 = bf16[256,1024]{1,0:T(8,128)(2,1)S(1)} collective-permute-done((bf16[256,1024]{1,0:T(8,128)(2,1)S(1)}, bf16[256,1024]{1,0:T(8,128)(2,1)S(1)}, u32[]{:S(2)}, u32[]{:S(2)}) %collective-permute-start.45) | collective-permute-done | bytes 524320 | tf_op jit(solution)/shard_map/ppermute | solution.py:179
  (296 shorter events, 95.1 us)
Async XLA Ops:
  0.7 26.5 %collective-permute-start = (bf16[512,1024]{1,0:T(8,128)(2,1)}, bf16[512,1024]{1,0:T(8,128)(2,1)}, u32[]{:S(2)}, u32[]{:S(2)}) collective-permute-start(bf16[512,1024]{1,0:T(8,128)(2,1)} %bitcast.75), channel_id=1, source_target_pairs={{0,8},{4,12},{8,0},{12,4},{1,9},{5,13},{9,1},{13,5},{2,10},{6,14},... | collective-permute-start | bytes 3145736 | tf_op jit(solution)/shard_map/ppermute | solution.py:179
  3.7 26.3 %collective-permute-start.2 = (bf16[512,1024]{1,0:T(8,128)(2,1)}, bf16[512,1024]{1,0:T(8,128)(2,1)}, u32[]{:S(2)}, u32[]{:S(2)}) collective-permute-start(bf16[512,1024]{1,0:T(8,128)(2,1)} %bitcast.76), channel_id=1, source_target_pairs={{0,4},{4,0},{8,12},{12,8},{1,5},{5,1},{9,13},{13,9},{2,6},{6,2},{1... | collective-permute-start | bytes 3145736 | tf_op jit(solution)/shard_map/ppermute | solution.py:179
  10.0 33.6 %collective-permute-start.4 = (bf16[3,88,1024]{2,1,0:T(8,128)(2,1)S(1)}, bf16[3,88,1024]{2,1,0:T(8,128)(2,1)S(1)}, u32[]{:S(2)}, u32[]{:S(2)}) collective-permute-start(bf16[3,88,1024]{2,1,0:T(8,128)(2,1)S(1)} %dynamic-slice_bitcast_fusion.2), channel_id=1, source_target_pairs={{0,2},{1,3},{2,0},{3,1},{4,6},{5,7},{6,4},{7,5},{8,10},{9,11},{10,... | collective-permute-start | bytes 1622024 | tf_op jit(solution)/shard_map/ppermute | solution.py:179
  28.3 15.4 %collective-permute-start.1 = (bf16[256,1024]{1,0:T(8,128)(2,1)S(1)}, bf16[256,1024]{1,0:T(8,128)(2,1)S(1)}, u32[]{:S(2)}, u32[]{:S(2)}) collective-permute-start(bf16[256,1024]{1,0:T(8,128)(2,1)S(1)} %slice.216), channel_id=1, source_target_pairs={{0,4},{4,0},{8,12},{12,8},{1,5},{5,1},{9,13},{13,9},{2,6},{6,2},{1... | collective-permute-start | bytes 1572872 | tf_op jit(solution)/shard_map/ppermute | solution.py:179
  31.1 12.6 %collective-permute-start.3 = (bf16[256,1024]{1,0:T(8,128)(2,1)S(1)}, bf16[256,1024]{1,0:T(8,128)(2,1)S(1)}, u32[]{:S(2)}, u32[]{:S(2)}) collective-permute-start(bf16[256,1024]{1,0:T(8,128)(2,1)S(1)} %slice.217), channel_id=1, source_target_pairs={{0,8},{4,12},{8,0},{12,4},{1,9},{5,13},{9,1},{13,5},{2,10},{6,14},... | collective-permute-start | bytes 1572872 | tf_op jit(solution)/shard_map/ppermute | solution.py:179
  45.9 41.4 %collective-permute-start.5 = (bf16[392,1024]{1,0:T(8,128)(2,1)S(1)}, bf16[392,1024]{1,0:T(8,128)(2,1)S(1)}, u32[]{:S(2)}, u32[]{:S(2)}) collective-permute-start(bf16[392,1024]{1,0:T(8,128)(2,1)S(1)} %pad_maximum_fusion.7.refs_0_), channel_id=1, source_target_pairs={{0,4},{4,0},{8,12},{12,8},{1,5},{5,1},{9,13},{13,9},{2,6},{6,2},{1... | collective-permute-start | bytes 2408456 | tf_op jit(solution)/shard_map/ppermute | solution.py:179
  46.5 40.8 %collective-permute-start.6 = (bf16[392,1024]{1,0:T(8,128)(2,1)S(1)}, bf16[392,1024]{1,0:T(8,128)(2,1)S(1)}, u32[]{:S(2)}, u32[]{:S(2)}) collective-permute-start(bf16[392,1024]{1,0:T(8,128)(2,1)S(1)} %pad_maximum_fusion.7.refs_0_), channel_id=1, source_target_pairs={{0,8},{4,12},{8,0},{12,4},{1,9},{5,13},{9,1},{13,5},{2,10},{6,14},... | collective-permute-start | bytes 2408456 | tf_op jit(solution)/shard_map/ppermute | solution.py:179
  47.7 39.5 %collective-permute-start.7 = (bf16[392,1024]{1,0:T(8,128)(2,1)S(1)}, bf16[392,1024]{1,0:T(8,128)(2,1)}, u32[]{:S(2)}, u32[]{:S(2)}) collective-permute-start(bf16[392,1024]{1,0:T(8,128)(2,1)S(1)} %pad_maximum_fusion.7.refs_0_), channel_id=1, source_target_pairs={{0,12},{4,8},{8,4},{12,0},{1,13},{5,9},{9,5},{13,1},{2,14},{6,10},... | collective-permute-start | bytes 2408456 | tf_op jit(solution)/shard_map/ppermute | solution.py:179
  65.6 21.6 %all-to-all-start = ((bf16[4,512,128]{2,1,0:T(8,128)(2,1)}), bf16[4,512,128]{2,1,0:T(8,128)(2,1)S(1)}, u32[]{:S(2)}, u32[]{:S(2)}) async-start(bf16[4,512,128]{2,1,0:T(8,128)(2,1)} %bitcast.88), calls=%async_computation | async-start | bytes 1048576 | tf_op jit(solution)/shard_map/all_to_all | solution.py:855
  92.6 6.6 %collective-permute-start.8 = (bf16[4,128,1024]{2,1,0:T(8,128)(2,1)}, bf16[4,128,1024]{2,1,0:T(8,128)(2,1)}, u32[]{:S(2)}, u32[]{:S(2)}) collective-permute-start(bf16[4,128,1024]{2,1,0:T(8,128)(2,1)} %get-tuple-element.105), channel_id=1, source_target_pairs={{0,16},{16,0},{1,17},{17,1},{2,18},{18,2},{3,19},{19,3},{4,20},{20... | collective-permute-start | bytes 3145736 | tf_op jit(solution)/shard_map/ppermute | solution.py:179
  92.6 18.3 %collective-permute-start.9 = (bf16[1056,1024]{1,0:T(8,128)(2,1)}, bf16[1056,1024]{1,0:T(8,128)(2,1)}, u32[]{:S(2)}, u32[]{:S(2)}) collective-permute-start(bf16[1056,1024]{1,0:T(8,128)(2,1)} %bitcast.97), channel_id=1, source_target_pairs={{0,16},{16,0},{1,17},{17,1},{2,18},{18,2},{3,19},{19,3},{4,20},{20... | collective-permute-start | bytes 6488072 | tf_op jit(solution)/shard_map/ppermute | solution.py:179
  93.1 34.8 %collective-permute-start.11 = (bf16[512,1024]{1,0:T(8,128)(2,1)}, bf16[512,1024]{1,0:T(8,128)(2,1)}, u32[]{:S(2)}, u32[]{:S(2)}) collective-permute-start(bf16[512,1024]{1,0:T(8,128)(2,1)} %bitcast.17.g_ref.grad_ref.refs_4_), channel_id=1, source_target_pairs={{0,1},{1,0},{2,3},{3,2},{4,5},{5,4},{6,7},{7,6},{8,9},{9,8},{10,11... | collective-permute-start | bytes 3145736 | tf_op jit(solution)/shard_map/ppermute | solution.py:179
  95.3 12.1 %all-to-all-start.1 = ((bf16[4,512,128]{2,1,0:T(8,128)(2,1)}), bf16[4,512,128]{2,1,0:T(8,128)(2,1)S(1)}, u32[]{:S(2)}, u32[]{:S(2)}) async-start(bf16[4,512,128]{2,1,0:T(8,128)(2,1)} %bitcast.14), calls=%async_computation.1 | async-start | bytes 1048576 | tf_op jit(solution)/shard_map/all_to_all | solution.py:855
  110.4 30.5 %collective-permute-start.10 = (bf16[512,1024]{1,0:T(8,128)(2,1)S(1)}, bf16[512,1024]{1,0:T(8,128)(2,1)S(1)}, u32[]{:S(2)}, u32[]{:S(2)}) collective-permute-start(bf16[512,1024]{1,0:T(8,128)(2,1)S(1)} %multiply_convert_fusion.x_ref.refs_2_), channel_id=1, source_target_pairs={{0,1},{1,0},{2,3},{3,2},{4,5},{5,4},{6,7},{7,6},{8,9},{9,8},{10,11... | collective-permute-start | bytes 3145736 | tf_op jit(solution)/shard_map/ppermute | solution.py:179
  158.0 24.7 %collective-permute-start.12 = (bf16[512,1024]{1,0:T(8,128)(2,1)}, bf16[512,1024]{1,0:T(8,128)(2,1)}, u32[]{:S(2)}, u32[]{:S(2)}) collective-permute-start(bf16[512,1024]{1,0:T(8,128)(2,1)} %get-tuple-element.113), channel_id=1, source_target_pairs={{0,1},{1,0},{2,3},{3,2},{4,5},{5,4},{6,7},{7,6},{8,9},{9,8},{10,11... | collective-permute-start | bytes 3145736 | tf_op jit(solution)/shard_map/ppermute | solution.py:179
  182.7 19.8 %collective-permute-start.13 = (bf16[1056,1024]{1,0:T(8,128)(2,1)}, bf16[1056,1024]{1,0:T(8,128)(2,1)}, u32[]{:S(2)}, u32[]{:S(2)}) collective-permute-start(bf16[1056,1024]{1,0:T(8,128)(2,1)} %after.27), channel_id=1, source_target_pairs={{0,16},{16,0},{1,17},{17,1},{2,18},{18,2},{3,19},{19,3},{4,20},{20... | collective-permute-start | bytes 6488072 | tf_op jit(solution)/shard_map/ppermute | solution.py:179
  193.4 20.6 %all-to-all-start.2 = ((bf16[4,512,256]{2,1,0:T(8,128)(2,1)}), bf16[4,512,256]{2,1,0:T(8,128)(2,1)S(1)}, u32[]{:S(2)}, u32[]{:S(2)}) async-start(bf16[4,512,256]{2,1,0:T(8,128)(2,1)} %get-tuple-element.114.refs_1_), calls=%async_computation.2 | async-start | bytes 2097152 | tf_op jit(solution)/shard_map/all_to_all | solution.py:892
  202.0 34.4 %collective-permute-start.15 = (bf16[4,128,1024]{2,1,0:T(8,128)(2,1)}, bf16[4,128,1024]{2,1,0:T(8,128)(2,1)}, u32[]{:S(2)}, u32[]{:S(2)}) collective-permute-start(bf16[4,128,1024]{2,1,0:T(8,128)(2,1)} %get-tuple-element.160), channel_id=1, source_target_pairs={{0,16},{16,0},{1,17},{17,1},{2,18},{18,2},{3,19},{19,3},{4,20},{20... | collective-permute-start | bytes 3145736 | tf_op jit(solution)/shard_map/ppermute | solution.py:179
  202.5 33.9 %collective-permute-start.14 = (bf16[1056,1024]{1,0:T(8,128)(2,1)}, bf16[1056,1024]{1,0:T(8,128)(2,1)}, u32[]{:S(2)}, u32[]{:S(2)}) collective-permute-start(bf16[1056,1024]{1,0:T(8,128)(2,1)} %after.28), channel_id=1, source_target_pairs={{0,16},{16,0},{1,17},{17,1},{2,18},{18,2},{3,19},{19,3},{4,20},{20... | collective-permute-start | bytes 6488072 | tf_op jit(solution)/shard_map/ppermute | solution.py:179
  210.5 35.4 %collective-permute-start.17 = (bf16[3,88,1024]{2,1,0:T(8,128)(2,1)}, bf16[3,88,1024]{2,1,0:T(8,128)(2,1)S(1)}, u32[]{:S(2)}, u32[]{:S(2)}) collective-permute-start(bf16[3,88,1024]{2,1,0:T(8,128)(2,1)} %get-tuple-element.122), channel_id=1, source_target_pairs={{0,4},{4,0},{8,12},{12,8},{1,5},{5,1},{9,13},{13,9},{2,6},{6,2},{1... | collective-permute-start | bytes 1622024 | tf_op jit(solution)/shard_map/ppermute | solution.py:179
  212.4 34.3 %collective-permute-start.18 = (bf16[3,88,1024]{2,1,0:T(8,128)(2,1)}, bf16[3,88,1024]{2,1,0:T(8,128)(2,1)S(1)}, u32[]{:S(2)}, u32[]{:S(2)}) collective-permute-start(bf16[3,88,1024]{2,1,0:T(8,128)(2,1)} %get-tuple-element.123), channel_id=1, source_target_pairs={{0,8},{4,12},{8,0},{12,4},{1,9},{5,13},{9,1},{13,5},{2,10},{6,14},... | collective-permute-start | bytes 1622024 | tf_op jit(solution)/shard_map/ppermute | solution.py:179
  213.9 33.7 %collective-permute-start.19 = (bf16[3,88,1024]{2,1,0:T(8,128)(2,1)}, bf16[3,88,1024]{2,1,0:T(8,128)(2,1)S(1)}, u32[]{:S(2)}, u32[]{:S(2)}) collective-permute-start(bf16[3,88,1024]{2,1,0:T(8,128)(2,1)} %get-tuple-element.124), channel_id=1, source_target_pairs={{0,12},{4,8},{8,4},{12,0},{1,13},{5,9},{9,5},{13,1},{2,14},{6,10},... | collective-permute-start | bytes 1622024 | tf_op jit(solution)/shard_map/ppermute | solution.py:179
  250.3 46.6 %collective-permute-start.39 = (bf16[3,88,1024]{2,1,0:T(8,128)(2,1)S(1)}, bf16[3,88,1024]{2,1,0:T(8,128)(2,1)}, u32[]{:S(2)}, u32[]{:S(2)}) collective-permute-start(bf16[3,88,1024]{2,1,0:T(8,128)(2,1)S(1)} %add_convert_fusion.2.refs_1_.rest_0_), channel_id=1, source_target_pairs={{0,2},{1,3},{2,0},{3,1},{4,6},{5,7},{6,4},{7,5},{8,10},{9,11},{10,... | collective-permute-start | bytes 1622024 | tf_op jit(solution)/shard_map/ppermute | solution.py:179
  251.1 33.3 %collective-permute-start.16 = (bf16[512,1024]{1,0:T(8,128)(2,1)}, bf16[512,1024]{1,0:T(8,128)(2,1)S(1)}, u32[]{:S(2)}, u32[]{:S(2)}) collective-permute-start(bf16[512,1024]{1,0:T(8,128)(2,1)} %after.33), channel_id=1, source_target_pairs={{0,1},{1,0},{2,3},{3,2},{4,5},{5,4},{6,7},{7,6},{8,9},{9,8},{10,11... | collective-permute-start | bytes 3145736 | tf_op jit(solution)/shard_map/ppermute | solution.py:179
  251.1 42.0 %collective-permute-start.22 = (bf16[392,1024]{1,0:T(8,128)(2,1)}, bf16[392,1024]{1,0:T(8,128)(2,1)}, u32[]{:S(2)}, u32[]{:S(2)}) collective-permute-start(bf16[392,1024]{1,0:T(8,128)(2,1)} %after.37.rest_1_), channel_id=1, source_target_pairs={{0,4},{4,0},{8,12},{12,8},{1,5},{5,1},{9,13},{13,9},{2,6},{6,2},{1... | collective-permute-start | bytes 2408456 | tf_op jit(solution)/shard_map/ppermute | solution.py:179
  253.1 40.0 %collective-permute-start.23 = (bf16[392,1024]{1,0:T(8,128)(2,1)}, bf16[392,1024]{1,0:T(8,128)(2,1)S(1)}, u32[]{:S(2)}, u32[]{:S(2)}) collective-permute-start(bf16[392,1024]{1,0:T(8,128)(2,1)} %after.38.rest_2_), channel_id=1, source_target_pairs={{0,8},{4,12},{8,0},{12,4},{1,9},{5,13},{9,1},{13,5},{2,10},{6,14},... | collective-permute-start | bytes 2408456 | tf_op jit(solution)/shard_map/ppermute | solution.py:179
  254.6 35.1 %collective-permute-start.20 = (bf16[392,1024]{1,0:T(8,128)(2,1)S(1)}, bf16[392,1024]{1,0:T(8,128)(2,1)S(1)}, u32[]{:S(2)}, u32[]{:S(2)}) collective-permute-start(bf16[392,1024]{1,0:T(8,128)(2,1)S(1)} %copy-done.38), channel_id=1, source_target_pairs={{0,12},{4,8},{8,4},{12,0},{1,13},{5,9},{9,5},{13,1},{2,14},{6,10},... | collective-permute-start | bytes 2408456 | tf_op jit(solution)/shard_map/ppermute | solution.py:179
  290.5 9.0 %collective-permute-start.21 = (bf16[512,768]{1,0:T(8,128)(2,1)}, bf16[512,768]{1,0:T(8,128)(2,1)}, u32[]{:S(2)}, u32[]{:S(2)}) collective-permute-start(bf16[512,768]{1,0:T(8,128)(2,1)} %after.41), channel_id=1, source_target_pairs={{0,16},{16,0},{1,17},{17,1},{2,18},{18,2},{3,19},{19,3},{4,20},{20... | collective-permute-start | bytes 2359304 | tf_op jit(solution)/shard_map/ppermute | solution.py:179
  291.6 24.0 %collective-permute-start.28 = (bf16[256,1024]{1,0:T(8,128)(2,1)S(1)}, bf16[256,1024]{1,0:T(8,128)(2,1)}, u32[]{:S(2)}, u32[]{:S(2)}) collective-permute-start(bf16[256,1024]{1,0:T(8,128)(2,1)S(1)} %copy-done.16), channel_id=1, source_target_pairs={{0,4},{4,0},{8,12},{12,8},{1,5},{5,1},{9,13},{13,9},{2,6},{6,2},{1... | collective-permute-start | bytes 1572872 | tf_op jit(solution)/shard_map/ppermute | solution.py:179
  295.3 31.2 %collective-permute-start.27 = (bf16[256,1024]{1,0:T(8,128)(2,1)}, bf16[256,1024]{1,0:T(8,128)(2,1)}, u32[]{:S(2)}, u32[]{:S(2)}) collective-permute-start(bf16[256,1024]{1,0:T(8,128)(2,1)} %get-tuple-element.132), channel_id=1, source_target_pairs={{0,8},{4,12},{8,0},{12,4},{1,9},{5,13},{9,1},{13,5},{2,10},{6,14},... | collective-permute-start | bytes 1572872 | tf_op jit(solution)/shard_map/ppermute | solution.py:179
  313.6 8.3 %collective-permute-start.40 = (bf16[128,1024]{1,0:T(8,128)(2,1)S(1)}, bf16[128,1024]{1,0:T(8,128)(2,1)S(1)}, u32[]{:S(2)}, u32[]{:S(2)}) collective-permute-start(bf16[128,1024]{1,0:T(8,128)(2,1)S(1)} %slice.225.refs_0_), channel_id=1, source_target_pairs={{0,4},{4,0},{8,12},{12,8},{1,5},{5,1},{9,13},{13,9},{2,6},{6,2},{1... | collective-permute-start | bytes 786440 | tf_op jit(solution)/shard_map/ppermute | solution.py:179
  314.2 11.5 %collective-permute-start.41 = (bf16[136,1024]{1,0:T(8,128)(2,1)S(1)}, bf16[136,1024]{1,0:T(8,128)(2,1)S(1)}, u32[]{:S(2)}, u32[]{:S(2)}) collective-permute-start(bf16[136,1024]{1,0:T(8,128)(2,1)S(1)} %slice.226.refs_1_), channel_id=1, source_target_pairs={{0,8},{4,12},{8,0},{12,4},{1,9},{5,13},{9,1},{13,5},{2,10},{6,14},... | collective-permute-start | bytes 835592 | tf_op jit(solution)/shard_map/ppermute | solution.py:179
  314.9 14.1 %collective-permute-start.24 = (bf16[128,1024]{1,0:T(8,128)(2,1)S(1)}, bf16[128,1024]{1,0:T(8,128)(2,1)S(1)}, u32[]{:S(2)}, u32[]{:S(2)}) collective-permute-start(bf16[128,1024]{1,0:T(8,128)(2,1)S(1)} %get-tuple-element.164), channel_id=1, source_target_pairs={{0,1},{1,0},{2,3},{3,2},{4,5},{5,4},{6,7},{7,6},{8,9},{9,8},{10,11... | collective-permute-start | bytes 786440 | tf_op jit(solution)/shard_map/ppermute | solution.py:179
  315.6 22.6 %collective-permute-start.25 = (bf16[128,1024]{1,0:T(8,128)(2,1)S(1)}, bf16[128,1024]{1,0:T(8,128)(2,1)S(1)}, u32[]{:S(2)}, u32[]{:S(2)}) collective-permute-start(bf16[128,1024]{1,0:T(8,128)(2,1)S(1)} %get-tuple-element.165), channel_id=1, source_target_pairs={{0,2},{1,3},{2,0},{3,1},{4,6},{5,7},{6,4},{7,5},{8,10},{9,11},{10,... | collective-permute-start | bytes 786440 | tf_op jit(solution)/shard_map/ppermute | solution.py:179
  321.9 16.3 %collective-permute-start.26 = (bf16[128,1024]{1,0:T(8,128)(2,1)S(1)}, bf16[128,1024]{1,0:T(8,128)(2,1)S(1)}, u32[]{:S(2)}, u32[]{:S(2)}) collective-permute-start(bf16[128,1024]{1,0:T(8,128)(2,1)S(1)} %get-tuple-element.166), channel_id=1, source_target_pairs={{0,3},{1,2},{2,1},{3,0},{4,7},{5,6},{6,5},{7,4},{8,11},{9,10},{10,... | collective-permute-start | bytes 786440 | tf_op jit(solution)/shard_map/ppermute | solution.py:179
  325.7 24.6 %collective-permute-start.43 = (bf16[256,1024]{1,0:T(8,128)(2,1)}, bf16[256,1024]{1,0:T(8,128)(2,1)}, u32[]{:S(2)}, u32[]{:S(2)}) collective-permute-start(bf16[256,1024]{1,0:T(8,128)(2,1)} %pad_maximum_fusion.9), channel_id=1, source_target_pairs={{0,8},{4,12},{8,0},{12,4},{1,9},{5,13},{9,1},{13,5},{2,10},{6,14},... | collective-permute-start | bytes 1572872 | tf_op jit(solution)/shard_map/ppermute | solution.py:179
  326.5 25.4 %collective-permute-start.42 = (bf16[272,1024]{1,0:T(8,128)(2,1)S(1)}, bf16[272,1024]{1,0:T(8,128)(2,1)}, u32[]{:S(2)}, u32[]{:S(2)}) collective-permute-start(bf16[272,1024]{1,0:T(8,128)(2,1)S(1)} %pad_maximum_fusion.8), channel_id=1, source_target_pairs={{0,4},{4,0},{8,12},{12,8},{1,5},{5,1},{9,13},{13,9},{2,6},{6,2},{1... | collective-permute-start | bytes 1671176 | tf_op jit(solution)/shard_map/ppermute | solution.py:179
  339.1 8.6 %collective-permute-start.31 = (bf16[128,1024]{1,0:T(8,128)(2,1)}, bf16[128,1024]{1,0:T(8,128)(2,1)S(1)}, u32[]{:S(2)}, u32[]{:S(2)}) collective-permute-start(bf16[128,1024]{1,0:T(8,128)(2,1)} %after.44.refs_1_.refs_0_), channel_id=1, source_target_pairs={{0,1},{1,0},{2,3},{3,2},{4,5},{5,4},{6,7},{7,6},{8,9},{9,8},{10,11... | collective-permute-start | bytes 786440 | tf_op jit(solution)/shard_map/ppermute | solution.py:179
  343.2 29.7 %collective-permute-start.30 = (bf16[512,1024]{1,0:T(8,128)(2,1)}, bf16[512,1024]{1,0:T(8,128)(2,1)}, u32[]{:S(2)}, u32[]{:S(2)}) collective-permute-start(bf16[512,1024]{1,0:T(8,128)(2,1)} %fusion.13.refs_2_), channel_id=1, source_target_pairs={{0,8},{4,12},{8,0},{12,4},{1,9},{5,13},{9,1},{13,5},{2,10},{6,14},... | collective-permute-start | bytes 3145736 | tf_op jit(solution)/shard_map/ppermute | solution.py:179
  344.6 28.3 %collective-permute-start.29 = (bf16[512,1024]{1,0:T(8,128)(2,1)}, bf16[512,1024]{1,0:T(8,128)(2,1)}, u32[]{:S(2)}, u32[]{:S(2)}) collective-permute-start(bf16[512,1024]{1,0:T(8,128)(2,1)} %copy-done.21), channel_id=1, source_target_pairs={{0,4},{4,0},{8,12},{12,8},{1,5},{5,1},{9,13},{13,9},{2,6},{6,2},{1... | collective-permute-start | bytes 3145736 | tf_op jit(solution)/shard_map/ppermute | solution.py:179
  348.4 8.2 %collective-permute-start.32 = (f32[3,1024]{1,0:T(4,128)}, f32[3,1024]{1,0:T(4,128)S(1)}, u32[]{:S(2)}, u32[]{:S(2)}) collective-permute-start(f32[3,1024]{1,0:T(4,128)} %after.46), channel_id=1, source_target_pairs={{0,1},{1,0},{2,3},{3,2},{4,5},{5,4},{6,7},{7,6},{8,9},{9,8},{10,11... | collective-permute-start | bytes 36872 | tf_op jit(solution)/shard_map/ppermute | solution.py:179
  350.4 6.3 %collective-permute-start.33 = (f32[3,1024]{1,0:T(4,128)}, f32[3,1024]{1,0:T(4,128)S(1)}, u32[]{:S(2)}, u32[]{:S(2)}) collective-permute-start(f32[3,1024]{1,0:T(4,128)} %after.46), channel_id=1, source_target_pairs={{0,2},{1,3},{2,0},{3,1},{4,6},{5,7},{6,4},{7,5},{8,10},{9,11},{10,... | collective-permute-start | bytes 36872 | tf_op jit(solution)/shard_map/ppermute | solution.py:179
  351.9 5.7 %collective-permute-start.34 = (f32[3,1024]{1,0:T(4,128)}, f32[3,1024]{1,0:T(4,128)S(1)}, u32[]{:S(2)}, u32[]{:S(2)}) collective-permute-start(f32[3,1024]{1,0:T(4,128)} %after.46), channel_id=1, source_target_pairs={{0,3},{1,2},{2,1},{3,0},{4,7},{5,6},{6,5},{7,4},{8,11},{9,10},{10,... | collective-permute-start | bytes 36872 | tf_op jit(solution)/shard_map/ppermute | solution.py:179
  356.6 22.6 %collective-permute-start.44 = (bf16[3,352,1024]{2,1,0:T(8,128)(2,1)}, bf16[3,352,1024]{2,1,0:T(8,128)(2,1)}, u32[]{:S(2)}, u32[]{:S(2)}) collective-permute-start(bf16[3,352,1024]{2,1,0:T(8,128)(2,1)} %after.48), channel_id=1, source_target_pairs={{0,16},{16,0},{1,17},{17,1},{2,18},{18,2},{3,19},{19,3},{4,20},{20... | collective-permute-start | bytes 6488072 | tf_op jit(solution)/shard_map/ppermute | solution.py:179
  360.9 6.7 %collective-permute-start.36 = (f32[3,1024]{1,0:T(4,128)S(1)}, f32[3,1024]{1,0:T(4,128)S(1)}, u32[]{:S(2)}, u32[]{:S(2)}) collective-permute-start(f32[3,1024]{1,0:T(4,128)S(1)} %add.240), channel_id=1, source_target_pairs={{0,4},{4,0},{8,12},{12,8},{1,5},{5,1},{9,13},{13,9},{2,6},{6,2},{1... | collective-permute-start | bytes 36872 | tf_op jit(solution)/shard_map/ppermute | solution.py:179
  365.4 3.7 collective-permute-start.37
  367.6 4.6 %collective-permute-start.38 = (f32[3,1024]{1,0:T(4,128)S(1)}, f32[3,1024]{1,0:T(4,128)S(1)}, u32[]{:S(2)}, u32[]{:S(2)}) collective-permute-start(f32[3,1024]{1,0:T(4,128)S(1)} %add.240), channel_id=1, source_target_pairs={{0,12},{4,8},{8,4},{12,0},{1,13},{5,9},{9,5},{13,1},{2,14},{6,10},... | collective-permute-start | bytes 36872 | tf_op jit(solution)/shard_map/ppermute | solution.py:179
  369.1 24.7 %collective-permute-start.45 = (bf16[256,1024]{1,0:T(8,128)(2,1)S(1)}, bf16[256,1024]{1,0:T(8,128)(2,1)S(1)}, u32[]{:S(2)}, u32[]{:S(2)}) collective-permute-start(bf16[256,1024]{1,0:T(8,128)(2,1)S(1)} %pad_maximum_fusion.10), channel_id=1, source_target_pairs={{0,2},{1,3},{2,0},{3,1},{4,6},{5,7},{6,4},{7,5},{8,10},{9,11},{10,... | collective-permute-start | bytes 1572872 | tf_op jit(solution)/shard_map/ppermute | solution.py:179
  (61 other events, 343.2 us)
